TPU v7x, 512 devices: a whole 4x4x16 slice. The times are simulated.
512 devices in a mesh: dp: 128 (over y_hi, z, x), outer: 4 (over y_lo, core).
Axes of the slice: x: 4, y: 4 (y_hi: 2, y_lo: 2; y = y_hi * 2 + y_lo), z: 16, core: 2. Of those that a mesh axis runs over, the one named last changes fastest.
Arguments:
- image_embeds: bfloat16 [4, 32768, 1152], P('outer', 'dp'), may hold values from -6 to 6
- text_features: bfloat16 [4, 32768, 1152], P('outer', 'dp'), may hold values from -92 to 92
- projection: bfloat16 [1152, 1152], replicated, may hold values from -0.1875 to 0.1875
- pair_step: int32 [4, 32768], P('outer'), may hold values from 0 to 5
- pair_col: int32 [4, 32768], P('outer'), may hold values from 0 to 255
Outputs:
- grad_text: bfloat16 [4, 32768, 1152], P('outer', 'dp')
- grad_proj: float32 [1152, 1152], P('dp', 'outer')
Inputs may be any that keep to these rules, and one draw needn't show every extreme that they name: pair_step of image row i in shard a points at text shard a - pair_step + 2 of the same group.
All inputs are finite; a program needn't handle non-finite values.
Results may differ from a plain program's by a relative error of at most 0.02.
Values may be sent and summed in bfloat16 or wider, within the bound.
No kernel may reach another device: no remote copies, remote signals or barrier semaphores. Data moves between devices by JAX's collectives and lax.ppermute only.
A program may use at most 64 MiB of HBM per device.

v0:
```python
import math

import jax
import jax.numpy as jnp
from jax import lax
from jax.sharding import PartitionSpec as P

WINDOW = 6


LOGIT_SCALE = 10.0
LOGIT_BIAS = -3.0
LOSS_SCALE = 256.0
EPSILON = 1e-06


def shifted(value, axis, steps):
    count = lax.axis_size(axis)
    pairs = [(source, (source + steps) % count) for source in range(count)]
    return lax.ppermute(value, axis, pairs)


def unit_rows(values):
    values = values.astype(jnp.float32)
    inverse = lax.rsqrt(jnp.sum(values * values, axis=-1, keepdims=True) + EPSILON)
    return (values * inverse, inverse)


def pair_grad(images, texts, step_ids, col_ids, position):
    logits = (
        LOGIT_SCALE * jnp.einsum("ie,ke->ik", images, texts, preferred_element_type=jnp.float32)
        + LOGIT_BIAS
    )
    columns = lax.broadcasted_iota(jnp.int32, logits.shape, 1)
    positive = (step_ids[:, None] == position) & (col_ids[:, None] == columns)
    target = jnp.where(positive, 1.0, -1.0).astype(jnp.float32)
    return (-LOSS_SCALE * LOGIT_SCALE * target * jax.nn.sigmoid(-target * logits)).astype(
        jnp.bfloat16
    )


def shard_rows(table, shard, cycle_size, row_count):
    start = (shard + cycle_size) % cycle_size * row_count
    return lax.dynamic_slice_in_dim(table, start, row_count)


def move_block(travel, hop):
    return shifted(travel, "dp", hop)


def local(image_embeds, text_features, projection, pair_step, pair_col):
    cycle_size = lax.axis_size("dp")
    my_index = lax.axis_index("dp")
    row_count = image_embeds.shape[1]
    window_len = min(WINDOW, cycle_size)
    back_reach = window_len // 2 - 1
    unit_img = unit_rows(image_embeds[0])[0].astype(jnp.bfloat16)
    features = text_features[0]
    hidden = jnp.dot(features, projection, preferred_element_type=jnp.float32)
    unit_text, inverse_norm = unit_rows(hidden)
    text_units = unit_text.astype(jnp.bfloat16)
    all_steps = pair_step[0]
    all_cols = pair_col[0]
    streams = [(-back_reach, 0)] + [(1, position) for position in range(1, window_len)]
    my_steps = shard_rows(all_steps, my_index, cycle_size, row_count)
    my_cols = shard_rows(all_cols, my_index, cycle_size, row_count)
    travel = text_units
    running = None
    for hop, position in streams:
        travel = move_block(travel, hop)
        if running is not None:
            running = shifted(running.astype(jnp.bfloat16), "dp", hop).astype(running.dtype)
        weights = pair_grad(unit_img, travel, my_steps, my_cols, position)
        contribution = jnp.einsum(
            "ik,ie->ke", weights, unit_img, preferred_element_type=jnp.float32
        )
        running = contribution if running is None else running + contribution
    unit_grad = shifted(running.astype(jnp.bfloat16), "dp", back_reach - streams[-1][1]).astype(
        running.dtype
    )
    radial = jnp.sum(unit_text * unit_grad, axis=-1, keepdims=True)
    hidden_grad = (inverse_norm * (unit_grad - unit_text * radial)).astype(jnp.bfloat16)
    grad_text = jnp.einsum(
        "ke,de->kd", hidden_grad, projection, preferred_element_type=jnp.float32
    ).astype(jnp.bfloat16)
    partial_value = jnp.einsum(
        "kd,ke->de", features, hidden_grad, preferred_element_type=jnp.float32
    )
    partial_value = lax.optimization_barrier(partial_value.astype(jnp.bfloat16)).astype(jnp.float32)
    pooled = lax.psum_scatter(
        partial_value.astype(jnp.bfloat16), "outer", scatter_dimension=1, tiled=True
    ).astype(jnp.float32)
    owned = lax.psum_scatter(pooled, "dp", scatter_dimension=0, tiled=True)
    global_sq = lax.psum(jnp.sum(owned * owned), ("dp", "outer"))
    threshold = math.sqrt(projection.shape[0] * projection.shape[1])
    factor = jnp.minimum(1.0, threshold / jnp.sqrt(global_sq))
    return (grad_text[None], owned * factor)


def solution(mesh):
    placed = (
        P("outer", "dp", None),
        P("outer", "dp", None),
        P(),
        P("outer", None),
        P("outer", None),
    )
    return jax.shard_map(
        local,
        mesh=mesh,
        in_specs=placed,
        out_specs=(P("outer", "dp", None), P("dp", "outer")),
        check_vma=False,
    )
```

profile of v0, /device:TPU:1, one launch (start us, length us, event | category | flops | bytes accessed | tf_op | source)
XLA Modules:
  0.0 1107.7 jit_solution(4364661840742678772)
XLA Ops:
  12.2 17.0 %collective-permute-start = (bf16[256,1152]{1,0:T(8,128)(2,1)S(1)}, bf16[256,1152]{1,0:T(8,128)(2,1)}, u32[]{:S(2)}, u32[]{:S(2)}) collective-permute-start(bf16[256,1152]{1,0:T(8,128)(2,1)S(1)} %multiply_convert_fusion), channel_id=1, source_target_pairs={{0,504},{4,508},{8,0},{12,4},{16,8},{20,12},{24,16},{28,20},{32,24... | collective-permute-start | bytes 1769480 | tf_op jit(solution)/shard_map/ppermute | solution.py:20
  32.0 9.3 collective-permute-done
  41.2 3.4 convolution_convert_fusion.2
  44.6 2.2 collective-permute-start.1
  48.7 18.2 %collective-permute-done.1 = bf16[256,1152]{1,0:T(8,128)(2,1)} collective-permute-done((bf16[256,1152]{1,0:T(8,128)(2,1)}, bf16[256,1152]{1,0:T(8,128)(2,1)}, u32[]{:S(2)}, u32[]{:S(2)}) %collective-permute-start.1) | collective-permute-done | bytes 589856 | tf_op jit(solution)/shard_map/ppermute | solution.py:20
  67.0 12.6 %collective-permute-done.2 = bf16[256,1152]{1,0:T(8,128)(2,1)} collective-permute-done((bf16[256,1152]{1,0:T(8,128)(2,1)}, bf16[256,1152]{1,0:T(8,128)(2,1)}, u32[]{:S(2)}, u32[]{:S(2)}) %collective-permute-start.2) | collective-permute-done | bytes 589856 | tf_op jit(solution)/shard_map/ppermute | solution.py:20
  79.6 3.1 add_convert_fusion.4
  86.6 16.7 %collective-permute-done.3 = bf16[256,1152]{1,0:T(8,128)(2,1)} collective-permute-done((bf16[256,1152]{1,0:T(8,128)(2,1)}, bf16[256,1152]{1,0:T(8,128)(2,1)}, u32[]{:S(2)}, u32[]{:S(2)}) %collective-permute-start.3) | collective-permute-done | bytes 589856 | tf_op jit(solution)/shard_map/ppermute | solution.py:20
  103.3 12.6 %collective-permute-done.4 = bf16[256,1152]{1,0:T(8,128)(2,1)} collective-permute-done((bf16[256,1152]{1,0:T(8,128)(2,1)}, bf16[256,1152]{1,0:T(8,128)(2,1)}, u32[]{:S(2)}, u32[]{:S(2)}) %collective-permute-start.4) | collective-permute-done | bytes 589856 | tf_op jit(solution)/shard_map/ppermute | solution.py:20
  115.9 3.1 add_convert_fusion.3
  122.9 15.8 %collective-permute-done.5 = bf16[256,1152]{1,0:T(8,128)(2,1)} collective-permute-done((bf16[256,1152]{1,0:T(8,128)(2,1)}, bf16[256,1152]{1,0:T(8,128)(2,1)}, u32[]{:S(2)}, u32[]{:S(2)}) %collective-permute-start.5) | collective-permute-done | bytes 589856 | tf_op jit(solution)/shard_map/ppermute | solution.py:20
  138.7 12.6 %collective-permute-done.6 = bf16[256,1152]{1,0:T(8,128)(2,1)} collective-permute-done((bf16[256,1152]{1,0:T(8,128)(2,1)}, bf16[256,1152]{1,0:T(8,128)(2,1)}, u32[]{:S(2)}, u32[]{:S(2)}) %collective-permute-start.6) | collective-permute-done | bytes 589856 | tf_op jit(solution)/shard_map/ppermute | solution.py:20
  151.3 3.1 add_convert_fusion.2
  158.3 14.9 %collective-permute-done.7 = bf16[256,1152]{1,0:T(8,128)(2,1)} collective-permute-done((bf16[256,1152]{1,0:T(8,128)(2,1)}, bf16[256,1152]{1,0:T(8,128)(2,1)}, u32[]{:S(2)}, u32[]{:S(2)}) %collective-permute-start.7) | collective-permute-done | bytes 589856 | tf_op jit(solution)/shard_map/ppermute | solution.py:20
  173.1 12.6 %collective-permute-done.8 = bf16[256,1152]{1,0:T(8,128)(2,1)} collective-permute-done((bf16[256,1152]{1,0:T(8,128)(2,1)}, bf16[256,1152]{1,0:T(8,128)(2,1)}, u32[]{:S(2)}, u32[]{:S(2)}) %collective-permute-start.8) | collective-permute-done | bytes 589856 | tf_op jit(solution)/shard_map/ppermute | solution.py:20
  185.8 3.1 add_convert_fusion.1
  192.7 13.9 %collective-permute-done.9 = bf16[256,1152]{1,0:T(8,128)(2,1)} collective-permute-done((bf16[256,1152]{1,0:T(8,128)(2,1)}, bf16[256,1152]{1,0:T(8,128)(2,1)}, u32[]{:S(2)}, u32[]{:S(2)}) %collective-permute-start.9) | collective-permute-done | bytes 589856 | tf_op jit(solution)/shard_map/ppermute | solution.py:20
  206.7 12.6 %collective-permute-done.10 = bf16[256,1152]{1,0:T(8,128)(2,1)} collective-permute-done((bf16[256,1152]{1,0:T(8,128)(2,1)}, bf16[256,1152]{1,0:T(8,128)(2,1)}, u32[]{:S(2)}, u32[]{:S(2)}) %collective-permute-start.10) | collective-permute-done | bytes 589856 | tf_op jit(solution)/shard_map/ppermute | solution.py:20
  219.3 3.1 add_convert_fusion
  224.5 10.1 collective-permute-done.11
  237.2 2.5 fusion
  241.7 34.5 %reduce-scatter.3.cloned.1.call-done = bf16[1152,288]{0,1:T(8,128)(2,1)} async-done(((bf16[1152,1152]{0,1:T(8,128)(2,1)}), bf16[1152,288]{0,1:T(8,128)(2,1)}) %reduce-scatter.3.cloned.1.call-update) | async-done | bytes 663568 | tf_op jit(solution)/shard_map/reduce_scatter | solution.py:90
  276.2 612.3 %all-reduce.2 = f32[1152,288]{0,1:T(8,128)} all-reduce(bf16[1152,288]{0,1:T(8,128)(2,1)} %reduce-scatter.3.cloned.1.call-done), channel_id=3, replica_groups=mesh['dp'=128,'outer'=4] {'dp'}, use_global_device_ids=true, to_apply=%region_4.5.clone | all-reduce | flops 331776 | bytes 1990656
  892.0 206.3 %psum.7 = f32[]{:T(128)} all-reduce(f32[]{:T(128)} %multiply_reduce_fusion.1), channel_id=1, replica_groups=mesh['dp'=128,'outer'=4] {'dp','outer'}, use_global_device_ids=true, to_apply=%region_6.7 | all-reduce | flops 1 | bytes 8 | tf_op jit(solution)/shard_map/psum | solution.py:94
  (36 shorter events, 36.2 us)
Async XLA Ops:
  7.2 1.8 copy-start
  7.2 269.0 %reduce-scatter.3.cloned.1.call-start = ((), (), s32[]{:S(2)}) async-start(), calls=%async_computation.1 | async-start | bytes 3317760 | tf_op jit(solution)/shard_map/reduce_scatter | solution.py:90
  11.1 1.0 copy-start.1
  12.2 29.0 %collective-permute-start = (bf16[256,1152]{1,0:T(8,128)(2,1)S(1)}, bf16[256,1152]{1,0:T(8,128)(2,1)}, u32[]{:S(2)}, u32[]{:S(2)}) collective-permute-start(bf16[256,1152]{1,0:T(8,128)(2,1)S(1)} %multiply_convert_fusion), channel_id=1, source_target_pairs={{0,504},{4,508},{8,0},{12,4},{16,8},{20,12},{24,16},{28,20},{32,24... | collective-permute-start | bytes 1769480 | tf_op jit(solution)/shard_map/ppermute | solution.py:20
  41.2 38.4 %copy-start.4 = (bf16[1,256,1152]{2,1,0:T(8,128)(2,1)S(1)}, bf16[1,256,1152]{2,1,0:T(8,128)(2,1)}, u32[]{:S(2)}) copy-start(bf16[1,256,1152]{2,1,0:T(8,128)(2,1)} %param.5) | copy-start | bytes 1769476
  44.6 22.4 %collective-permute-start.1 = (bf16[256,1152]{1,0:T(8,128)(2,1)}, bf16[256,1152]{1,0:T(8,128)(2,1)}, u32[]{:S(2)}, u32[]{:S(2)}) collective-permute-start(bf16[256,1152]{1,0:T(8,128)(2,1)} %convolution_convert_fusion.2), channel_id=1, source_target_pairs={{0,4},{4,8},{8,12},{12,16},{16,20},{20,24},{24,28},{28,32},{32,36}... | collective-permute-start | bytes 1769480 | tf_op jit(solution)/shard_map/ppermute | solution.py:20
  46.8 32.8 %collective-permute-start.2 = (bf16[256,1152]{1,0:T(8,128)(2,1)}, bf16[256,1152]{1,0:T(8,128)(2,1)}, u32[]{:S(2)}, u32[]{:S(2)}) collective-permute-start(bf16[256,1152]{1,0:T(8,128)(2,1)} %collective-permute-done), channel_id=1, source_target_pairs={{0,4},{4,8},{8,12},{12,16},{16,20},{20,24},{24,28},{28,32},{32,36}... | collective-permute-start | bytes 1769480 | tf_op jit(solution)/shard_map/ppermute | solution.py:20
  82.7 20.6 %collective-permute-start.3 = (bf16[256,1152]{1,0:T(8,128)(2,1)}, bf16[256,1152]{1,0:T(8,128)(2,1)}, u32[]{:S(2)}, u32[]{:S(2)}) collective-permute-start(bf16[256,1152]{1,0:T(8,128)(2,1)} %add_convert_fusion.4), channel_id=1, source_target_pairs={{0,4},{4,8},{8,12},{12,16},{16,20},{20,24},{24,28},{28,32},{32,36}... | collective-permute-start | bytes 1769480 | tf_op jit(solution)/shard_map/ppermute | solution.py:20
  84.6 31.3 %collective-permute-start.4 = (bf16[256,1152]{1,0:T(8,128)(2,1)}, bf16[256,1152]{1,0:T(8,128)(2,1)}, u32[]{:S(2)}, u32[]{:S(2)}) collective-permute-start(bf16[256,1152]{1,0:T(8,128)(2,1)} %collective-permute-done.2), channel_id=1, source_target_pairs={{0,4},{4,8},{8,12},{12,16},{16,20},{20,24},{24,28},{28,32},{32,36}... | collective-permute-start | bytes 1769480 | tf_op jit(solution)/shard_map/ppermute | solution.py:20
  119.0 19.6 %collective-permute-start.5 = (bf16[256,1152]{1,0:T(8,128)(2,1)}, bf16[256,1152]{1,0:T(8,128)(2,1)}, u32[]{:S(2)}, u32[]{:S(2)}) collective-permute-start(bf16[256,1152]{1,0:T(8,128)(2,1)} %add_convert_fusion.3), channel_id=1, source_target_pairs={{0,4},{4,8},{8,12},{12,16},{16,20},{20,24},{24,28},{28,32},{32,36}... | collective-permute-start | bytes 1769480 | tf_op jit(solution)/shard_map/ppermute | solution.py:20
  120.9 30.4 %collective-permute-start.6 = (bf16[256,1152]{1,0:T(8,128)(2,1)}, bf16[256,1152]{1,0:T(8,128)(2,1)}, u32[]{:S(2)}, u32[]{:S(2)}) collective-permute-start(bf16[256,1152]{1,0:T(8,128)(2,1)} %collective-permute-done.4), channel_id=1, source_target_pairs={{0,4},{4,8},{8,12},{12,16},{16,20},{20,24},{24,28},{28,32},{32,36}... | collective-permute-start | bytes 1769480 | tf_op jit(solution)/shard_map/ppermute | solution.py:20
  154.4 18.7 %collective-permute-start.7 = (bf16[256,1152]{1,0:T(8,128)(2,1)}, bf16[256,1152]{1,0:T(8,128)(2,1)}, u32[]{:S(2)}, u32[]{:S(2)}) collective-permute-start(bf16[256,1152]{1,0:T(8,128)(2,1)} %add_convert_fusion.2), channel_id=1, source_target_pairs={{0,4},{4,8},{8,12},{12,16},{16,20},{20,24},{24,28},{28,32},{32,36}... | collective-permute-start | bytes 1769480 | tf_op jit(solution)/shard_map/ppermute | solution.py:20
  156.3 29.4 %collective-permute-start.8 = (bf16[256,1152]{1,0:T(8,128)(2,1)}, bf16[256,1152]{1,0:T(8,128)(2,1)}, u32[]{:S(2)}, u32[]{:S(2)}) collective-permute-start(bf16[256,1152]{1,0:T(8,128)(2,1)} %collective-permute-done.6), channel_id=1, source_target_pairs={{0,4},{4,8},{8,12},{12,16},{16,20},{20,24},{24,28},{28,32},{32,36}... | collective-permute-start | bytes 1769480 | tf_op jit(solution)/shard_map/ppermute | solution.py:20
  188.9 17.8 %collective-permute-start.9 = (bf16[256,1152]{1,0:T(8,128)(2,1)}, bf16[256,1152]{1,0:T(8,128)(2,1)}, u32[]{:S(2)}, u32[]{:S(2)}) collective-permute-start(bf16[256,1152]{1,0:T(8,128)(2,1)} %add_convert_fusion.1), channel_id=1, source_target_pairs={{0,4},{4,8},{8,12},{12,16},{16,20},{20,24},{24,28},{28,32},{32,36}... | collective-permute-start | bytes 1769480 | tf_op jit(solution)/shard_map/ppermute | solution.py:20
  190.8 28.5 %collective-permute-start.10 = (bf16[256,1152]{1,0:T(8,128)(2,1)}, bf16[256,1152]{1,0:T(8,128)(2,1)}, u32[]{:S(2)}, u32[]{:S(2)}) collective-permute-start(bf16[256,1152]{1,0:T(8,128)(2,1)} %collective-permute-done.8), channel_id=1, source_target_pairs={{0,4},{4,8},{8,12},{12,16},{16,20},{20,24},{24,28},{28,32},{32,36}... | collective-permute-start | bytes 1769480 | tf_op jit(solution)/shard_map/ppermute | solution.py:20
  222.4 13.7 %copy-start.2 = (f32[256,1152]{1,0:T(8,128)S(1)}, f32[256,1152]{1,0:T(8,128)}, u32[]{:S(2)}) copy-start(f32[256,1152]{1,0:T(8,128)} %copy-done.1) | copy-start | bytes 3538948
  222.4 12.2 %collective-permute-start.11 = (bf16[256,1152]{1,0:T(8,128)(2,1)}, bf16[256,1152]{1,0:T(8,128)(2,1)S(1)}, u32[]{:S(2)}, u32[]{:S(2)}) collective-permute-start(bf16[256,1152]{1,0:T(8,128)(2,1)} %add_convert_fusion), channel_id=1, source_target_pairs={{0,500},{4,504},{8,508},{12,0},{16,4},{20,8},{24,12},{28,16},{32,2... | collective-permute-start | bytes 1769480 | tf_op jit(solution)/shard_map/ppermute | solution.py:20
  236.2 1.1 copy-start.3
Sparse Core Ops, SparseCore 0:
  239.9 36.2 reduce-scatter.2
where the time goes:
time: 1110 us
  blocking collectives  819 us (74%)
  waiting for transfers between devices  197 us (18%)
  starting transfers between devices  38.6 us (3%)
  matrix products  25.4 us (2%)
  between operations  15.6 us (1%)
    unnamed x1, blocking collectives  612 us
    psum x1, blocking collectives, local(): global_sq = lax.psum(jnp.sum(owned * owned), ('dp', 'outer'))  206 us
    ppermute x12, waiting for transfers between devices, shifted(): return lax.ppermute(value, axis, pairs)  162 us
    ppermute x12, starting transfers between devices, shifted(): return lax.ppermute(value, axis, pairs)  38.5 us
    reduce_scatter x1, waiting for transfers between devices, local(): lax.psum_scatter(partial_value.astype(jnp.bfloat16), 'outer', scatter_dim...  34.5 us
  transfers between devices with their start and end apart: 13, of which 13 were waited for; matrix products, arithmetic and copies ran while one was open for 0% of the time, Pallas kernels for 0%

commit v1 on v0

v1 whole, which is shorter than its diff:
```python
import math

import jax
import jax.numpy as jnp
from jax import lax
from jax.sharding import Mesh, PartitionSpec as P

LOGIT_SCALE = 10.0
LOGIT_BIAS = -3.0
LOSS_SCALE = 256.0
EPSILON = 1e-06

SHARDS = 128
ROWS = 256
SHAPE = (2, 4, 4, 4, 2, 2)
AXES = ("yh", "zh", "zl", "x", "yl", "c")
DP = ("yh", "zh", "zl", "x")
OUTER = ("yl", "c")
Y = ("yl", "yh")
WIDTH = 2688
FIRST = 1280


def shifted(value, hop):
    pairs = [(source, (source + hop) % SHARDS) for source in range(SHARDS)]
    return lax.ppermute(value, DP, pairs)


def unit_rows(values):
    values = values.astype(jnp.float32)
    inverse = lax.rsqrt(jnp.sum(values * values, axis=-1, keepdims=True) + EPSILON)
    return (values * inverse, inverse)


def pair_grad(images, texts, step_ids, col_ids, position):
    logits = (
        LOGIT_SCALE * jnp.einsum("ke,ie->ki", texts, images, preferred_element_type=jnp.float32)
        + LOGIT_BIAS
    )
    rows = lax.broadcasted_iota(jnp.int32, logits.shape, 0)
    positive = (step_ids[None, :] == position) & (col_ids[None, :] == rows)
    target = jnp.where(positive, 1.0, -1.0).astype(jnp.float32)
    weights = (-LOSS_SCALE * LOGIT_SCALE * target * jax.nn.sigmoid(-target * logits)).astype(
        jnp.bfloat16
    )
    return jnp.einsum("ki,ie->ke", weights, images, preferred_element_type=jnp.float32)


def traded(value, axis):
    return lax.all_to_all(value, axis, split_axis=0, concat_axis=0)


def total(value):
    return jnp.sum(value.astype(jnp.float32), axis=0)


def local(image_embeds, text_features, projection, pair_step, pair_col):
    me = lax.axis_index(DP)
    core = lax.axis_index("c")
    image = image_embeds[0]
    before = shifted(image, 1)
    after = shifted(image, -1)
    before2 = shifted(before, 1)
    after2 = shifted(after, -1)
    after3 = shifted(before, -4)

    features = text_features[0]
    hidden = jnp.dot(features, projection, preferred_element_type=jnp.float32)
    unit_text, inverse_norm = unit_rows(hidden)
    text_units = unit_text.astype(jnp.bfloat16)
    step_table = pair_step.reshape(SHARDS, ROWS)
    col_table = pair_col.reshape(SHARDS, ROWS)
    unit_grad = None
    for position, block in ((2, image), (1, before), (3, after), (0, before2), (4, after2), (5, after3)):
        shard = (me + position - 2) % SHARDS
        steps = lax.dynamic_index_in_dim(step_table, shard, 0, keepdims=False)
        cols = lax.dynamic_index_in_dim(col_table, shard, 0, keepdims=False)
        images = unit_rows(block)[0].astype(jnp.bfloat16)
        part = pair_grad(images, text_units, steps, cols, position)
        unit_grad = part if unit_grad is None else unit_grad + part

    radial = jnp.sum(unit_text * unit_grad, axis=-1, keepdims=True)
    hidden_grad = (inverse_norm * (unit_grad - unit_text * radial)).astype(jnp.bfloat16)
    grad_text = jnp.einsum(
        "ke,de->kd", hidden_grad, projection, preferred_element_type=jnp.float32
    ).astype(jnp.bfloat16)

    ordered = features.reshape(ROWS, 2, 4, 4, 4, 9).transpose(5, 1, 4, 3, 2, 0)
    partial = jnp.einsum(
        "rpk,ke->rpe",
        ordered.reshape(9, SHARDS, ROWS),
        hidden_grad,
        preferred_element_type=jnp.float32,
    ).astype(jnp.bfloat16)
    partial = partial.reshape(9, SHARDS, 2, 2, 288).transpose(3, 2, 1, 0, 4)
    partial = partial.reshape(2, 2, SHARDS, 2592)
    partial = jnp.pad(partial, ((0, 0), (0, 0), (0, 0), (0, WIDTH - 2592)))
    there = lax.dynamic_index_in_dim(partial, 1 - core, 0, keepdims=False)
    here = lax.dynamic_index_in_dim(partial, core, 0, keepdims=False)
    came = lax.ppermute(there, "c", [(0, 1), (1, 0)])
    both = (here.astype(jnp.float32) + came.astype(jnp.float32)).astype(jnp.bfloat16)
    both = both.reshape(4, 4, 16, WIDTH)

    one = traded(both[..., :FIRST], Y)
    two = traded(both[..., FIRST:].transpose(1, 0, 2, 3), "x")
    one = traded(total(one).astype(jnp.bfloat16), "x")
    two = traded(total(two).astype(jnp.bfloat16), Y)
    rows = jnp.concatenate([total(one), total(two)], axis=-1).astype(jnp.bfloat16)
    rows = total(traded(rows.reshape(4, 4, WIDTH), "zl")).astype(jnp.bfloat16)
    rows = total(traded(jnp.broadcast_to(rows[None], (4, 4, WIDTH)), "zh"))
    square = jnp.sum(rows * rows)
    for axis in ("c", Y, "x", "zl"):
        square = lax.psum(square, axis)
    owned = lax.dynamic_index_in_dim(rows, lax.axis_index("zh"), 0, keepdims=False)
    owned = owned[:2592].reshape(9, 288)
    threshold = math.sqrt(projection.shape[0] * projection.shape[1])
    factor = jnp.minimum(1.0, threshold / jnp.sqrt(square))
    return (grad_text[None], owned * factor)


def solution(mesh):
    split = Mesh(mesh.devices.reshape(SHAPE), AXES)
    placed = (
        P(OUTER, DP, None),
        P(OUTER, DP, None),
        P(),
        P(OUTER, None),
        P(OUTER, None),
    )
    return jax.shard_map(
        local,
        mesh=split,
        in_specs=placed,
        out_specs=(P(OUTER, DP, None), P(DP, OUTER)),
        check_vma=False,
    )
```

time: 1110 us -> 216 us (0.19)
  the two profiles are of different devices: /device:TPU:1 before, /device:TPU:2 now
where the time goes in v1:
time: 216 us; the launch traced here: 215 us
  blocking collectives  61.8 us (29%)
  starting transfers between devices  51.8 us (24%)
  waiting for transfers between devices  33.4 us (15%)
  matrix products  28.7 us (13%)
  other arithmetic  20.3 us (9%)
  local copies, waits for them, and re-layouts  16.9 us (8%)
    psum x4, blocking collectives, local(): square = lax.psum(square, axis)  33.5 us
    all_to_all x2, blocking collectives, traded(): return lax.all_to_all(value, axis, split_axis=0, concat_axis=0)  28.3 us
    ppermute x5, starting transfers between devices, shifted(): return lax.ppermute(value, DP, pairs)  26.6 us
    all_to_all x4, waiting for transfers between devices, traded(): return lax.all_to_all(value, axis, split_axis=0, concat_axis=0)  26 us
    all_to_all x4, starting transfers between devices, traded(): return lax.all_to_all(value, axis, split_axis=0, concat_axis=0)  23.1 us
    dot_general x6, matrix products, pair_grad(): jnp.einsum('ki,ie->ke', weights, images, preferred_element_type=jnp.float32)  22.8 us
    reduce_sum x6, other arithmetic, unit_rows(): jnp.sum(values * values, axis=-1, keepdims=True) + EPSILON  6.5 us
  transfers between devices with their start and end apart: 10, of which 6 were waited for; matrix products, arithmetic and copies ran while one was open for 17% of the time, Pallas kernels for 0%

profile of v1, /device:TPU:2, one launch (start us, length us, event | category | flops | bytes accessed | tf_op | source)
XLA Modules:
  0.0 214.6 jit_solution(7038996714828667841)
XLA Ops:
  0.7 3.7 %collective-permute-start = (bf16[256,1152]{1,0:T(8,128)(2,1)}, bf16[256,1152]{1,0:T(8,128)(2,1)}, u32[]{:S(2)}, u32[]{:S(2)}) collective-permute-start(bf16[256,1152]{1,0:T(8,128)(2,1)} %bitcast.60), channel_id=1, source_target_pairs={{0,4},{4,8},{8,12},{12,16},{16,20},{20,24},{24,28},{28,32},{32,36}... | collective-permute-start | bytes 1769480 | tf_op jit(solution)/shard_map/ppermute | solution.py:26
  4.3 6.3 %collective-permute-start.1 = (bf16[256,1152]{1,0:T(8,128)(2,1)}, bf16[256,1152]{1,0:T(8,128)(2,1)}, u32[]{:S(2)}, u32[]{:S(2)}) collective-permute-start(bf16[256,1152]{1,0:T(8,128)(2,1)} %bitcast.61), channel_id=1, source_target_pairs={{0,508},{4,0},{8,4},{12,8},{16,12},{20,16},{24,20},{28,24},{32,28}... | collective-permute-start | bytes 1769480 | tf_op jit(solution)/shard_map/ppermute | solution.py:26
  25.4 3.4 %fusion.68 = f32[256,1152]{1,0:T(8,128)} fusion(bf16[256,1152]{1,0:T(8,128)(2,1)S(1)} %multiply_convert_fusion.1, f32[256]{0:T(256)S(1)} %add_rsqrt_fusion.5, s32[256]{0:T(256)S(1)} %bitcast.67, pred[256]{0:T(512)(128)(4,1)S(1)} %get-tuple-element.7, bf16[1,256,1152]{2,1,0:T(8,128)(2,1)} %param.5), kind=kOutput, calls=%fused_computation.97 | convolution fusion | flops 304611328 | bytes 2361600 | tf_op jit(solution)/shard_map/ki,ie->ke/dot_general | solution.py:46
  28.8 10.1 %collective-permute-start.4 = (bf16[256,1152]{1,0:T(8,128)(2,1)}, bf16[256,1152]{1,0:T(8,128)(2,1)}, u32[]{:S(2)}, u32[]{:S(2)}) collective-permute-start(bf16[256,1152]{1,0:T(8,128)(2,1)} %collective-permute-done), channel_id=1, source_target_pairs={{0,496},{4,500},{8,504},{12,508},{16,0},{20,4},{24,8},{28,12},{32,... | collective-permute-start | bytes 1769480 | tf_op jit(solution)/shard_map/ppermute | solution.py:26
  38.9 3.4 %collective-permute-start.2 = (bf16[256,1152]{1,0:T(8,128)(2,1)}, bf16[256,1152]{1,0:T(8,128)(2,1)S(1)}, u32[]{:S(2)}, u32[]{:S(2)}) collective-permute-start(bf16[256,1152]{1,0:T(8,128)(2,1)} %collective-permute-done), channel_id=1, source_target_pairs={{0,4},{4,8},{8,12},{12,16},{16,20},{20,24},{24,28},{28,32},{32,36}... | collective-permute-start | bytes 1769480 | tf_op jit(solution)/shard_map/ppermute | solution.py:26
  46.7 3.9 %convolution_add_fusion.2 = f32[256,1152]{1,0:T(8,128)} fusion(f32[256,1152]{1,0:T(8,128)} %fusion.68, bf16[256,1152]{1,0:T(8,128)(2,1)} %copy-done.6, bf16[256,1152]{1,0:T(8,128)(2,1)} %collective-permute-done, f32[256]{0:T(256)S(1)} %add_rsqrt_fusion.4, s32[256]{0:T(256)S(1)} %bitcast.66, pred[256]{0:T(512)(128)(4,1)S(1)} %get-tuple-element.6), kind=kOutput, calls=%fused_computation.3 | convolution fusion | flops 304906240 | bytes 3541248 | tf_op jit(solution)/shard_map/ki,ie->ke/dot_general | solution.py:46
  51.8 3.9 %convolution_add_fusion.1 = f32[256,1152]{1,0:T(8,128)} fusion(f32[256,1152]{1,0:T(8,128)} %convolution_add_fusion.2, bf16[256,1152]{1,0:T(8,128)(2,1)} %copy-done.6, bf16[256,1152]{1,0:T(8,128)(2,1)} %collective-permute-done.1, f32[256]{0:T(256)S(1)} %add_rsqrt_fusion.3, s32[256]{0:T(256)S(1)} %bitcast.65, pred[256]{0:T(512)(128)(4,1)S(1)} %get-tuple-element.5), kind=kOutput, calls=%fused_computation.2 | convolution fusion | flops 304906240 | bytes 3541248 | tf_op jit(solution)/shard_map/ki,ie->ke/dot_general | solution.py:46
  55.7 4.0 %collective-permute-done.3 = bf16[256,1152]{1,0:T(8,128)(2,1)} collective-permute-done((bf16[256,1152]{1,0:T(8,128)(2,1)}, bf16[256,1152]{1,0:T(8,128)(2,1)}, u32[]{:S(2)}, u32[]{:S(2)}) %collective-permute-start.3) | collective-permute-done | bytes 589856 | tf_op jit(solution)/shard_map/ppermute | solution.py:26
  62.5 3.5 %fusion.67 = f32[256,1152]{1,0:T(8,128)} fusion(bf16[256,1152]{1,0:T(8,128)(2,1)} %copy-done.6, bf16[256,1152]{1,0:T(8,128)(2,1)} %collective-permute-done.3, f32[256]{0:T(256)S(1)} %add_rsqrt_fusion.1, s32[256]{0:T(256)S(1)} %bitcast.64, pred[256]{0:T(512)(128)(4,1)S(1)} %get-tuple-element.4), kind=kOutput, calls=%fused_computation.96 | convolution fusion | flops 304611328 | bytes 2361600 | tf_op jit(solution)/shard_map/ki,ie->ke/dot_general | solution.py:46
  66.1 3.5 %fusion.66 = f32[256,1152]{1,0:T(8,128)} fusion(bf16[256,1152]{1,0:T(8,128)(2,1)} %copy-done.6, bf16[256,1152]{1,0:T(8,128)(2,1)} %collective-permute-done.4, f32[256]{0:T(256)S(1)} %add_rsqrt_fusion, s32[256]{0:T(256)S(1)} %bitcast.63, pred[256]{0:T(512)(128)(4,1)S(1)} %get-tuple-element.3), kind=kOutput, calls=%fused_computation.95 | convolution fusion | flops 304611328 | bytes 2361600 | tf_op jit(solution)/shard_map/ki,ie->ke/dot_general | solution.py:46
  69.5 4.6 %multiply_reduce_fusion = (f32[256]{0:T(256)S(1)}, f32[256,1152]{1,0:T(8,128)}) fusion(f32[256,1152]{1,0:T(8,128)} %get-tuple-element.15, f32[256]{0:T(256)S(1)} %add_rsqrt_fusion.6, f32[256,1152]{1,0:T(8,128)} %fusion.66, f32[256,1152]{1,0:T(8,128)} %fusion.67, f32[256,1152]{1,0:T(8,128)} %convolution_add_fusion.1, ...), kind=kOutput, calls=%fused_computation.39 | convolution fusion | flops 306380544 | bytes 7082240 | tf_op jit(solution)/shard_map/ki,ie->ke/dot_general | solution.py:46
  92.3 3.5 %all-to-all-start = ((bf16[4,4,16,1280]{3,2,1,0:T(8,128)(2,1)}), bf16[4,4,16,1280]{3,2,1,0:T(8,128)(2,1)S(1)}, u32[]{:S(2)}, u32[]{:S(2)}) async-start(bf16[4,4,16,1280]{3,2,1,0:T(8,128)(2,1)} %slice.13), calls=%async_computation | async-start | bytes 1310720 | tf_op jit(solution)/shard_map/all_to_all | solution.py:50
  97.8 9.1 %all-to-all-done = bf16[4,4,16,1280]{3,2,1,0:T(8,128)(2,1)S(1)} async-done(((bf16[4,4,16,1280]{3,2,1,0:T(8,128)(2,1)}), bf16[4,4,16,1280]{3,2,1,0:T(8,128)(2,1)S(1)}, u32[]{:S(2)}, u32[]{:S(2)}) %all-to-all-start) | async-done | bytes 655392 | tf_op jit(solution)/shard_map/all_to_all | solution.py:50
  107.7 11.5 %all-to-all-start.2 = ((bf16[4,4,16,1408]{3,2,1,0:T(8,128)(2,1)}), bf16[4,4,16,1408]{3,2,1,0:T(8,128)(2,1)S(1)}, u32[]{:S(2)}, u32[]{:S(2)}) async-start(bf16[4,4,16,1408]{3,2,1,0:T(8,128)(2,1)} %copy.28), calls=%async_computation.2 | async-start | bytes 1441792 | tf_op jit(solution)/shard_map/all_to_all | solution.py:50
  121.1 8.1 %all-to-all-done.2 = bf16[4,4,16,1408]{3,2,1,0:T(8,128)(2,1)S(1)} async-done(((bf16[4,4,16,1408]{3,2,1,0:T(8,128)(2,1)}), bf16[4,4,16,1408]{3,2,1,0:T(8,128)(2,1)S(1)}, u32[]{:S(2)}, u32[]{:S(2)}) %all-to-all-start.2) | async-done | bytes 720928 | tf_op jit(solution)/shard_map/all_to_all | solution.py:50
  129.3 4.8 %all-to-all-start.1 = ((bf16[4,16,1280]{2,1,0:T(8,128)(2,1)}), bf16[4,16,1280]{2,1,0:T(8,128)(2,1)S(1)}, u32[]{:S(2)}, u32[]{:S(2)}) async-start(bf16[4,16,1280]{2,1,0:T(8,128)(2,1)} %reduce_sum.152), calls=%async_computation.1 | async-start | bytes 327680 | tf_op jit(solution)/shard_map/all_to_all | solution.py:50
  134.8 3.9 %all-to-all-done.1 = bf16[4,16,1280]{2,1,0:T(8,128)(2,1)S(1)} async-done(((bf16[4,16,1280]{2,1,0:T(8,128)(2,1)}), bf16[4,16,1280]{2,1,0:T(8,128)(2,1)S(1)}, u32[]{:S(2)}, u32[]{:S(2)}) %all-to-all-start.1) | async-done | bytes 163872 | tf_op jit(solution)/shard_map/all_to_all | solution.py:50
  139.4 3.4 %all-to-all-start.3 = ((bf16[4,16,1408]{2,1,0:T(8,128)(2,1)}), bf16[4,16,1408]{2,1,0:T(8,128)(2,1)S(1)}, u32[]{:S(2)}, u32[]{:S(2)}) async-start(bf16[4,16,1408]{2,1,0:T(8,128)(2,1)} %reduce_sum.154), calls=%async_computation.3 | async-start | bytes 360448 | tf_op jit(solution)/shard_map/all_to_all | solution.py:50
  143.7 4.9 %all-to-all-done.3 = bf16[4,16,1408]{2,1,0:T(8,128)(2,1)S(1)} async-done(((bf16[4,16,1408]{2,1,0:T(8,128)(2,1)}), bf16[4,16,1408]{2,1,0:T(8,128)(2,1)S(1)}, u32[]{:S(2)}, u32[]{:S(2)}) %all-to-all-start.3) | async-done | bytes 180256 | tf_op jit(solution)/shard_map/all_to_all | solution.py:50
  148.8 8.2 %all_to_all.30 = bf16[4,4,2688]{2,1,0:T(4,128)(2,1)S(1)} all-to-all(bf16[4,4,2688]{2,1,0:T(4,128)(2,1)S(1)} %pad_maximum_fusion), channel_id=1, replica_groups=mesh['yh'=2,'zh'=4,'zl'=4,'x'=4,'yl'=2,'c'=2] {'zl'}, dimensions={0} | all-to-all | bytes 172032 | tf_op jit(solution)/shard_map/all_to_all | solution.py:50
  157.0 20.1 %all_to_all.31 = bf16[4,4,2688]{2,1,0:T(4,128)(2,1)S(1)} all-to-all(bf16[4,4,2688]{2,1,0:T(4,128)(2,1)S(1)} %broadcast_in_dim.25), channel_id=1, replica_groups=mesh['yh'=2,'zh'=4,'zl'=4,'x'=4,'yl'=2,'c'=2] {'zh'}, dimensions={0} | all-to-all | bytes 172032 | tf_op jit(solution)/shard_map/all_to_all | solution.py:50
  180.9 9.8 %psum.29 = f32[]{:T(128)} all-reduce(f32[]{:T(128)} %psum.28), channel_id=1, replica_groups=mesh['yh'=2,'zh'=4,'zl'=4,'x'=4,'yl'=2,'c'=2] {'yl','yh'}, use_global_device_ids=true, to_apply=%region_16.17 | all-reduce | flops 1 | bytes 8 | tf_op jit(solution)/shard_map/psum | solution.py:113
  190.7 9.8 %psum.30 = f32[]{:T(128)} all-reduce(f32[]{:T(128)} %psum.29), channel_id=1, replica_groups=mesh['yh'=2,'zh'=4,'zl'=4,'x'=4,'yl'=2,'c'=2] {'x'}, use_global_device_ids=true, to_apply=%region_17.18 | all-reduce | flops 1 | bytes 8 | tf_op jit(solution)/shard_map/psum | solution.py:113
  202.4 10.8 %psum.31 = f32[]{:T(128)} all-reduce(f32[]{:T(128)} %psum.30), channel_id=1, replica_groups=mesh['yh'=2,'zh'=4,'zl'=4,'x'=4,'yl'=2,'c'=2] {'zl'}, use_global_device_ids=true, to_apply=%region_18.19 | all-reduce | flops 1 | bytes 8 | tf_op jit(solution)/shard_map/psum | solution.py:113
  (75 shorter events, 54.6 us)
Async XLA Ops:
  0.6 16.2 %copy-start = (bf16[1152,1152]{1,0:T(8,128)(2,1)S(1)}, bf16[1152,1152]{1,0:T(8,128)(2,1)}, u32[]{:S(2)}) copy-start(bf16[1152,1152]{1,0:T(8,128)(2,1)} %param.7) | copy-start | bytes 7962628
  0.6 13.8 %copy-start.8 = (s32[1,32768]{1,0:T(1,128)S(1)}, s32[1,32768]{1,0:T(1,128)}, u32[]{:S(2)}) copy-start(s32[1,32768]{1,0:T(1,128)} %param.9) | copy-start | bytes 393220
  0.7 28.1 %collective-permute-start = (bf16[256,1152]{1,0:T(8,128)(2,1)}, bf16[256,1152]{1,0:T(8,128)(2,1)}, u32[]{:S(2)}, u32[]{:S(2)}) collective-permute-start(bf16[256,1152]{1,0:T(8,128)(2,1)} %bitcast.60), channel_id=1, source_target_pairs={{0,4},{4,8},{8,12},{12,16},{16,20},{20,24},{24,28},{28,32},{32,36}... | collective-permute-start | bytes 1769480 | tf_op jit(solution)/shard_map/ppermute | solution.py:26
  4.3 39.3 %collective-permute-start.1 = (bf16[256,1152]{1,0:T(8,128)(2,1)}, bf16[256,1152]{1,0:T(8,128)(2,1)}, u32[]{:S(2)}, u32[]{:S(2)}) collective-permute-start(bf16[256,1152]{1,0:T(8,128)(2,1)} %bitcast.61), channel_id=1, source_target_pairs={{0,508},{4,0},{8,4},{12,8},{16,12},{20,16},{24,20},{28,24},{32,28}... | collective-permute-start | bytes 1769480 | tf_op jit(solution)/shard_map/ppermute | solution.py:26
  25.2 3.5 %copy-start.6 = (bf16[256,1152]{1,0:T(8,128)(2,1)}, bf16[256,1152]{1,0:T(8,128)(2,1)S(1)}, u32[]{:S(2)}) copy-start(bf16[256,1152]{1,0:T(8,128)(2,1)S(1)} %multiply_convert_fusion.1) | copy-start | bytes 1769476
  28.8 32.3 %collective-permute-start.4 = (bf16[256,1152]{1,0:T(8,128)(2,1)}, bf16[256,1152]{1,0:T(8,128)(2,1)}, u32[]{:S(2)}, u32[]{:S(2)}) collective-permute-start(bf16[256,1152]{1,0:T(8,128)(2,1)} %collective-permute-done), channel_id=1, source_target_pairs={{0,496},{4,500},{8,504},{12,508},{16,0},{20,4},{24,8},{28,12},{32,... | collective-permute-start | bytes 1769480 | tf_op jit(solution)/shard_map/ppermute | solution.py:26
  38.9 23.4 %collective-permute-start.2 = (bf16[256,1152]{1,0:T(8,128)(2,1)}, bf16[256,1152]{1,0:T(8,128)(2,1)S(1)}, u32[]{:S(2)}, u32[]{:S(2)}) collective-permute-start(bf16[256,1152]{1,0:T(8,128)(2,1)} %collective-permute-done), channel_id=1, source_target_pairs={{0,4},{4,8},{8,12},{12,16},{16,20},{20,24},{24,28},{28,32},{32,36}... | collective-permute-start | bytes 1769480 | tf_op jit(solution)/shard_map/ppermute | solution.py:26
  43.6 16.2 %collective-permute-start.3 = (bf16[256,1152]{1,0:T(8,128)(2,1)}, bf16[256,1152]{1,0:T(8,128)(2,1)}, u32[]{:S(2)}, u32[]{:S(2)}) collective-permute-start(bf16[256,1152]{1,0:T(8,128)(2,1)} %collective-permute-done.1), channel_id=1, source_target_pairs={{0,508},{4,0},{8,4},{12,8},{16,12},{20,16},{24,20},{28,24},{32,28}... | collective-permute-start | bytes 1769480 | tf_op jit(solution)/shard_map/ppermute | solution.py:26
  74.1 1.9 copy-start.2
  76.1 1.0 copy-start.4
  77.3 2.0 copy-start.1
  79.2 5.4 %collective-permute-start.5 = (bf16[2,128,2688]{1,2,0:T(8,128)(2,1)}, bf16[2,128,2688]{1,2,0:T(8,128)(2,1)}, u32[]{:S(2)}, u32[]{:S(2)}) collective-permute-start(bf16[2,128,2688]{1,2,0:T(8,128)(2,1)} %fusion.5), channel_id=1, source_target_pairs={{0,1},{1,0},{2,3},{3,2},{4,5},{5,4},{6,7},{7,6},{8,9},{9,8},{10,11... | collective-permute-start | bytes 4128776 | tf_op jit(solution)/shard_map/ppermute | solution.py:100
  92.3 14.6 %all-to-all-start = ((bf16[4,4,16,1280]{3,2,1,0:T(8,128)(2,1)}), bf16[4,4,16,1280]{3,2,1,0:T(8,128)(2,1)S(1)}, u32[]{:S(2)}, u32[]{:S(2)}) async-start(bf16[4,4,16,1280]{3,2,1,0:T(8,128)(2,1)} %slice.13), calls=%async_computation | async-start | bytes 1310720 | tf_op jit(solution)/shard_map/all_to_all | solution.py:50
  106.9 0.8 copy-start.3
  107.7 21.6 %all-to-all-start.2 = ((bf16[4,4,16,1408]{3,2,1,0:T(8,128)(2,1)}), bf16[4,4,16,1408]{3,2,1,0:T(8,128)(2,1)S(1)}, u32[]{:S(2)}, u32[]{:S(2)}) async-start(bf16[4,4,16,1408]{3,2,1,0:T(8,128)(2,1)} %copy.28), calls=%async_computation.2 | async-start | bytes 1441792 | tf_op jit(solution)/shard_map/all_to_all | solution.py:50
  129.3 9.5 %all-to-all-start.1 = ((bf16[4,16,1280]{2,1,0:T(8,128)(2,1)}), bf16[4,16,1280]{2,1,0:T(8,128)(2,1)S(1)}, u32[]{:S(2)}, u32[]{:S(2)}) async-start(bf16[4,16,1280]{2,1,0:T(8,128)(2,1)} %reduce_sum.152), calls=%async_computation.1 | async-start | bytes 327680 | tf_op jit(solution)/shard_map/all_to_all | solution.py:50
  134.8 65.7 %copy-start.5 = (bf16[256,1152]{1,0:T(8,128)(2,1)S(1)}, bf16[256,1152]{1,0:T(8,128)(2,1)}, u32[]{:S(2)}) copy-start(bf16[256,1152]{1,0:T(8,128)(2,1)} %copy-done.4) | copy-start | bytes 1769476
  138.8 0.7 copy-start.7
  139.4 9.3 %all-to-all-start.3 = ((bf16[4,16,1408]{2,1,0:T(8,128)(2,1)}), bf16[4,16,1408]{2,1,0:T(8,128)(2,1)S(1)}, u32[]{:S(2)}, u32[]{:S(2)}) async-start(bf16[4,16,1408]{2,1,0:T(8,128)(2,1)} %reduce_sum.154), calls=%async_computation.3 | async-start | bytes 360448 | tf_op jit(solution)/shard_map/all_to_all | solution.py:50

commit v2 on v1

v2 whole, which is shorter than its diff:
```python
import functools
import math

import jax
import jax.numpy as jnp
from jax import lax
from jax.experimental import pallas as pl
from jax.experimental.pallas import tpu as pltpu
from jax.sharding import Mesh, PartitionSpec as P

LOGIT_SCALE = 10.0
LOGIT_BIAS = -3.0
LOSS_SCALE = 256.0
EPSILON = 1e-06

SHARDS = 128
ROWS = 256
D = 1152
E = 1152
SHAPE = (2, 4, 4, 4, 2, 2)
AXES = ("yh", "zh", "zl", "x", "yl", "c")
DP = ("yh", "zh", "zl", "x")
OUTER = ("yl", "c")
PLANE = ("yl", "yh", "x")
RB = 9
CB = 288
MAIN = 256
REST = 32
SPLIT = RB * MAIN
WIDTH = 2688
PICK = 2 * MAIN + 2 * 128

F32 = jnp.float32
BF16 = jnp.bfloat16
VMEM = pl.BlockSpec(memory_space=pltpu.VMEM)
SMEM = pl.BlockSpec(memory_space=pltpu.SMEM)


def shifted(value, hop):
    pairs = [(source, (source + hop) % SHARDS) for source in range(SHARDS)]
    return lax.ppermute(value, DP, pairs)


def dot(a, b):
    return jnp.dot(a, b, preferred_element_type=F32)


def dot_t(a, b):
    return lax.dot_general(a, b, (((1,), (1,)), ((), ())), preferred_element_type=F32)


def unit_rows(values):
    values = values.astype(F32)
    inverse = lax.rsqrt(jnp.sum(values * values, axis=-1, keepdims=True) + EPSILON)
    return values * inverse, inverse


def pair_grad(place, step_ref, col_ref, texts, block, position):
    images = unit_rows(block)[0].astype(BF16)
    shard = (place + (SHARDS + position - 2)) % SHARDS
    spot = pl.ds(pl.multiple_of(shard * ROWS, ROWS), ROWS)
    steps = step_ref[:, spot]
    cols = col_ref[:, spot]
    logits = LOGIT_SCALE * dot_t(texts, images) + LOGIT_BIAS
    rows = lax.broadcasted_iota(jnp.int32, logits.shape, 0)
    positive = (steps == position) & (cols == rows)
    scale = LOSS_SCALE * LOGIT_SCALE
    chance = 1.0 / (1.0 + jnp.exp(jnp.where(positive, logits, -logits)))
    weights = (jnp.where(positive, -scale, scale) * chance).astype(BF16)
    return dot(weights, images)


def first_kernel(place_ref, feat_ref, proj_ref, image_ref, step_ref, col_ref, unit_ref, inv_ref, text_ref, acc_ref):
    hidden = dot(feat_ref[...], proj_ref[...])
    unit, inverse = unit_rows(hidden)
    texts = unit.astype(BF16)
    unit_ref[...] = unit
    inv_ref[...] = jnp.broadcast_to(inverse, inv_ref.shape)
    text_ref[...] = texts
    acc_ref[...] = pair_grad(place_ref[0], step_ref, col_ref, texts, image_ref[...], 2)


def column_of(lane, core):
    tail = lane - 2 * MAIN
    pair = jnp.where(lane < 2 * MAIN, lane >> 8, tail >> 7)
    inside = jnp.where(lane < 2 * MAIN, lane & (MAIN - 1), MAIN + (lane & (REST - 1)))
    return CB * (2 * pair + core) + inside


def second_kernel(
    place_ref, feat_ref, before_ref, after_ref, step_ref, col_ref, text_ref, acc_ref, out_ref, turned_ref, there_ref, here_ref
):
    texts = text_ref[...]
    place = place_ref[0]
    total = acc_ref[...] + pair_grad(place, step_ref, col_ref, texts, before_ref[...], 1)
    out_ref[...] = total + pair_grad(place, step_ref, col_ref, texts, after_ref[...], 3)

    spot = lax.broadcasted_iota(jnp.int32, (D, 1), 0)
    within, peer = spot >> 7, spot & (SHARDS - 1)
    yh, x, zl, zh = peer >> 6, (peer >> 4) & 3, (peer >> 2) & 3, peer & 3
    source = RB * (64 * yh + 16 * zh + 4 * zl + x) + within
    lanes = lax.broadcasted_iota(jnp.int32, (D, D), 1)
    order = jnp.where(lanes == source, 1.0, 0.0).astype(BF16)
    turned_ref[...] = dot_t(order, feat_ref[...]).astype(BF16)

    core = place_ref[1]
    lane = lax.broadcasted_iota(jnp.int32, (1, PICK), 1)
    rows = lax.broadcasted_iota(jnp.int32, (E, PICK), 0)
    there_ref[...] = jnp.where(rows == column_of(lane, 1 - core), 1.0, 0.0).astype(BF16)
    here_ref[...] = jnp.where(rows == column_of(lane, core), 1.0, 0.0).astype(BF16)


def write_partial(turned_ref, picked, out_ref):
    group = lax.broadcasted_iota(jnp.int32, (SHARDS, 128), 1) // REST
    rest = [[jnp.zeros((SHARDS, 128), F32) for _ in range(3)] for _ in range(2)]
    for r in range(RB):
        block = dot(turned_ref[r * SHARDS : (r + 1) * SHARDS, :], picked)
        for pair in range(2):
            out_ref[pair, :, r * MAIN : (r + 1) * MAIN] = block[:, pair * MAIN : (pair + 1) * MAIN].astype(BF16)
            tail = block[:, 2 * MAIN + pair * 128 : 2 * MAIN + (pair + 1) * 128]
            rest[pair][r // 4] = jnp.where(group == r % 4, tail, rest[pair][r // 4])
    for pair in range(2):
        for t in range(3):
            out_ref[pair, :, SPLIT + t * 128 : SPLIT + (t + 1) * 128] = rest[pair][t].astype(BF16)


def third_kernel(
    place_ref, before2_ref, after2_ref, after3_ref, step_ref, col_ref, text_ref, acc_ref, unit_ref, inv_ref, turned_ref, pick_ref,
    grad_ref, out_ref,
):
    texts = text_ref[...]
    place = place_ref[0]
    total = acc_ref[...]
    for position, block in ((0, before2_ref), (4, after2_ref), (5, after3_ref)):
        total = total + pair_grad(place, step_ref, col_ref, texts, block[...], position)
    unit = unit_ref[...]
    radial = jnp.sum(unit * total, axis=-1, keepdims=True)
    grad = (inv_ref[:, :1] * (total - unit * radial)).astype(BF16)
    grad_ref[...] = grad
    write_partial(turned_ref, dot(grad, pick_ref[...]).astype(BF16), out_ref)


def fourth_kernel(grad_ref, turned_ref, pick_ref, proj_ref, out_ref, text_grad_ref):
    grad = grad_ref[...]
    write_partial(turned_ref, dot(grad, pick_ref[...]).astype(BF16), out_ref)
    text_grad_ref[...] = dot_t(grad, proj_ref[...]).astype(BF16)


def block_kernel(place_ref, came_ref, block_ref, square_ref):
    rows = jnp.sum(came_ref[...].astype(F32), axis=0)
    sums = jnp.sum(rows * rows, axis=0, keepdims=True)
    square = functools.reduce(jnp.add, [sums[:, t * 128 : (t + 1) * 128] for t in range(WIDTH // 128)])
    lines = lax.broadcasted_iota(jnp.int32, (8, 128), 0)
    square = jnp.where(lines == 0, jnp.broadcast_to(square, (8, 128)), 0.0)
    square_ref[...] = jnp.broadcast_to(square[None], square_ref.shape)
    mine = lax.broadcasted_iota(jnp.int32, rows.shape, 0) == place_ref[2]
    own = jnp.sum(jnp.where(mine, rows, 0.0), axis=0, keepdims=True)
    for r in range(RB):
        block_ref[r : r + 1, :MAIN] = own[:, r * MAIN : (r + 1) * MAIN]
        block_ref[r : r + 1, MAIN:] = own[:, SPLIT + r * REST : SPLIT + (r + 1) * REST]


def clip_kernel(square_ref, block_ref, out_ref):
    square = jnp.sum(jnp.sum(square_ref[...], axis=0), keepdims=True)
    factor = jnp.minimum(1.0, math.sqrt(D * E) * lax.rsqrt(square))
    out_ref[...] = block_ref[...] * factor


def call(kernel, inputs, outputs, flops, size, name):
    return pl.pallas_call(
        kernel,
        out_shape=[jax.ShapeDtypeStruct(shape, dtype) for shape, dtype in outputs],
        in_specs=[SMEM if value.shape == (3,) else VMEM for value in inputs],
        out_specs=[VMEM] * len(outputs),
        compiler_params=pltpu.CompilerParams(vmem_limit_bytes=size << 20),
        cost_estimate=pl.CostEstimate(flops=flops, bytes_accessed=4 << 20, transcendentals=0),
        name=name,
    )(*inputs)


def traded(value, axis):
    return lax.all_to_all(value, axis, split_axis=0, concat_axis=0)


def total(value):
    return jnp.sum(value.astype(F32), axis=0)


def local(image_embeds, text_features, projection, pair_step, pair_col):
    place = jnp.stack([lax.axis_index(DP), lax.axis_index("c"), lax.axis_index("zh")]).astype(jnp.int32)
    image = image_embeds[0]
    features = text_features[0]
    before = shifted(image, 1)
    after = shifted(image, -1)
    before2 = shifted(before, 1)
    after2 = shifted(after, -1)
    after3 = shifted(before, -4)

    full = (ROWS, E)
    unit, inverse, texts, acc = call(
        first_kernel,
        (place, features, projection, image, pair_step, pair_col),
        ((full, F32), ((ROWS, 128), F32), (full, BF16), (full, F32)),
        1 << 30, 24, "hidden_and_own",
    )
    acc, turned, pick_there, pick_here = call(
        second_kernel,
        (place, features, before, after, pair_step, pair_col, texts, acc),
        ((full, F32), ((D, ROWS), BF16), ((E, PICK), BF16), ((E, PICK), BF16)),
        1 << 30, 32, "near_pairs",
    )
    shape = (2, SHARDS, WIDTH)
    grad, there = call(
        third_kernel,
        (place, before2, after2, after3, pair_step, pair_col, texts, acc, unit, inverse, turned, pick_there),
        ((full, BF16), (shape, BF16)),
        1 << 30, 32, "far_pairs",
    )
    came = lax.ppermute(there, "c", [(0, 1), (1, 0)])
    here, grad_text = call(
        fourth_kernel, (grad, turned, pick_here, projection), ((shape, BF16), (full, BF16)), 1 << 30, 32, "own_half"
    )
    both = (here.astype(F32) + came.astype(F32)).astype(BF16)

    rows = total(traded(both.reshape(16, 16, WIDTH), PLANE)).astype(BF16)
    rows = total(traded(rows.reshape(4, 4, WIDTH), "zl")).astype(BF16)
    rows = traded(jnp.broadcast_to(rows[None], (4, 4, WIDTH)), "zh")
    block, square = call(
        block_kernel, (place, rows), (((RB, CB), F32), ((8, 8, 128), F32)), 1 << 20, 16, "block"
    )
    square = total(traded(square, ("yl", "yh", "c")))
    square = traded(jnp.broadcast_to(square[None], (16, 8, 128)), ("x", "zl"))
    (block,) = call(clip_kernel, (square, block), (((RB, CB), F32),), 1 << 20, 16, "clip")
    return (grad_text[None], block)


def solution(mesh):
    split = Mesh(mesh.devices.reshape(SHAPE), AXES)
    placed = (
        P(OUTER, DP, None),
        P(OUTER, DP, None),
        P(),
        P(OUTER, None),
        P(OUTER, None),
    )
    return jax.shard_map(
        local,
        mesh=split,
        in_specs=placed,
        out_specs=(P(OUTER, DP, None), P(DP, OUTER)),
        check_vma=False,
    )
```

time: 216 us -> 151 us (0.70)
  the two profiles are of different devices: /device:TPU:2 before, /device:TPU:1 now
where the time goes in v2:
time: 151 us
  blocking collectives  73 us (48%)
  starting transfers between devices  36 us (24%)
  waiting for transfers between devices  18.4 us (12%)
  Pallas kernels  16.2 us (11%)
  local copies, waits for them, and re-layouts  5.76 us (4%)
    all_to_all x5, blocking collectives, traded(): return lax.all_to_all(value, axis, split_axis=0, concat_axis=0)  73 us
    ppermute x5, starting transfers between devices, shifted(): return lax.ppermute(value, DP, pairs)  31.6 us
    ppermute x5, waiting for transfers between devices, shifted(): return lax.ppermute(value, DP, pairs)  18.4 us
    pallas_call x6, Pallas kernels, call(): pl.pallas_call(kernel, out_shape=[jax.ShapeDtypeStruct(shape, dtype) for...  16.2 us
    unnamed x16, local copies, waits for them, and re-layouts  5.7 us
    ppermute x1, starting transfers between devices, local(): came = lax.ppermute(there, 'c', [(0, 1), (1, 0)])  4.38 us
  transfers between devices with their start and end apart: 6, of which 2 were waited for; matrix products, arithmetic and copies ran while one was open for 0% of the time, Pallas kernels for 7%

profile of v2, /device:TPU:1, one launch (start us, length us, event | category | flops | bytes accessed | tf_op | source)
XLA Modules:
  0.0 150.7 jit_solution(2478316970676544290)
XLA Ops:
  0.6 4.0 %collective-permute-start = (bf16[256,1152]{1,0:T(8,128)(2,1)}, bf16[256,1152]{1,0:T(8,128)(2,1)S(1)}, u32[]{:S(2)}, u32[]{:S(2)}) collective-permute-start(bf16[256,1152]{1,0:T(8,128)(2,1)} %bitcast.7), channel_id=1, source_target_pairs={{0,4},{4,8},{8,12},{12,16},{16,20},{20,24},{24,28},{28,32},{32,36}... | collective-permute-start | bytes 1769480 | tf_op jit(solution)/shard_map/ppermute | solution.py:41
  4.6 14.8 %collective-permute-start.2 = (bf16[256,1152]{1,0:T(8,128)(2,1)}, bf16[256,1152]{1,0:T(8,128)(2,1)S(1)}, u32[]{:S(2)}, u32[]{:S(2)}) collective-permute-start(bf16[256,1152]{1,0:T(8,128)(2,1)} %bitcast.8), channel_id=1, source_target_pairs={{0,508},{4,0},{8,4},{12,8},{16,12},{20,16},{24,20},{28,24},{32,28}... | collective-permute-start | bytes 1769480 | tf_op jit(solution)/shard_map/ppermute | solution.py:41
  19.3 11.3 %collective-permute-done.before_ref = bf16[256,1152]{1,0:T(8,128)(2,1)S(1)} collective-permute-done((bf16[256,1152]{1,0:T(8,128)(2,1)}, bf16[256,1152]{1,0:T(8,128)(2,1)S(1)}, u32[]{:S(2)}, u32[]{:S(2)}) %collective-permute-start) | collective-permute-done | bytes 589856 | tf_op jit(solution)/shard_map/ppermute | solution.py:41
  30.7 1.9 %collective-permute-start.1 = (bf16[256,1152]{1,0:T(8,128)(2,1)S(1)}, bf16[256,1152]{1,0:T(8,128)(2,1)S(1)}, u32[]{:S(2)}, u32[]{:S(2)}) collective-permute-start(bf16[256,1152]{1,0:T(8,128)(2,1)S(1)} %collective-permute-done.before_ref), channel_id=1, source_target_pairs={{0,4},{4,8},{8,12},{12,16},{16,20},{20,24},{24,28},{28,32},{32,36}... | collective-permute-start | bytes 1769480 | tf_op jit(solution)/shard_map/ppermute | solution.py:41
  32.6 3.0 %collective-permute-start.4 = (bf16[256,1152]{1,0:T(8,128)(2,1)S(1)}, bf16[256,1152]{1,0:T(8,128)(2,1)S(1)}, u32[]{:S(2)}, u32[]{:S(2)}) collective-permute-start(bf16[256,1152]{1,0:T(8,128)(2,1)S(1)} %collective-permute-done.before_ref), channel_id=1, source_target_pairs={{0,496},{4,500},{8,504},{12,508},{16,0},{20,4},{24,8},{28,12},{32,... | collective-permute-start | bytes 1769480 | tf_op jit(solution)/shard_map/ppermute | solution.py:41
  35.6 8.0 %collective-permute-start.3 = (bf16[256,1152]{1,0:T(8,128)(2,1)S(1)}, bf16[256,1152]{1,0:T(8,128)(2,1)S(1)}, u32[]{:S(2)}, u32[]{:S(2)}) collective-permute-start(bf16[256,1152]{1,0:T(8,128)(2,1)S(1)} %collective-permute-done.2.after_ref), channel_id=1, source_target_pairs={{0,508},{4,0},{8,4},{12,8},{16,12},{20,16},{24,20},{28,24},{32,28}... | collective-permute-start | bytes 1769480 | tf_op jit(solution)/shard_map/ppermute | solution.py:41
  43.7 1.7 %copy-done = bf16[1152,1152]{1,0:T(8,128)(2,1)S(1)} copy-done((bf16[1152,1152]{1,0:T(8,128)(2,1)S(1)}, bf16[1152,1152]{1,0:T(8,128)(2,1)}, u32[]{:S(2)}) %copy-start) | copy-done | bytes 2654232
  45.5 1.1 copy-done.2
  46.5 1.1 copy-done.3
  47.6 0.9 copy-done.5
  48.5 0.9 copy-done.7
  49.4 2.6 %hidden_and_own.1 = (f32[256,1152]{1,0:T(8,128)S(1)}, f32[256,128]{1,0:T(8,128)S(1)}, bf16[256,1152]{1,0:T(8,128)(2,1)S(1)}, f32[256,1152]{1,0:T(8,128)S(1)}) custom-call(s32[3]{0:T(128)S(1)} %pad_add_fusion.place_ref, bf16[256,1152]{1,0:T(8,128)(2,1)S(1)} %bitcast.10, bf16[1152,1152]{1,0:T(8,128)(2,1)S(1)} %copy-done, bf16[256,1152]{1,0:T(8,128)(2,1)S(1)} %bitcast.9, ...), custom_call_target="tpu_custom_call" | custom-call | flops 1073741824 | bytes 4194304 | tf_op jit(solution)/shard_map/hidden_and_own/pallas_call | solution.py:170
  52.0 4.1 %near_pairs.1 = (f32[256,1152]{1,0:T(8,128)S(1)}, bf16[1152,256]{1,0:T(8,128)(2,1)S(1)}, bf16[1152,768]{1,0:T(8,128)(2,1)S(1)}, bf16[1152,768]{1,0:T(8,128)(2,1)S(1)}) custom-call(s32[3]{0:T(128)S(1)} %pad_add_fusion.place_ref, bf16[256,1152]{1,0:T(8,128)(2,1)S(1)} %bitcast.11, bf16[256,1152]{1,0:T(8,128)(2,1)S(1)} %collective-permute-done.before_ref, ...), custom_call_target="tpu_custom_call" | custom-call | flops 1073741824 | bytes 4194304 | tf_op jit(solution)/shard_map/near_pairs/pallas_call | solution.py:170
  56.1 7.0 %collective-permute-done.3.after2_ref = bf16[256,1152]{1,0:T(8,128)(2,1)S(1)} collective-permute-done((bf16[256,1152]{1,0:T(8,128)(2,1)S(1)}, bf16[256,1152]{1,0:T(8,128)(2,1)S(1)}, u32[]{:S(2)}, u32[]{:S(2)}) %collective-permute-start.3) | collective-permute-done | bytes 589856 | tf_op jit(solution)/shard_map/ppermute | solution.py:41
  63.1 4.6 %far_pairs.1 = (bf16[256,1152]{1,0:T(8,128)(2,1)S(1)}, bf16[2,128,2688]{2,1,0:T(8,128)(2,1)S(1)}) custom-call(s32[3]{0:T(128)S(1)} %pad_add_fusion.place_ref, bf16[256,1152]{1,0:T(8,128)(2,1)S(1)} %collective-permute-done.1.before2_ref, bf16[256,1152]{1,0:T(8,128)(2,1)S(1)} %collective-permute-done.3.after2_ref, ...), custom_call_target="tpu_custom_call" | custom-call | flops 1073741824 | bytes 4194304 | tf_op jit(solution)/shard_map/far_pairs/pallas_call | solution.py:170
  67.8 4.4 %collective-permute-start.5 = (bf16[2,128,2688]{2,1,0:T(8,128)(2,1)S(1)}, bf16[2,128,2688]{2,1,0:T(8,128)(2,1)S(1)}, u32[]{:S(2)}, u32[]{:S(2)}) collective-permute-start(bf16[2,128,2688]{2,1,0:T(8,128)(2,1)S(1)} %get-tuple-element.27), channel_id=1, source_target_pairs={{0,1},{1,0},{2,3},{3,2},{4,5},{5,4},{6,7},{7,6},{8,9},{9,8},{10,11... | collective-permute-start | bytes 4128776 | tf_op jit(solution)/shard_map/ppermute | solution.py:219
  72.1 3.5 %own_half.1 = (bf16[2,128,2688]{2,1,0:T(8,128)(2,1)S(1)}, bf16[256,1152]{1,0:T(8,128)(2,1)}) custom-call(bf16[256,1152]{1,0:T(8,128)(2,1)S(1)} %get-tuple-element.23.grad_ref, bf16[1152,256]{1,0:T(8,128)(2,1)S(1)} %get-tuple-element.21.turned_ref, bf16[1152,768]{1,0:T(8,128)(2,1)S(1)} %get-tuple-element.24.pick_ref, bf16[1152,1152]{1,0:T(8,128)(2,1)S(1)} %copy-done.1), custom_call_target="tpu_custom_call" | custom-call | flops 1073741824 | bytes 4194304 | tf_op jit(solution)/shard_map/own_half/pallas_call | solution.py:170
  75.9 23.2 %all_to_all.25 = bf16[16,16,2688]{2,1,0:T(8,128)(2,1)S(1)} all-to-all(bf16[16,16,2688]{2,1,0:T(8,128)(2,1)S(1)} %bitcast.12), channel_id=1, replica_groups=mesh['yh'=2,'zh'=4,'zl'=4,'x'=4,'yl'=2,'c'=2] {'yl','yh','x'}, dimensions={0} | all-to-all | bytes 2752512 | tf_op jit(solution)/shard_map/all_to_all | solution.py:182
  99.4 7.0 %all_to_all.26 = bf16[4,4,2688]{2,1,0:T(4,128)(2,1)S(1)} all-to-all(bf16[4,4,2688]{2,1,0:T(4,128)(2,1)S(1)} %reshape.13), channel_id=1, replica_groups=mesh['yh'=2,'zh'=4,'zl'=4,'x'=4,'yl'=2,'c'=2] {'zl'}, dimensions={0} | all-to-all | bytes 172032 | tf_op jit(solution)/shard_map/all_to_all | solution.py:182
  106.5 21.4 %all_to_all.27.came_ref = bf16[4,4,2688]{2,1,0:T(4,128)(2,1)S(1)} all-to-all(bf16[4,4,2688]{2,1,0:T(4,128)(2,1)S(1)} %broadcast_in_dim.7), channel_id=1, replica_groups=mesh['yh'=2,'zh'=4,'zl'=4,'x'=4,'yl'=2,'c'=2] {'zh'}, dimensions={0} | all-to-all | bytes 172032 | tf_op jit(solution)/shard_map/all_to_all | solution.py:182
  127.9 0.7 block.1
  128.6 11.1 %all_to_all.28 = f32[8,8,128]{2,1,0:T(8,128)S(1)} all-to-all(f32[8,8,128]{2,1,0:T(8,128)S(1)} %get-tuple-element.28), channel_id=1, replica_groups=mesh['yh'=2,'zh'=4,'zl'=4,'x'=4,'yl'=2,'c'=2] {'yl','yh','c'}, dimensions={0} | all-to-all | bytes 65536 | tf_op jit(solution)/shard_map/all_to_all | solution.py:182
  139.7 10.3 %all_to_all.29.square_ref = f32[16,8,128]{2,1,0:T(8,128)S(1)} all-to-all(f32[16,8,128]{2,1,0:T(8,128)S(1)} %broadcast_in_dim.8), channel_id=1, replica_groups=mesh['yh'=2,'zh'=4,'zl'=4,'x'=4,'yl'=2,'c'=2] {'x','zl'}, dimensions={0} | all-to-all | bytes 131072 | tf_op jit(solution)/shard_map/all_to_all | solution.py:182
  150.0 0.7 clip.1
  (23 shorter events, 0.7 us)
Async XLA Ops:
  0.6 30.0 %collective-permute-start = (bf16[256,1152]{1,0:T(8,128)(2,1)}, bf16[256,1152]{1,0:T(8,128)(2,1)S(1)}, u32[]{:S(2)}, u32[]{:S(2)}) collective-permute-start(bf16[256,1152]{1,0:T(8,128)(2,1)} %bitcast.7), channel_id=1, source_target_pairs={{0,4},{4,8},{8,12},{12,16},{16,20},{20,24},{24,28},{28,32},{32,36}... | collective-permute-start | bytes 1769480 | tf_op jit(solution)/shard_map/ppermute | solution.py:41
  4.6 31.0 %collective-permute-start.2 = (bf16[256,1152]{1,0:T(8,128)(2,1)}, bf16[256,1152]{1,0:T(8,128)(2,1)S(1)}, u32[]{:S(2)}, u32[]{:S(2)}) collective-permute-start(bf16[256,1152]{1,0:T(8,128)(2,1)} %bitcast.8), channel_id=1, source_target_pairs={{0,508},{4,0},{8,4},{12,8},{16,12},{20,16},{24,20},{28,24},{32,28}... | collective-permute-start | bytes 1769480 | tf_op jit(solution)/shard_map/ppermute | solution.py:41
  30.7 25.4 %collective-permute-start.1 = (bf16[256,1152]{1,0:T(8,128)(2,1)S(1)}, bf16[256,1152]{1,0:T(8,128)(2,1)S(1)}, u32[]{:S(2)}, u32[]{:S(2)}) collective-permute-start(bf16[256,1152]{1,0:T(8,128)(2,1)S(1)} %collective-permute-done.before_ref), channel_id=1, source_target_pairs={{0,4},{4,8},{8,12},{12,16},{16,20},{20,24},{24,28},{28,32},{32,36}... | collective-permute-start | bytes 1769480 | tf_op jit(solution)/shard_map/ppermute | solution.py:41
  32.6 23.5 %collective-permute-start.4 = (bf16[256,1152]{1,0:T(8,128)(2,1)S(1)}, bf16[256,1152]{1,0:T(8,128)(2,1)S(1)}, u32[]{:S(2)}, u32[]{:S(2)}) collective-permute-start(bf16[256,1152]{1,0:T(8,128)(2,1)S(1)} %collective-permute-done.before_ref), channel_id=1, source_target_pairs={{0,496},{4,500},{8,504},{12,508},{16,0},{20,4},{24,8},{28,12},{32,... | collective-permute-start | bytes 1769480 | tf_op jit(solution)/shard_map/ppermute | solution.py:41
  35.6 27.6 %collective-permute-start.3 = (bf16[256,1152]{1,0:T(8,128)(2,1)S(1)}, bf16[256,1152]{1,0:T(8,128)(2,1)S(1)}, u32[]{:S(2)}, u32[]{:S(2)}) collective-permute-start(bf16[256,1152]{1,0:T(8,128)(2,1)S(1)} %collective-permute-done.2.after_ref), channel_id=1, source_target_pairs={{0,508},{4,0},{8,4},{12,8},{16,12},{20,16},{24,20},{28,24},{32,28}... | collective-permute-start | bytes 1769480 | tf_op jit(solution)/shard_map/ppermute | solution.py:41
  43.7 1.8 %copy-start = (bf16[1152,1152]{1,0:T(8,128)(2,1)S(1)}, bf16[1152,1152]{1,0:T(8,128)(2,1)}, u32[]{:S(2)}) copy-start(bf16[1152,1152]{1,0:T(8,128)(2,1)} %proj_ref.3) | copy-start | bytes 7962628
  45.5 1.1 copy-start.2
  46.5 1.1 copy-start.3
  47.6 0.9 copy-start.5
  48.5 0.9 copy-start.7
  49.4 2.6 %copy-start.4 = (bf16[1,256,1152]{2,1,0:T(8,128)(2,1)S(1)}, bf16[1,256,1152]{2,1,0:T(8,128)(2,1)}, u32[]{:S(2)}) copy-start(bf16[1,256,1152]{2,1,0:T(8,128)(2,1)} %param.6) | copy-start | bytes 1769476
  49.4 2.6 %copy-start.6 = (s32[1,32768]{1,0:T(1,128)S(1)}, s32[1,32768]{1,0:T(1,128)}, u32[]{:S(2)}) copy-start(s32[1,32768]{1,0:T(1,128)} %step_ref.5) | copy-start | bytes 393220
  63.1 9.0 %copy-start.1 = (bf16[1152,1152]{1,0:T(8,128)(2,1)S(1)}, bf16[1152,1152]{1,0:T(8,128)(2,1)}, u32[]{:S(2)}) copy-start(bf16[1152,1152]{1,0:T(8,128)(2,1)} %proj_ref.3) | copy-start | bytes 7962628
  67.8 7.9 %collective-permute-start.5 = (bf16[2,128,2688]{2,1,0:T(8,128)(2,1)S(1)}, bf16[2,128,2688]{2,1,0:T(8,128)(2,1)S(1)}, u32[]{:S(2)}, u32[]{:S(2)}) collective-permute-start(bf16[2,128,2688]{2,1,0:T(8,128)(2,1)S(1)} %get-tuple-element.27), channel_id=1, source_target_pairs={{0,1},{1,0},{2,3},{3,2},{4,5},{5,4},{6,7},{7,6},{8,9},{9,8},{10,11... | collective-permute-start | bytes 4128776 | tf_op jit(solution)/shard_map/ppermute | solution.py:219

commit v3 on v2

--- a/solution.py
+++ b/solution.py
@@ -21,7 +21,8 @@
 AXES = ("yh", "zh", "zl", "x", "yl", "c")
 DP = ("yh", "zh", "zl", "x")
 OUTER = ("yl", "c")
-PLANE = ("yl", "yh", "x")
+PLANE = ("yh", "yl", "x")
+LINE = ("zh", "zl")
 RB = 9
 CB = 288
 MAIN = 256
@@ -36,9 +37,25 @@
 SMEM = pl.BlockSpec(memory_space=pltpu.SMEM)
 
 
-def shifted(value, hop):
-    pairs = [(source, (source + hop) % SHARDS) for source in range(SHARDS)]
+RIGHT = (1, 1, 1, -3)
+LEFT = (-1, -1, -1, -1)
+RIGHT2 = (1, 1, 1, 1)
+LEFT2 = (-1, -1, 3, -1)
+ACROSS = (4, -4, -4, -4)
+RIGHT_AT = (5, 1, 1, 1)
+LEFT_AT = (3, 3, 3, 3)
+RIGHT2_AT = (0, 4, 0, 0)
+LEFT2_AT = (4, 0, 4, 4)
+ACROSS_AT = (1, 5, 5, 5)
+
+
+def shifted(value, hops):
+    pairs = [(source, (source + hops[source % 4]) % SHARDS) for source in range(SHARDS)]
     return lax.ppermute(value, DP, pairs)
+
+
+def position_of(x, places):
+    return jnp.where(x == 0, places[0], jnp.where(x == 1, places[1], jnp.where(x == 2, places[2], places[3])))
 
 
 def dot(a, b):
@@ -57,7 +74,7 @@
 
 def pair_grad(place, step_ref, col_ref, texts, block, position):
     images = unit_rows(block)[0].astype(BF16)
-    shard = (place + (SHARDS + position - 2)) % SHARDS
+    shard = (place + (position + (SHARDS - 2))) & (SHARDS - 1)
     spot = pl.ds(pl.multiple_of(shard * ROWS, ROWS), ROWS)
     steps = step_ref[:, spot]
     cols = col_ref[:, spot]
@@ -92,13 +109,13 @@
 ):
     texts = text_ref[...]
     place = place_ref[0]
-    total = acc_ref[...] + pair_grad(place, step_ref, col_ref, texts, before_ref[...], 1)
+    total = acc_ref[...] + pair_grad(place, step_ref, col_ref, texts, before_ref[...], place_ref[2])
     out_ref[...] = total + pair_grad(place, step_ref, col_ref, texts, after_ref[...], 3)
 
     spot = lax.broadcasted_iota(jnp.int32, (D, 1), 0)
     within, peer = spot >> 7, spot & (SHARDS - 1)
-    yh, x, zl, zh = peer >> 6, (peer >> 4) & 3, (peer >> 2) & 3, peer & 3
-    source = RB * (64 * yh + 16 * zh + 4 * zl + x) + within
+    yh, x, z = peer >> 6, (peer >> 4) & 3, peer & 15
+    source = RB * (64 * yh + 4 * z + x) + within
     lanes = lax.broadcasted_iota(jnp.int32, (D, D), 1)
     order = jnp.where(lanes == source, 1.0, 0.0).astype(BF16)
     turned_ref[...] = dot_t(order, feat_ref[...]).astype(BF16)
@@ -111,28 +128,33 @@
 
 
 def write_partial(turned_ref, picked, out_ref):
+    half = SHARDS // 2
     group = lax.broadcasted_iota(jnp.int32, (SHARDS, 128), 1) // REST
     rest = [[jnp.zeros((SHARDS, 128), F32) for _ in range(3)] for _ in range(2)]
     for r in range(RB):
         block = dot(turned_ref[r * SHARDS : (r + 1) * SHARDS, :], picked)
         for pair in range(2):
-            out_ref[pair, :, r * MAIN : (r + 1) * MAIN] = block[:, pair * MAIN : (pair + 1) * MAIN].astype(BF16)
+            main = block[:, pair * MAIN : (pair + 1) * MAIN].astype(BF16)
+            for yh in range(2):
+                out_ref[yh, pair, :, r * MAIN : (r + 1) * MAIN] = main[yh * half : (yh + 1) * half]
             tail = block[:, 2 * MAIN + pair * 128 : 2 * MAIN + (pair + 1) * 128]
             rest[pair][r // 4] = jnp.where(group == r % 4, tail, rest[pair][r // 4])
     for pair in range(2):
         for t in range(3):
-            out_ref[pair, :, SPLIT + t * 128 : SPLIT + (t + 1) * 128] = rest[pair][t].astype(BF16)
+            tail = rest[pair][t].astype(BF16)
+            for yh in range(2):
+                out_ref[yh, pair, :, SPLIT + t * 128 : SPLIT + (t + 1) * 128] = tail[yh * half : (yh + 1) * half]
 
 
 def third_kernel(
-    place_ref, before2_ref, after2_ref, after3_ref, step_ref, col_ref, text_ref, acc_ref, unit_ref, inv_ref, turned_ref, pick_ref,
+    place_ref, right_ref, left_ref, across_ref, step_ref, col_ref, text_ref, acc_ref, unit_ref, inv_ref, turned_ref, pick_ref,
     grad_ref, out_ref,
 ):
     texts = text_ref[...]
     place = place_ref[0]
     total = acc_ref[...]
-    for position, block in ((0, before2_ref), (4, after2_ref), (5, after3_ref)):
-        total = total + pair_grad(place, step_ref, col_ref, texts, block[...], position)
+    for at, block in ((3, right_ref), (4, left_ref), (5, across_ref)):
+        total = total + pair_grad(place, step_ref, col_ref, texts, block[...], place_ref[at])
     unit = unit_ref[...]
     radial = jnp.sum(unit * total, axis=-1, keepdims=True)
     grad = (inv_ref[:, :1] * (total - unit * radial)).astype(BF16)
@@ -146,15 +168,13 @@
     text_grad_ref[...] = dot_t(grad, proj_ref[...]).astype(BF16)
 
 
-def block_kernel(place_ref, came_ref, block_ref, square_ref):
-    rows = jnp.sum(came_ref[...].astype(F32), axis=0)
-    sums = jnp.sum(rows * rows, axis=0, keepdims=True)
+def block_kernel(came_ref, block_ref, square_ref):
+    own = jnp.sum(came_ref[...].astype(F32), axis=0, keepdims=True)
+    sums = own * own
     square = functools.reduce(jnp.add, [sums[:, t * 128 : (t + 1) * 128] for t in range(WIDTH // 128)])
     lines = lax.broadcasted_iota(jnp.int32, (8, 128), 0)
     square = jnp.where(lines == 0, jnp.broadcast_to(square, (8, 128)), 0.0)
     square_ref[...] = jnp.broadcast_to(square[None], square_ref.shape)
-    mine = lax.broadcasted_iota(jnp.int32, rows.shape, 0) == place_ref[2]
-    own = jnp.sum(jnp.where(mine, rows, 0.0), axis=0, keepdims=True)
     for r in range(RB):
         block_ref[r : r + 1, :MAIN] = own[:, r * MAIN : (r + 1) * MAIN]
         block_ref[r : r + 1, MAIN:] = own[:, SPLIT + r * REST : SPLIT + (r + 1) * REST]
@@ -170,7 +190,7 @@
     return pl.pallas_call(
         kernel,
         out_shape=[jax.ShapeDtypeStruct(shape, dtype) for shape, dtype in outputs],
-        in_specs=[SMEM if value.shape == (3,) else VMEM for value in inputs],
+        in_specs=[SMEM if value.ndim == 1 else VMEM for value in inputs],
         out_specs=[VMEM] * len(outputs),
         compiler_params=pltpu.CompilerParams(vmem_limit_bytes=size << 20),
         cost_estimate=pl.CostEstimate(flops=flops, bytes_accessed=4 << 20, transcendentals=0),
@@ -187,14 +207,16 @@
 
 
 def local(image_embeds, text_features, projection, pair_step, pair_col):
-    place = jnp.stack([lax.axis_index(DP), lax.axis_index("c"), lax.axis_index("zh")]).astype(jnp.int32)
+    x = lax.axis_index("x")
+    places = (RIGHT_AT, RIGHT2_AT, LEFT2_AT, ACROSS_AT)
+    place = jnp.stack([lax.axis_index(DP), lax.axis_index("c")] + [position_of(x, at) for at in places]).astype(jnp.int32)
     image = image_embeds[0]
     features = text_features[0]
-    before = shifted(image, 1)
-    after = shifted(image, -1)
-    before2 = shifted(before, 1)
-    after2 = shifted(after, -1)
-    after3 = shifted(before, -4)
+    right = shifted(image, RIGHT)
+    left = shifted(image, LEFT)
+    right2 = shifted(right, RIGHT2)
+    left2 = shifted(left, LEFT2)
+    across = shifted(right, ACROSS)
 
     full = (ROWS, E)
     unit, inverse, texts, acc = call(
@@ -205,14 +227,14 @@
     )
     acc, turned, pick_there, pick_here = call(
         second_kernel,
-        (place, features, before, after, pair_step, pair_col, texts, acc),
+        (place, features, right, left, pair_step, pair_col, texts, acc),
         ((full, F32), ((D, ROWS), BF16), ((E, PICK), BF16), ((E, PICK), BF16)),
         1 << 30, 32, "near_pairs",
     )
-    shape = (2, SHARDS, WIDTH)
+    shape = (2, 2, SHARDS // 2, WIDTH)
     grad, there = call(
         third_kernel,
-        (place, before2, after2, after3, pair_step, pair_col, texts, acc, unit, inverse, turned, pick_there),
+        (place, right2, left2, across, pair_step, pair_col, texts, acc, unit, inverse, turned, pick_there),
         ((full, BF16), (shape, BF16)),
         1 << 30, 32, "far_pairs",
     )
@@ -223,13 +245,10 @@
     both = (here.astype(F32) + came.astype(F32)).astype(BF16)
 
     rows = total(traded(both.reshape(16, 16, WIDTH), PLANE)).astype(BF16)
-    rows = total(traded(rows.reshape(4, 4, WIDTH), "zl")).astype(BF16)
-    rows = traded(jnp.broadcast_to(rows[None], (4, 4, WIDTH)), "zh")
-    block, square = call(
-        block_kernel, (place, rows), (((RB, CB), F32), ((8, 8, 128), F32)), 1 << 20, 16, "block"
-    )
-    square = total(traded(square, ("yl", "yh", "c")))
-    square = traded(jnp.broadcast_to(square[None], (16, 8, 128)), ("x", "zl"))
+    rows = traded(rows.reshape(16, 1, WIDTH), LINE).reshape(16, WIDTH)
+    block, square = call(block_kernel, (rows,), (((RB, CB), F32), ((32, 8, 128), F32)), 1 << 20, 16, "block")
+    square = total(traded(square, PLANE + ("c",)))
+    square = traded(jnp.broadcast_to(square[None], (16, 8, 128)), LINE)
     (block,) = call(clip_kernel, (square, block), (((RB, CB), F32),), 1 << 20, 16, "clip")
     return (grad_text[None], block)
 

time: 151 us -> 144 us (0.954)
  waiting for transfers between devices: 18.4 us -> 11.3 us
  blocking collectives: 73 us -> 69.7 us
  starting transfers between devices: 36 us -> 38.1 us
    ppermute x5, waiting for transfers between devices: 18.4 us -> 11.3 us  [shifted(): return lax.ppermute(value, DP, pairs)]
    all_to_all x5 -> x4, blocking collectives: 73 us -> 69.7 us  [traded(): return lax.all_to_all(value, axis, split_axis=0, concat_axis=0)]
    ppermute x5, starting transfers between devices: 31.6 us -> 33.5 us  [shifted(): return lax.ppermute(value, DP, pairs)]
    unnamed x16 -> x19, local copies, waits for them, and re-layouts: 5.7 us -> 5.99 us
  transfers between devices with their start and end apart: 6 -> 6, of which waited for: 2 -> 3; matrix products, arithmetic and copies ran while one was open for 0% -> 0% of each run, Pallas kernels for 7% -> 7%
where the time goes in v3:
time: 144 us; the launch traced here: 143 us
  blocking collectives  69.7 us (48%)
  starting transfers between devices  38.1 us (26%)
  Pallas kernels  15.5 us (11%)
  waiting for transfers between devices  11.3 us (8%)
  local copies, waits for them, and re-layouts  6.6 us (5%)
    all_to_all x4, blocking collectives, traded(): return lax.all_to_all(value, axis, split_axis=0, concat_axis=0)  69.7 us
    ppermute x5, starting transfers between devices, shifted(): return lax.ppermute(value, DP, pairs)  33.5 us
    pallas_call x6, Pallas kernels, call(): pl.pallas_call(kernel, out_shape=[jax.ShapeDtypeStruct(shape, dtype) for...  15.5 us
    ppermute x5, waiting for transfers between devices, shifted(): return lax.ppermute(value, DP, pairs)  11.3 us
    unnamed x19, local copies, waits for them, and re-layouts  5.99 us
    ppermute x1, starting transfers between devices, local(): came = lax.ppermute(there, 'c', [(0, 1), (1, 0)])  4.66 us
  transfers between devices with their start and end apart: 6, of which 3 were waited for; matrix products, arithmetic and copies ran while one was open for 0% of the time, Pallas kernels for 7%

profile of v3, /device:TPU:1, one launch (start us, length us, event | category | flops | bytes accessed | tf_op | source)
XLA Modules:
  0.0 143.2 jit_solution(4643562906882138014)
XLA Ops:
  0.6 4.0 %collective-permute-start = (bf16[256,1152]{1,0:T(8,128)(2,1)}, bf16[256,1152]{1,0:T(8,128)(2,1)S(1)}, u32[]{:S(2)}, u32[]{:S(2)}) collective-permute-start(bf16[256,1152]{1,0:T(8,128)(2,1)} %bitcast.14), channel_id=1, source_target_pairs={{0,4},{4,8},{8,12},{12,0},{16,20},{20,24},{24,28},{28,16},{32,36},... | collective-permute-start | bytes 1769480 | tf_op jit(solution)/shard_map/ppermute | solution.py:54
  4.6 14.9 %collective-permute-start.2 = (bf16[256,1152]{1,0:T(8,128)(2,1)}, bf16[256,1152]{1,0:T(8,128)(2,1)S(1)}, u32[]{:S(2)}, u32[]{:S(2)}) collective-permute-start(bf16[256,1152]{1,0:T(8,128)(2,1)} %bitcast.15), channel_id=1, source_target_pairs={{0,508},{4,0},{8,4},{12,8},{16,12},{20,16},{24,20},{28,24},{32,28}... | collective-permute-start | bytes 1769480 | tf_op jit(solution)/shard_map/ppermute | solution.py:54
  19.5 1.9 %collective-permute-start.1 = (bf16[256,1152]{1,0:T(8,128)(2,1)S(1)}, bf16[256,1152]{1,0:T(8,128)(2,1)S(1)}, u32[]{:S(2)}, u32[]{:S(2)}) collective-permute-start(bf16[256,1152]{1,0:T(8,128)(2,1)S(1)} %collective-permute-done.before_ref), channel_id=1, source_target_pairs={{0,4},{4,8},{8,12},{12,16},{16,20},{20,24},{24,28},{28,32},{32,36}... | collective-permute-start | bytes 1769480 | tf_op jit(solution)/shard_map/ppermute | solution.py:54
  21.5 3.0 %collective-permute-start.4 = (bf16[256,1152]{1,0:T(8,128)(2,1)S(1)}, bf16[256,1152]{1,0:T(8,128)(2,1)S(1)}, u32[]{:S(2)}, u32[]{:S(2)}) collective-permute-start(bf16[256,1152]{1,0:T(8,128)(2,1)S(1)} %collective-permute-done.before_ref), channel_id=1, source_target_pairs={{0,16},{4,500},{8,504},{12,508},{16,32},{20,4},{24,8},{28,12},{32,... | collective-permute-start | bytes 1769480 | tf_op jit(solution)/shard_map/ppermute | solution.py:54
  24.4 7.1 %collective-permute-done.2.after_ref = bf16[256,1152]{1,0:T(8,128)(2,1)S(1)} collective-permute-done((bf16[256,1152]{1,0:T(8,128)(2,1)}, bf16[256,1152]{1,0:T(8,128)(2,1)S(1)}, u32[]{:S(2)}, u32[]{:S(2)}) %collective-permute-start.2) | collective-permute-done | bytes 589856 | tf_op jit(solution)/shard_map/ppermute | solution.py:54
  31.5 9.7 %collective-permute-start.3 = (bf16[256,1152]{1,0:T(8,128)(2,1)S(1)}, bf16[256,1152]{1,0:T(8,128)(2,1)S(1)}, u32[]{:S(2)}, u32[]{:S(2)}) collective-permute-start(bf16[256,1152]{1,0:T(8,128)(2,1)S(1)} %collective-permute-done.2.after_ref), channel_id=1, source_target_pairs={{0,508},{4,0},{8,20},{12,8},{16,12},{20,16},{24,36},{28,24},{32,28... | collective-permute-start | bytes 1769480 | tf_op jit(solution)/shard_map/ppermute | solution.py:54
  41.3 1.8 %copy-done = bf16[1152,1152]{1,0:T(8,128)(2,1)S(1)} copy-done((bf16[1152,1152]{1,0:T(8,128)(2,1)S(1)}, bf16[1152,1152]{1,0:T(8,128)(2,1)}, u32[]{:S(2)}) %copy-start) | copy-done | bytes 2654232
  43.1 1.1 copy-done.2
  44.2 1.1 copy-done.3
  45.2 0.9 copy-done.5
  46.1 0.9 copy-done.7
  47.0 2.6 %hidden_and_own.1 = (f32[256,1152]{1,0:T(8,128)S(1)}, f32[256,128]{1,0:T(8,128)S(1)}, bf16[256,1152]{1,0:T(8,128)(2,1)S(1)}, f32[256,1152]{1,0:T(8,128)S(1)}) custom-call(s32[6]{0:T(128)S(1)} %stack.27.place_ref, bf16[256,1152]{1,0:T(8,128)(2,1)S(1)} %bitcast.17, bf16[1152,1152]{1,0:T(8,128)(2,1)S(1)} %copy-done, bf16[256,1152]{1,0:T(8,128)(2,1)S(1)} %bitcast.16, ...), custom_call_target="tpu_custom_call" | custom-call | flops 1073741824 | bytes 4194304 | tf_op jit(solution)/shard_map/hidden_and_own/pallas_call | solution.py:190
  49.6 4.0 %near_pairs.1 = (f32[256,1152]{1,0:T(8,128)S(1)}, bf16[1152,256]{1,0:T(8,128)(2,1)S(1)}, bf16[1152,768]{1,0:T(8,128)(2,1)S(1)}, bf16[1152,768]{1,0:T(8,128)(2,1)S(1)}) custom-call(s32[6]{0:T(128)S(1)} %stack.27.place_ref, bf16[256,1152]{1,0:T(8,128)(2,1)S(1)} %bitcast.18, bf16[256,1152]{1,0:T(8,128)(2,1)S(1)} %collective-permute-done.before_ref, ...), custom_call_target="tpu_custom_call" | custom-call | flops 1073741824 | bytes 4194304 | tf_op jit(solution)/shard_map/near_pairs/pallas_call | solution.py:190
  53.9 4.0 %collective-permute-done.4.across_ref = bf16[256,1152]{1,0:T(8,128)(2,1)S(1)} collective-permute-done((bf16[256,1152]{1,0:T(8,128)(2,1)S(1)}, bf16[256,1152]{1,0:T(8,128)(2,1)S(1)}, u32[]{:S(2)}, u32[]{:S(2)}) %collective-permute-start.4) | collective-permute-done | bytes 589856 | tf_op jit(solution)/shard_map/ppermute | solution.py:54
  57.9 4.6 %far_pairs.1 = (bf16[256,1152]{1,0:T(8,128)(2,1)S(1)}, bf16[2,2,64,2688]{3,2,1,0:T(8,128)(2,1)S(1)}) custom-call(s32[6]{0:T(128)S(1)} %stack.27.place_ref, bf16[256,1152]{1,0:T(8,128)(2,1)S(1)} %collective-permute-done.1.right_ref, bf16[256,1152]{1,0:T(8,128)(2,1)S(1)} %collective-permute-done.3.left_ref, ...), custom_call_target="tpu_custom_call" | custom-call | flops 1073741824 | bytes 4194304 | tf_op jit(solution)/shard_map/far_pairs/pallas_call | solution.py:190
  62.5 4.7 %collective-permute-start.5 = (bf16[2,2,64,2688]{3,2,1,0:T(8,128)(2,1)S(1)}, bf16[2,2,64,2688]{3,2,1,0:T(8,128)(2,1)S(1)}, u32[]{:S(2)}, u32[]{:S(2)}) collective-permute-start(bf16[2,2,64,2688]{3,2,1,0:T(8,128)(2,1)S(1)} %get-tuple-element.27), channel_id=1, source_target_pairs={{0,1},{1,0},{2,3},{3,2},{4,5},{5,4},{6,7},{7,6},{8,9},{9,8},{10,11... | collective-permute-start | bytes 4128776 | tf_op jit(solution)/shard_map/ppermute | solution.py:241
  67.2 3.5 %own_half.1 = (bf16[2,2,64,2688]{3,2,1,0:T(8,128)(2,1)S(1)}, bf16[256,1152]{1,0:T(8,128)(2,1)}) custom-call(bf16[256,1152]{1,0:T(8,128)(2,1)S(1)} %get-tuple-element.23.grad_ref, bf16[1152,256]{1,0:T(8,128)(2,1)S(1)} %get-tuple-element.21.turned_ref, bf16[1152,768]{1,0:T(8,128)(2,1)S(1)} %get-tuple-element.24.pick_ref, bf16[1152,1152]{1,0:T(8,128)(2,1)S(1)} %copy-done.1), custom_call_target="tpu_custom_call" | custom-call | flops 1073741824 | bytes 4194304 | tf_op jit(solution)/shard_map/own_half/pallas_call | solution.py:190
  71.0 23.2 %all_to_all.20 = bf16[16,16,2688]{2,1,0:T(8,128)(2,1)S(1)} all-to-all(bf16[16,16,2688]{2,1,0:T(8,128)(2,1)S(1)} %bitcast.20), channel_id=1, replica_groups=mesh['yh'=2,'zh'=4,'zl'=4,'x'=4,'yl'=2,'c'=2] {'yh','yl','x'}, dimensions={0} | all-to-all | bytes 2752512 | tf_op jit(solution)/shard_map/all_to_all | solution.py:202
  94.4 0.5 broadcast.1
  94.9 0.7 reduce.1
  95.7 18.6 %all_to_all.21 = bf16[16,2,1344]{2,1,0:T(2,128)(2,1)S(1)} all-to-all(bf16[16,2,1344]{2,1,0:T(2,128)(2,1)S(1)} %reshape.17), channel_id=1, replica_groups=mesh['yh'=2,'zh'=4,'zl'=4,'x'=4,'yl'=2,'c'=2] {'zh','zl'}, dimensions={0} | all-to-all | bytes 172032 | tf_op jit(solution)/shard_map/all_to_all | solution.py:202
  114.5 13.5 %all_to_all.22 = f32[32,8,128]{2,1,0:T(8,128)S(1)} all-to-all(f32[32,8,128]{2,1,0:T(8,128)S(1)} %get-tuple-element.28), channel_id=1, replica_groups=mesh['yh'=2,'zh'=4,'zl'=4,'x'=4,'yl'=2,'c'=2] {'yh','yl','x','c'}, dimensions={0} | all-to-all | bytes 262144 | tf_op jit(solution)/shard_map/all_to_all | solution.py:202
  128.1 14.4 %all_to_all.23.square_ref = f32[16,8,128]{2,1,0:T(8,128)S(1)} all-to-all(f32[16,8,128]{2,1,0:T(8,128)S(1)} %broadcast_in_dim.10), channel_id=1, replica_groups=mesh['yh'=2,'zh'=4,'zl'=4,'x'=4,'yl'=2,'c'=2] {'zh','zl'}, dimensions={0} | all-to-all | bytes 131072 | tf_op jit(solution)/shard_map/all_to_all | solution.py:202
  142.5 0.7 clip.1
  (24 shorter events, 1.2 us)
Async XLA Ops:
  0.6 18.9 %collective-permute-start = (bf16[256,1152]{1,0:T(8,128)(2,1)}, bf16[256,1152]{1,0:T(8,128)(2,1)S(1)}, u32[]{:S(2)}, u32[]{:S(2)}) collective-permute-start(bf16[256,1152]{1,0:T(8,128)(2,1)} %bitcast.14), channel_id=1, source_target_pairs={{0,4},{4,8},{8,12},{12,0},{16,20},{20,24},{24,28},{28,16},{32,36},... | collective-permute-start | bytes 1769480 | tf_op jit(solution)/shard_map/ppermute | solution.py:54
  4.6 26.9 %collective-permute-start.2 = (bf16[256,1152]{1,0:T(8,128)(2,1)}, bf16[256,1152]{1,0:T(8,128)(2,1)S(1)}, u32[]{:S(2)}, u32[]{:S(2)}) collective-permute-start(bf16[256,1152]{1,0:T(8,128)(2,1)} %bitcast.15), channel_id=1, source_target_pairs={{0,508},{4,0},{8,4},{12,8},{16,12},{20,16},{24,20},{28,24},{32,28}... | collective-permute-start | bytes 1769480 | tf_op jit(solution)/shard_map/ppermute | solution.py:54
  19.5 34.3 %collective-permute-start.1 = (bf16[256,1152]{1,0:T(8,128)(2,1)S(1)}, bf16[256,1152]{1,0:T(8,128)(2,1)S(1)}, u32[]{:S(2)}, u32[]{:S(2)}) collective-permute-start(bf16[256,1152]{1,0:T(8,128)(2,1)S(1)} %collective-permute-done.before_ref), channel_id=1, source_target_pairs={{0,4},{4,8},{8,12},{12,16},{16,20},{20,24},{24,28},{28,32},{32,36}... | collective-permute-start | bytes 1769480 | tf_op jit(solution)/shard_map/ppermute | solution.py:54
  21.5 36.4 %collective-permute-start.4 = (bf16[256,1152]{1,0:T(8,128)(2,1)S(1)}, bf16[256,1152]{1,0:T(8,128)(2,1)S(1)}, u32[]{:S(2)}, u32[]{:S(2)}) collective-permute-start(bf16[256,1152]{1,0:T(8,128)(2,1)S(1)} %collective-permute-done.before_ref), channel_id=1, source_target_pairs={{0,16},{4,500},{8,504},{12,508},{16,32},{20,4},{24,8},{28,12},{32,... | collective-permute-start | bytes 1769480 | tf_op jit(solution)/shard_map/ppermute | solution.py:54
  31.5 26.4 %collective-permute-start.3 = (bf16[256,1152]{1,0:T(8,128)(2,1)S(1)}, bf16[256,1152]{1,0:T(8,128)(2,1)S(1)}, u32[]{:S(2)}, u32[]{:S(2)}) collective-permute-start(bf16[256,1152]{1,0:T(8,128)(2,1)S(1)} %collective-permute-done.2.after_ref), channel_id=1, source_target_pairs={{0,508},{4,0},{8,20},{12,8},{16,12},{20,16},{24,36},{28,24},{32,28... | collective-permute-start | bytes 1769480 | tf_op jit(solution)/shard_map/ppermute | solution.py:54
  41.3 1.8 %copy-start = (bf16[1152,1152]{1,0:T(8,128)(2,1)S(1)}, bf16[1152,1152]{1,0:T(8,128)(2,1)}, u32[]{:S(2)}) copy-start(bf16[1152,1152]{1,0:T(8,128)(2,1)} %proj_ref.3) | copy-start | bytes 7962628
  43.1 1.1 copy-start.2
  44.2 1.1 copy-start.3
  45.2 0.9 copy-start.5
  46.1 0.9 copy-start.7
  47.0 2.6 %copy-start.4 = (bf16[1,256,1152]{2,1,0:T(8,128)(2,1)S(1)}, bf16[1,256,1152]{2,1,0:T(8,128)(2,1)}, u32[]{:S(2)}) copy-start(bf16[1,256,1152]{2,1,0:T(8,128)(2,1)} %param.6) | copy-start | bytes 1769476
  47.0 2.6 %copy-start.6 = (s32[1,32768]{1,0:T(1,128)S(1)}, s32[1,32768]{1,0:T(1,128)}, u32[]{:S(2)}) copy-start(s32[1,32768]{1,0:T(1,128)} %step_ref.5) | copy-start | bytes 393220
  57.9 9.3 %copy-start.1 = (bf16[1152,1152]{1,0:T(8,128)(2,1)S(1)}, bf16[1152,1152]{1,0:T(8,128)(2,1)}, u32[]{:S(2)}) copy-start(bf16[1152,1152]{1,0:T(8,128)(2,1)} %proj_ref.3) | copy-start | bytes 7962628
  62.5 8.1 %collective-permute-start.5 = (bf16[2,2,64,2688]{3,2,1,0:T(8,128)(2,1)S(1)}, bf16[2,2,64,2688]{3,2,1,0:T(8,128)(2,1)S(1)}, u32[]{:S(2)}, u32[]{:S(2)}) collective-permute-start(bf16[2,2,64,2688]{3,2,1,0:T(8,128)(2,1)S(1)} %get-tuple-element.27), channel_id=1, source_target_pairs={{0,1},{1,0},{2,3},{3,2},{4,5},{5,4},{6,7},{7,6},{8,9},{9,8},{10,11... | collective-permute-start | bytes 4128776 | tf_op jit(solution)/shard_map/ppermute | solution.py:241

commit v4 on v3

--- a/solution.py
+++ b/solution.py
@@ -17,12 +17,11 @@
 ROWS = 256
 D = 1152
 E = 1152
-SHAPE = (2, 4, 4, 4, 2, 2)
-AXES = ("yh", "zh", "zl", "x", "yl", "c")
-DP = ("yh", "zh", "zl", "x")
+SHAPE = (2, 4, 2, 2, 4, 2, 2)
+AXES = ("yh", "zh", "z1", "z0", "x", "yl", "c")
+DP = ("yh", "zh", "z1", "z0", "x")
 OUTER = ("yl", "c")
-PLANE = ("yh", "yl", "x")
-LINE = ("zh", "zl")
+NEAR = ("yh", "yl", "x", "z0")
 RB = 9
 CB = 288
 MAIN = 256
@@ -114,8 +113,8 @@
 
     spot = lax.broadcasted_iota(jnp.int32, (D, 1), 0)
     within, peer = spot >> 7, spot & (SHARDS - 1)
-    yh, x, z = peer >> 6, (peer >> 4) & 3, peer & 15
-    source = RB * (64 * yh + 4 * z + x) + within
+    yh, x, z0, z = peer >> 6, (peer >> 4) & 3, (peer >> 3) & 1, peer & 7
+    source = RB * (64 * yh + 8 * z + 4 * z0 + x) + within
     lanes = lax.broadcasted_iota(jnp.int32, (D, D), 1)
     order = jnp.where(lanes == source, 1.0, 0.0).astype(BF16)
     turned_ref[...] = dot_t(order, feat_ref[...]).astype(BF16)
@@ -146,15 +145,16 @@
                 out_ref[yh, pair, :, SPLIT + t * 128 : SPLIT + (t + 1) * 128] = tail[yh * half : (yh + 1) * half]
 
 
+def far_kernel(at, place_ref, image_ref, step_ref, col_ref, text_ref, acc_ref, out_ref):
+    part = pair_grad(place_ref[0], step_ref, col_ref, text_ref[...], image_ref[...], place_ref[at])
+    out_ref[...] = acc_ref[...] + part
+
+
 def third_kernel(
-    place_ref, right_ref, left_ref, across_ref, step_ref, col_ref, text_ref, acc_ref, unit_ref, inv_ref, turned_ref, pick_ref,
-    grad_ref, out_ref,
+    place_ref, left_ref, step_ref, col_ref, text_ref, acc_ref, unit_ref, inv_ref, turned_ref, pick_ref, grad_ref, out_ref
 ):
-    texts = text_ref[...]
-    place = place_ref[0]
-    total = acc_ref[...]
-    for at, block in ((3, right_ref), (4, left_ref), (5, across_ref)):
-        total = total + pair_grad(place, step_ref, col_ref, texts, block[...], place_ref[at])
+    part = pair_grad(place_ref[0], step_ref, col_ref, text_ref[...], left_ref[...], place_ref[4])
+    total = acc_ref[...] + part
     unit = unit_ref[...]
     radial = jnp.sum(unit * total, axis=-1, keepdims=True)
     grad = (inv_ref[:, :1] * (total - unit * radial)).astype(BF16)
@@ -168,13 +168,15 @@
     text_grad_ref[...] = dot_t(grad, proj_ref[...]).astype(BF16)
 
 
-def block_kernel(came_ref, block_ref, square_ref):
-    own = jnp.sum(came_ref[...].astype(F32), axis=0, keepdims=True)
-    sums = own * own
+def block_kernel(place_ref, came_ref, block_ref, square_ref):
+    rows = jnp.sum(came_ref[...].astype(F32), axis=0)
+    sums = jnp.sum(rows * rows, axis=0, keepdims=True)
     square = functools.reduce(jnp.add, [sums[:, t * 128 : (t + 1) * 128] for t in range(WIDTH // 128)])
     lines = lax.broadcasted_iota(jnp.int32, (8, 128), 0)
     square = jnp.where(lines == 0, jnp.broadcast_to(square, (8, 128)), 0.0)
     square_ref[...] = jnp.broadcast_to(square[None], square_ref.shape)
+    mine = lax.broadcasted_iota(jnp.int32, rows.shape, 0) == place_ref[6]
+    own = jnp.sum(jnp.where(mine, rows, 0.0), axis=0, keepdims=True)
     for r in range(RB):
         block_ref[r : r + 1, :MAIN] = own[:, r * MAIN : (r + 1) * MAIN]
         block_ref[r : r + 1, MAIN:] = own[:, SPLIT + r * REST : SPLIT + (r + 1) * REST]
@@ -209,7 +211,7 @@
 def local(image_embeds, text_features, projection, pair_step, pair_col):
     x = lax.axis_index("x")
     places = (RIGHT_AT, RIGHT2_AT, LEFT2_AT, ACROSS_AT)
-    place = jnp.stack([lax.axis_index(DP), lax.axis_index("c")] + [position_of(x, at) for at in places]).astype(jnp.int32)
+    place = jnp.stack([lax.axis_index(DP), lax.axis_index("c")] + [position_of(x, at) for at in places] + [lax.axis_index(("zh", "z1"))]).astype(jnp.int32)
     image = image_embeds[0]
     features = text_features[0]
     right = shifted(image, RIGHT)
@@ -232,11 +234,15 @@
         1 << 30, 32, "near_pairs",
     )
     shape = (2, 2, SHARDS // 2, WIDTH)
+    for at, block, name in ((3, right2, "far_right"), (5, across, "far_across")):
+        (acc,) = call(
+            functools.partial(far_kernel, at), (place, block, pair_step, pair_col, texts, acc), ((full, F32),), 1 << 28, 24, name
+        )
     grad, there = call(
         third_kernel,
-        (place, right2, left2, across, pair_step, pair_col, texts, acc, unit, inverse, turned, pick_there),
+        (place, left2, pair_step, pair_col, texts, acc, unit, inverse, turned, pick_there),
         ((full, BF16), (shape, BF16)),
-        1 << 30, 32, "far_pairs",
+        1 << 30, 32, "far_left",
     )
     came = lax.ppermute(there, "c", [(0, 1), (1, 0)])
     here, grad_text = call(
@@ -244,11 +250,11 @@
     )
     both = (here.astype(F32) + came.astype(F32)).astype(BF16)
 
-    rows = total(traded(both.reshape(16, 16, WIDTH), PLANE)).astype(BF16)
-    rows = traded(rows.reshape(16, 1, WIDTH), LINE).reshape(16, WIDTH)
-    block, square = call(block_kernel, (rows,), (((RB, CB), F32), ((32, 8, 128), F32)), 1 << 20, 16, "block")
-    square = total(traded(square, PLANE + ("c",)))
-    square = traded(jnp.broadcast_to(square[None], (16, 8, 128)), LINE)
+    rows = total(traded(both.reshape(32, 8, WIDTH), NEAR)).astype(BF16)
+    rows = (rows.astype(F32) + lax.ppermute(rows, "z1", [(0, 1), (1, 0)]).astype(F32)).astype(BF16)
+    rows = traded(jnp.broadcast_to(rows[None], (4, 8, WIDTH)), "zh")
+    block, square = call(block_kernel, (place, rows), (((RB, CB), F32), ((64, 8, 128), F32)), 1 << 20, 16, "block")
+    square = traded(square, NEAR + ("c",))
     (block,) = call(clip_kernel, (square, block), (((RB, CB), F32),), 1 << 20, 16, "clip")
     return (grad_text[None], block)
 

time: 144 us -> 142 us (0.986)
  blocking collectives: 69.7 us -> 61.9 us
  Pallas kernels: 15.5 us -> 18.2 us
  waiting for transfers between devices: 11.3 us -> 13.7 us
  starting transfers between devices: 38.1 us -> 40.2 us
    all_to_all x4 -> x3, blocking collectives: 69.7 us -> 61.9 us  [traded(): return lax.all_to_all(value, axis, split_axis=0, concat_axis=0)]
    ppermute x0 -> x1, waiting for transfers between devices: none -> 4.2 us  [local(): lax.ppermute(rows, 'z1', [(0, 1), (1, 0)]).astype(F32)]
    pallas_call x6 -> x8, Pallas kernels: 15.5 us -> 18.2 us  [call(): pl.pallas_call(kernel, out_shape=[jax.ShapeDtypeStruct(shape, dtype) for...]
    ppermute x0 -> x1, starting transfers between devices: none -> 1.92 us  [local(): lax.ppermute(rows, 'z1', [(0, 1), (1, 0)]).astype(F32)]
    ppermute x5, waiting for transfers between devices: 11.3 us -> 9.54 us  [shifted(): return lax.ppermute(value, DP, pairs)]
    unnamed x19 -> x18, local copies, waits for them, and re-layouts: 5.99 us -> 5.7 us
  transfers between devices with their start and end apart: 6 -> 7, of which waited for: 3 -> 4; matrix products, arithmetic and copies ran while one was open for 0% -> 0% of each run, Pallas kernels for 7% -> 9%
where the time goes in v4:
time: 142 us; the launch traced here: 141 us
  blocking collectives  61.9 us (44%)
  starting transfers between devices  40.2 us (28%)
  Pallas kernels  18.2 us (13%)
  waiting for transfers between devices  13.7 us (10%)
  local copies, waits for them, and re-layouts  5.8 us (4%)
    all_to_all x3, blocking collectives, traded(): return lax.all_to_all(value, axis, split_axis=0, concat_axis=0)  61.9 us
    ppermute x5, starting transfers between devices, shifted(): return lax.ppermute(value, DP, pairs)  33.5 us
    pallas_call x8, Pallas kernels, call(): pl.pallas_call(kernel, out_shape=[jax.ShapeDtypeStruct(shape, dtype) for...  18.2 us
    ppermute x5, waiting for transfers between devices, shifted(): return lax.ppermute(value, DP, pairs)  9.54 us
    unnamed x18, local copies, waits for them, and re-layouts  5.7 us
    ppermute x1, starting transfers between devices, local(): came = lax.ppermute(there, 'c', [(0, 1), (1, 0)])  4.84 us
    ppermute x1, waiting for transfers between devices, local(): lax.ppermute(rows, 'z1', [(0, 1), (1, 0)]).astype(F32)  4.2 us
  transfers between devices with their start and end apart: 7, of which 4 were waited for; matrix products, arithmetic and copies ran while one was open for 0% of the time, Pallas kernels for 9%

profile of v4, /device:TPU:1, one launch (start us, length us, event | category | flops | bytes accessed | tf_op | source)
XLA Modules:
  0.0 141.4 jit_solution(10922116709984621750)
XLA Ops:
  0.6 4.0 %collective-permute-start.2 = (bf16[256,1152]{1,0:T(8,128)(2,1)}, bf16[256,1152]{1,0:T(8,128)(2,1)S(1)}, u32[]{:S(2)}, u32[]{:S(2)}) collective-permute-start(bf16[256,1152]{1,0:T(8,128)(2,1)} %bitcast.11), channel_id=1, source_target_pairs={{0,4},{4,8},{8,12},{12,0},{16,20},{20,24},{24,28},{28,16},{32,36},... | collective-permute-start | bytes 1769480 | tf_op jit(solution)/shard_map/ppermute | solution.py:53
  4.6 14.9 %collective-permute-start = (bf16[256,1152]{1,0:T(8,128)(2,1)}, bf16[256,1152]{1,0:T(8,128)(2,1)S(1)}, u32[]{:S(2)}, u32[]{:S(2)}) collective-permute-start(bf16[256,1152]{1,0:T(8,128)(2,1)} %bitcast.12), channel_id=1, source_target_pairs={{0,508},{4,0},{8,4},{12,8},{16,12},{20,16},{24,20},{28,24},{32,28}... | collective-permute-start | bytes 1769480 | tf_op jit(solution)/shard_map/ppermute | solution.py:53
  19.5 1.9 %collective-permute-start.4 = (bf16[256,1152]{1,0:T(8,128)(2,1)S(1)}, bf16[256,1152]{1,0:T(8,128)(2,1)S(1)}, u32[]{:S(2)}, u32[]{:S(2)}) collective-permute-start(bf16[256,1152]{1,0:T(8,128)(2,1)S(1)} %collective-permute-done.2.before_ref), channel_id=1, source_target_pairs={{0,4},{4,8},{8,12},{12,16},{16,20},{20,24},{24,28},{28,32},{32,36}... | collective-permute-start | bytes 1769480 | tf_op jit(solution)/shard_map/ppermute | solution.py:53
  21.5 3.0 %collective-permute-start.3 = (bf16[256,1152]{1,0:T(8,128)(2,1)S(1)}, bf16[256,1152]{1,0:T(8,128)(2,1)S(1)}, u32[]{:S(2)}, u32[]{:S(2)}) collective-permute-start(bf16[256,1152]{1,0:T(8,128)(2,1)S(1)} %collective-permute-done.2.before_ref), channel_id=1, source_target_pairs={{0,16},{4,500},{8,504},{12,508},{16,32},{20,4},{24,8},{28,12},{32,... | collective-permute-start | bytes 1769480 | tf_op jit(solution)/shard_map/ppermute | solution.py:53
  24.4 7.1 %collective-permute-done.after_ref = bf16[256,1152]{1,0:T(8,128)(2,1)S(1)} collective-permute-done((bf16[256,1152]{1,0:T(8,128)(2,1)}, bf16[256,1152]{1,0:T(8,128)(2,1)S(1)}, u32[]{:S(2)}, u32[]{:S(2)}) %collective-permute-start) | collective-permute-done | bytes 589856 | tf_op jit(solution)/shard_map/ppermute | solution.py:53
  31.5 9.7 %collective-permute-start.1 = (bf16[256,1152]{1,0:T(8,128)(2,1)S(1)}, bf16[256,1152]{1,0:T(8,128)(2,1)S(1)}, u32[]{:S(2)}, u32[]{:S(2)}) collective-permute-start(bf16[256,1152]{1,0:T(8,128)(2,1)S(1)} %collective-permute-done.after_ref), channel_id=1, source_target_pairs={{0,508},{4,0},{8,20},{12,8},{16,12},{20,16},{24,36},{28,24},{32,28... | collective-permute-start | bytes 1769480 | tf_op jit(solution)/shard_map/ppermute | solution.py:53
  41.3 1.7 %copy-done = bf16[1152,1152]{1,0:T(8,128)(2,1)S(1)} copy-done((bf16[1152,1152]{1,0:T(8,128)(2,1)S(1)}, bf16[1152,1152]{1,0:T(8,128)(2,1)}, u32[]{:S(2)}) %copy-start) | copy-done | bytes 2654232
  43.1 0.9 copy-done.2
  44.0 0.9 copy-done.4
  44.9 1.1 copy-done.6
  46.0 1.1 copy-done.7
  47.0 2.6 %hidden_and_own.1 = (f32[256,1152]{1,0:T(8,128)S(1)}, f32[256,128]{1,0:T(8,128)S(1)}, bf16[256,1152]{1,0:T(8,128)(2,1)S(1)}, f32[256,1152]{1,0:T(8,128)S(1)}) custom-call(s32[7]{0:T(128)S(1)} %stack.31.place_ref, bf16[256,1152]{1,0:T(8,128)(2,1)S(1)} %bitcast.14, bf16[1152,1152]{1,0:T(8,128)(2,1)S(1)} %copy-done, bf16[256,1152]{1,0:T(8,128)(2,1)S(1)} %bitcast.13, ...), custom_call_target="tpu_custom_call" | custom-call | flops 1073741824 | bytes 4194304 | tf_op jit(solution)/shard_map/hidden_and_own/pallas_call | solution.py:192
  49.6 4.1 %near_pairs.1 = (f32[256,1152]{1,0:T(8,128)S(1)}, bf16[1152,256]{1,0:T(8,128)(2,1)S(1)}, bf16[1152,768]{1,0:T(8,128)(2,1)S(1)}, bf16[1152,768]{1,0:T(8,128)(2,1)S(1)}) custom-call(s32[7]{0:T(128)S(1)} %stack.31.place_ref, bf16[256,1152]{1,0:T(8,128)(2,1)S(1)} %bitcast.15, bf16[256,1152]{1,0:T(8,128)(2,1)S(1)} %collective-permute-done.2.before_ref, ...), custom_call_target="tpu_custom_call" | custom-call | flops 1073741824 | bytes 4194304 | tf_op jit(solution)/shard_map/near_pairs/pallas_call | solution.py:192
  53.9 1.6 %far_right.1.acc_ref = f32[256,1152]{1,0:T(8,128)S(1)} custom-call(s32[7]{0:T(128)S(1)} %stack.31.place_ref, bf16[256,1152]{1,0:T(8,128)(2,1)S(1)} %collective-permute-done.4.image_ref, s32[1,32768]{1,0:T(1,128)S(1)} %copy-done.3, s32[1,32768]{1,0:T(1,128)S(1)} %copy-done.5, bf16[256,1152]{1,0:T(8,128)(2,1)S(1)} %get-tuple-element.16.text_ref, ...), custom_call_target="tpu_custom_call" | custom-call | flops 268435456 | bytes 4194304 | tf_op jit(solution)/shard_map/far_right/pallas_call | solution.py:192
  55.5 2.4 %collective-permute-done.3.image_ref = bf16[256,1152]{1,0:T(8,128)(2,1)S(1)} collective-permute-done((bf16[256,1152]{1,0:T(8,128)(2,1)S(1)}, bf16[256,1152]{1,0:T(8,128)(2,1)S(1)}, u32[]{:S(2)}, u32[]{:S(2)}) %collective-permute-start.3) | collective-permute-done | bytes 589856 | tf_op jit(solution)/shard_map/ppermute | solution.py:53
  57.9 1.6 %far_across.1.acc_ref = f32[256,1152]{1,0:T(8,128)S(1)} custom-call(s32[7]{0:T(128)S(1)} %stack.31.place_ref, bf16[256,1152]{1,0:T(8,128)(2,1)S(1)} %collective-permute-done.3.image_ref, s32[1,32768]{1,0:T(1,128)S(1)} %copy-done.3, s32[1,32768]{1,0:T(1,128)S(1)} %copy-done.5, bf16[256,1152]{1,0:T(8,128)(2,1)S(1)} %get-tuple-element.16.text_ref, ...), custom_call_target="tpu_custom_call" | custom-call | flops 268435456 | bytes 4194304 | tf_op jit(solution)/shard_map/far_across/pallas_call | solution.py:192
  59.5 3.4 %far_left.1 = (bf16[256,1152]{1,0:T(8,128)(2,1)S(1)}, bf16[2,2,64,2688]{3,2,1,0:T(8,128)(2,1)S(1)}) custom-call(s32[7]{0:T(128)S(1)} %stack.31.place_ref, bf16[256,1152]{1,0:T(8,128)(2,1)S(1)} %collective-permute-done.1.left_ref, s32[1,32768]{1,0:T(1,128)S(1)} %copy-done.3, s32[1,32768]{1,0:T(1,128)S(1)} %copy-done.5, ...), custom_call_target="tpu_custom_call" | custom-call | flops 1073741824 | bytes 4194304 | tf_op jit(solution)/shard_map/far_left/pallas_call | solution.py:192
  62.9 4.8 %collective-permute-start.5 = (bf16[2,2,64,2688]{3,2,1,0:T(8,128)(2,1)S(1)}, bf16[2,2,64,2688]{3,2,1,0:T(8,128)(2,1)S(1)}, u32[]{:S(2)}, u32[]{:S(2)}) collective-permute-start(bf16[2,2,64,2688]{3,2,1,0:T(8,128)(2,1)S(1)} %get-tuple-element.27), channel_id=1, source_target_pairs={{0,1},{1,0},{2,3},{3,2},{4,5},{5,4},{6,7},{7,6},{8,9},{9,8},{10,11... | collective-permute-start | bytes 4128776 | tf_op jit(solution)/shard_map/ppermute | solution.py:247
  67.8 3.5 %own_half.1 = (bf16[2,2,64,2688]{3,2,1,0:T(8,128)(2,1)S(1)}, bf16[256,1152]{1,0:T(8,128)(2,1)}) custom-call(bf16[256,1152]{1,0:T(8,128)(2,1)S(1)} %get-tuple-element.23.grad_ref, bf16[1152,256]{1,0:T(8,128)(2,1)S(1)} %get-tuple-element.21.turned_ref, bf16[1152,768]{1,0:T(8,128)(2,1)S(1)} %get-tuple-element.24.pick_ref, bf16[1152,1152]{1,0:T(8,128)(2,1)S(1)} %copy-done.1), custom_call_target="tpu_custom_call" | custom-call | flops 1073741824 | bytes 4194304 | tf_op jit(solution)/shard_map/own_half/pallas_call | solution.py:192
  71.6 24.2 %all_to_all.15 = bf16[32,8,2688]{2,1,0:T(8,128)(2,1)S(1)} all-to-all(bf16[32,8,2688]{2,1,0:T(8,128)(2,1)S(1)} %bitcast.16), channel_id=1, replica_groups=mesh['yh'=2,'zh'=4,'z1'=2,'z0'=2,'x'=4,'yl'=2,'c'=2] {'yh','yl','x','z0'}, dimensions={0} | all-to-all | bytes 2752512 | tf_op jit(solution)/shard_map/all_to_all | solution.py:204
  96.0 1.9 %collective-permute-start.6 = (bf16[8,2688]{1,0:T(8,128)(2,1)S(1)}, bf16[8,2688]{1,0:T(8,128)(2,1)S(1)}, u32[]{:S(2)}, u32[]{:S(2)}) collective-permute-start(bf16[8,2688]{1,0:T(8,128)(2,1)S(1)} %reduce_sum.12), channel_id=1, source_target_pairs={{0,32},{32,0},{1,33},{33,1},{2,34},{34,2},{3,35},{35,3},{4,36},{36... | collective-permute-start | bytes 129032 | tf_op jit(solution)/shard_map/ppermute | solution.py:254
  97.9 4.2 %collective-permute-done.6 = bf16[8,2688]{1,0:T(8,128)(2,1)S(1)} collective-permute-done((bf16[8,2688]{1,0:T(8,128)(2,1)S(1)}, bf16[8,2688]{1,0:T(8,128)(2,1)S(1)}, u32[]{:S(2)}, u32[]{:S(2)}) %collective-permute-start.6) | collective-permute-done | bytes 43040 | tf_op jit(solution)/shard_map/ppermute | solution.py:254
  102.1 18.9 %all_to_all.16.came_ref = bf16[4,8,2688]{2,1,0:T(8,128)(2,1)S(1)} all-to-all(bf16[4,8,2688]{2,1,0:T(8,128)(2,1)S(1)} %broadcast_in_dim.10), channel_id=1, replica_groups=mesh['yh'=2,'zh'=4,'z1'=2,'z0'=2,'x'=4,'yl'=2,'c'=2] {'zh'}, dimensions={0} | all-to-all | bytes 344064 | tf_op jit(solution)/shard_map/all_to_all | solution.py:204
  121.7 18.8 %all_to_all.17.square_ref = f32[64,8,128]{2,1,0:T(8,128)S(1)} all-to-all(f32[64,8,128]{2,1,0:T(8,128)S(1)} %get-tuple-element.28), channel_id=1, replica_groups=mesh['yh'=2,'zh'=4,'z1'=2,'z0'=2,'x'=4,'yl'=2,'c'=2] {'yh','yl','x','z0'..., dimensions={0} | all-to-all | bytes 524288 | tf_op jit(solution)/shard_map/all_to_all | solution.py:204
  (24 shorter events, 2.3 us)
Async XLA Ops:
  0.6 18.9 %collective-permute-start.2 = (bf16[256,1152]{1,0:T(8,128)(2,1)}, bf16[256,1152]{1,0:T(8,128)(2,1)S(1)}, u32[]{:S(2)}, u32[]{:S(2)}) collective-permute-start(bf16[256,1152]{1,0:T(8,128)(2,1)} %bitcast.11), channel_id=1, source_target_pairs={{0,4},{4,8},{8,12},{12,0},{16,20},{20,24},{24,28},{28,16},{32,36},... | collective-permute-start | bytes 1769480 | tf_op jit(solution)/shard_map/ppermute | solution.py:53
  4.6 26.9 %collective-permute-start = (bf16[256,1152]{1,0:T(8,128)(2,1)}, bf16[256,1152]{1,0:T(8,128)(2,1)S(1)}, u32[]{:S(2)}, u32[]{:S(2)}) collective-permute-start(bf16[256,1152]{1,0:T(8,128)(2,1)} %bitcast.12), channel_id=1, source_target_pairs={{0,508},{4,0},{8,4},{12,8},{16,12},{20,16},{24,20},{28,24},{32,28}... | collective-permute-start | bytes 1769480 | tf_op jit(solution)/shard_map/ppermute | solution.py:53
  19.5 34.3 %collective-permute-start.4 = (bf16[256,1152]{1,0:T(8,128)(2,1)S(1)}, bf16[256,1152]{1,0:T(8,128)(2,1)S(1)}, u32[]{:S(2)}, u32[]{:S(2)}) collective-permute-start(bf16[256,1152]{1,0:T(8,128)(2,1)S(1)} %collective-permute-done.2.before_ref), channel_id=1, source_target_pairs={{0,4},{4,8},{8,12},{12,16},{16,20},{20,24},{24,28},{28,32},{32,36}... | collective-permute-start | bytes 1769480 | tf_op jit(solution)/shard_map/ppermute | solution.py:53
  21.5 36.4 %collective-permute-start.3 = (bf16[256,1152]{1,0:T(8,128)(2,1)S(1)}, bf16[256,1152]{1,0:T(8,128)(2,1)S(1)}, u32[]{:S(2)}, u32[]{:S(2)}) collective-permute-start(bf16[256,1152]{1,0:T(8,128)(2,1)S(1)} %collective-permute-done.2.before_ref), channel_id=1, source_target_pairs={{0,16},{4,500},{8,504},{12,508},{16,32},{20,4},{24,8},{28,12},{32,... | collective-permute-start | bytes 1769480 | tf_op jit(solution)/shard_map/ppermute | solution.py:53
  31.5 28.0 %collective-permute-start.1 = (bf16[256,1152]{1,0:T(8,128)(2,1)S(1)}, bf16[256,1152]{1,0:T(8,128)(2,1)S(1)}, u32[]{:S(2)}, u32[]{:S(2)}) collective-permute-start(bf16[256,1152]{1,0:T(8,128)(2,1)S(1)} %collective-permute-done.after_ref), channel_id=1, source_target_pairs={{0,508},{4,0},{8,20},{12,8},{16,12},{20,16},{24,36},{28,24},{32,28... | collective-permute-start | bytes 1769480 | tf_op jit(solution)/shard_map/ppermute | solution.py:53
  41.3 1.8 %copy-start = (bf16[1152,1152]{1,0:T(8,128)(2,1)S(1)}, bf16[1152,1152]{1,0:T(8,128)(2,1)}, u32[]{:S(2)}) copy-start(bf16[1152,1152]{1,0:T(8,128)(2,1)} %proj_ref.3) | copy-start | bytes 7962628
  43.1 0.9 copy-start.2
  44.0 0.9 copy-start.4
  44.9 1.1 copy-start.6
  46.0 1.1 copy-start.7
  47.0 2.6 %copy-start.3 = (s32[1,32768]{1,0:T(1,128)S(1)}, s32[1,32768]{1,0:T(1,128)}, u32[]{:S(2)}) copy-start(s32[1,32768]{1,0:T(1,128)} %step_ref.9) | copy-start | bytes 393220
  47.0 2.6 %copy-start.5 = (s32[1,32768]{1,0:T(1,128)S(1)}, s32[1,32768]{1,0:T(1,128)}, u32[]{:S(2)}) copy-start(s32[1,32768]{1,0:T(1,128)} %col_ref.9) | copy-start | bytes 393220
  47.0 2.6 %copy-start.8 = (bf16[1,256,1152]{2,1,0:T(8,128)(2,1)S(1)}, bf16[1,256,1152]{2,1,0:T(8,128)(2,1)}, u32[]{:S(2)}) copy-start(bf16[1,256,1152]{2,1,0:T(8,128)(2,1)} %param.6) | copy-start | bytes 1769476
  59.5 8.2 %copy-start.1 = (bf16[1152,1152]{1,0:T(8,128)(2,1)S(1)}, bf16[1152,1152]{1,0:T(8,128)(2,1)}, u32[]{:S(2)}) copy-start(bf16[1152,1152]{1,0:T(8,128)(2,1)} %proj_ref.3) | copy-start | bytes 7962628
  62.9 8.3 %collective-permute-start.5 = (bf16[2,2,64,2688]{3,2,1,0:T(8,128)(2,1)S(1)}, bf16[2,2,64,2688]{3,2,1,0:T(8,128)(2,1)S(1)}, u32[]{:S(2)}, u32[]{:S(2)}) collective-permute-start(bf16[2,2,64,2688]{3,2,1,0:T(8,128)(2,1)S(1)} %get-tuple-element.27), channel_id=1, source_target_pairs={{0,1},{1,0},{2,3},{3,2},{4,5},{5,4},{6,7},{7,6},{8,9},{9,8},{10,11... | collective-permute-start | bytes 4128776 | tf_op jit(solution)/shard_map/ppermute | solution.py:247
  96.0 6.1 %collective-permute-start.6 = (bf16[8,2688]{1,0:T(8,128)(2,1)S(1)}, bf16[8,2688]{1,0:T(8,128)(2,1)S(1)}, u32[]{:S(2)}, u32[]{:S(2)}) collective-permute-start(bf16[8,2688]{1,0:T(8,128)(2,1)S(1)} %reduce_sum.12), channel_id=1, source_target_pairs={{0,32},{32,0},{1,33},{33,1},{2,34},{34,2},{3,35},{35,3},{4,36},{36... | collective-permute-start | bytes 129032 | tf_op jit(solution)/shard_map/ppermute | solution.py:254

commit v5 on v4

v5 whole, which is shorter than its diff:
```python
import functools
import math

import jax
import jax.numpy as jnp
from jax import lax
from jax.experimental import pallas as pl
from jax.experimental.pallas import tpu as pltpu
from jax.sharding import Mesh, PartitionSpec as P

LOGIT_SCALE = 10.0
LOGIT_BIAS = -3.0
LOSS_SCALE = 256.0
EPSILON = 1e-06

SHARDS = 128
ROWS = 256
D = 1152
E = 1152
SHAPE = (2, 4, 2, 2, 4, 2, 2)
AXES = ("yh", "zh", "z1", "z0", "x", "yl", "c")
DP = ("yh", "zh", "z1", "z0", "x")
OUTER = ("yl", "c")
SIDE = ("yh", "x", "z0")
NEAR = ("yh", "x", "z0", "yl", "c")
RB = 9
CB = 288
MAIN = 256
REST = 32
SPLIT = RB * MAIN
WIDTH = 2688
PICK = MAIN + 128

F32 = jnp.float32
BF16 = jnp.bfloat16
VMEM = pl.BlockSpec(memory_space=pltpu.VMEM)
SMEM = pl.BlockSpec(memory_space=pltpu.SMEM)


RIGHT = (1, 1, 1, -3)
LEFT = (-1, -1, -1, -1)
RIGHT2 = (1, 1, 1, 1)
LEFT2 = (-1, -1, 3, -1)
ACROSS = (4, -4, -4, -4)
RIGHT_AT = (5, 1, 1, 1)
LEFT_AT = (3, 3, 3, 3)
RIGHT2_AT = (0, 4, 0, 0)
LEFT2_AT = (4, 0, 4, 4)
ACROSS_AT = (1, 5, 5, 5)


def shifted(value, hops):
    pairs = [(source, (source + hops[source % 4]) % SHARDS) for source in range(SHARDS)]
    return lax.ppermute(value, DP, pairs)


def position_of(x, places):
    return jnp.where(x == 0, places[0], jnp.where(x == 1, places[1], jnp.where(x == 2, places[2], places[3])))


def dot(a, b):
    return jnp.dot(a, b, preferred_element_type=F32)


def dot_t(a, b):
    return lax.dot_general(a, b, (((1,), (1,)), ((), ())), preferred_element_type=F32)


def unit_rows(values):
    values = values.astype(F32)
    inverse = lax.rsqrt(jnp.sum(values * values, axis=-1, keepdims=True) + EPSILON)
    return values * inverse, inverse


def pair_grad(step_ref, col_ref, texts, block, position):
    images = unit_rows(block)[0].astype(BF16)
    steps = step_ref[pl.ds(position, 1), :]
    cols = col_ref[pl.ds(position, 1), :]
    logits = LOGIT_SCALE * dot_t(texts, images) + LOGIT_BIAS
    rows = lax.broadcasted_iota(jnp.int32, logits.shape, 0)
    positive = (steps == position) & (cols == rows)
    scale = LOSS_SCALE * LOGIT_SCALE
    chance = 1.0 / (1.0 + jnp.exp(jnp.where(positive, logits, -logits)))
    weights = (jnp.where(positive, -scale, scale) * chance).astype(BF16)
    return dot(weights, images)


def first_kernel(
    place_ref, feat_hbm, proj_hbm, image_hbm, step_hbm, col_hbm, unit_ref, inv_ref, text_ref, acc_ref, steps_ref, cols_ref,
    feat_ref, proj_ref, image_ref, step_ref, col_ref, sems,
):
    pairs = (
        (feat_hbm, feat_ref), (proj_hbm, proj_ref), (image_hbm, image_ref), (step_hbm, step_ref), (col_hbm, col_ref)
    )
    copies = [pltpu.make_async_copy(src, dst, sems.at[i]) for i, (src, dst) in enumerate(pairs)]
    for copy in copies:
        copy.start()
    copies[0].wait()
    copies[1].wait()
    hidden = dot(feat_ref[...], proj_ref[...])
    unit, inverse = unit_rows(hidden)
    texts = unit.astype(BF16)
    unit_ref[...] = unit
    inv_ref[...] = jnp.broadcast_to(inverse, inv_ref.shape)
    text_ref[...] = texts
    for copy in copies[2:]:
        copy.wait()
    for position in range(8):
        shard = (place_ref[0] + (position + (SHARDS - 2))) & (SHARDS - 1)
        spot = pl.ds(pl.multiple_of(shard * ROWS, ROWS), ROWS)
        steps_ref[position : position + 1, :] = step_ref[:, spot]
        cols_ref[position : position + 1, :] = col_ref[:, spot]
    acc_ref[...] = pair_grad(steps_ref, cols_ref, texts, image_ref[...], 2)


def near_kernel(place_ref, right_ref, left_ref, step_ref, col_ref, text_ref, acc_ref, out_ref):
    texts = text_ref[...]
    total = acc_ref[...] + pair_grad(step_ref, col_ref, texts, right_ref[...], place_ref[1])
    out_ref[...] = total + pair_grad(step_ref, col_ref, texts, left_ref[...], 3)


def order_kernel(feat_ref, other_ref, turned_ref, pick_ref):
    spot = lax.broadcasted_iota(jnp.int32, (D, 1), 0)
    within, peer = spot >> 7, spot & (SHARDS - 1)
    yh, x, z0, z = peer >> 6, (peer >> 4) & 3, (peer >> 3) & 1, peer & 7
    source = RB * (64 * yh + 8 * z + 4 * z0 + x) + within
    lanes = lax.broadcasted_iota(jnp.int32, (D, D), 1)
    order = jnp.where(lanes == source, 1.0, 0.0).astype(BF16)
    turned_ref[0] = dot_t(order, feat_ref[...]).astype(BF16)
    turned_ref[1] = dot_t(order, other_ref[...]).astype(BF16)
    lane = lax.broadcasted_iota(jnp.int32, (1, PICK), 1)
    column = jnp.where(lane < MAIN, lane, MAIN + (lane & (REST - 1)))
    rows = lax.broadcasted_iota(jnp.int32, (E, PICK), 0)
    for block in range(4):
        pick_ref[:, block * PICK : (block + 1) * PICK] = jnp.where(rows == column + CB * block, 1.0, 0.0).astype(BF16)


def far_kernel(at, place_ref, image_ref, step_ref, col_ref, text_ref, acc_ref, out_ref):
    part = pair_grad(step_ref, col_ref, text_ref[...], image_ref[...], place_ref[at])
    out_ref[...] = acc_ref[...] + part


def last_kernel(
    place_ref, left_ref, step_ref, col_ref, text_ref, acc_ref, unit_ref, inv_ref, pick_ref, grad_ref, out_ref
):
    part = pair_grad(step_ref, col_ref, text_ref[...], left_ref[...], place_ref[3])
    total = acc_ref[...] + part
    unit = unit_ref[...]
    radial = jnp.sum(unit * total, axis=-1, keepdims=True)
    grad = (inv_ref[:, :1] * (total - unit * radial)).astype(BF16)
    grad_ref[...] = grad
    for block in range(4):
        out_ref[block] = dot(grad, pick_ref[:, block * PICK : (block + 1) * PICK]).astype(BF16)


def partial_kernel(place_ref, came_ref, turned_ref, across_ref, out_ref):
    me = place_ref[5]
    parts = [came_ref[me ^ flip] for flip in range(4)]
    group = lax.broadcasted_iota(jnp.int32, (SHARDS, 128), 1) // REST
    rest = [jnp.zeros((SHARDS, 128), F32) for _ in range(3)]
    for r in range(RB):
        rows = slice(r * SHARDS, (r + 1) * SHARDS)
        block = dot(turned_ref[0, rows, :], parts[0]) + dot(across_ref[0, rows, :], parts[1])
        block = block + dot(turned_ref[1, rows, :], parts[2]) + dot(across_ref[1, rows, :], parts[3])
        out_ref[:, r * MAIN : (r + 1) * MAIN] = block[:, :MAIN].astype(BF16)
        rest[r // 4] = jnp.where(group == r % 4, block[:, MAIN:], rest[r // 4])
    for t in range(3):
        out_ref[:, SPLIT + t * 128 : SPLIT + (t + 1) * 128] = rest[t].astype(BF16)


def text_kernel(grad_ref, proj_ref, out_ref):
    out_ref[...] = dot_t(grad_ref[...], proj_ref[...]).astype(BF16)


def block_kernel(place_ref, came_ref, block_ref, square_ref):
    rows = jnp.sum(came_ref[...].astype(F32), axis=0)
    sums = jnp.sum(rows * rows, axis=0, keepdims=True)
    square = functools.reduce(jnp.add, [sums[:, t * 128 : (t + 1) * 128] for t in range(WIDTH // 128)])
    lines = lax.broadcasted_iota(jnp.int32, (8, 128), 0)
    square = jnp.where(lines == 0, jnp.broadcast_to(square, (8, 128)), 0.0)
    square_ref[...] = jnp.broadcast_to(square[None], square_ref.shape)
    mine = lax.broadcasted_iota(jnp.int32, rows.shape, 0) == place_ref[6]
    own = jnp.sum(jnp.where(mine, rows, 0.0), axis=0, keepdims=True)
    for r in range(RB):
        block_ref[r : r + 1, :MAIN] = own[:, r * MAIN : (r + 1) * MAIN]
        block_ref[r : r + 1, MAIN:] = own[:, SPLIT + r * REST : SPLIT + (r + 1) * REST]


def clip_kernel(square_ref, block_ref, out_ref):
    square = jnp.sum(jnp.sum(square_ref[...], axis=0), keepdims=True)
    factor = jnp.minimum(1.0, math.sqrt(D * E) * lax.rsqrt(square))
    out_ref[...] = block_ref[...] * factor


def call(kernel, inputs, outputs, flops, size, name, spaces=(), scratch=()):
    specs = [SMEM if value.ndim == 1 else VMEM for value in inputs]
    for i in spaces:
        specs[i] = pl.BlockSpec(memory_space=pl.ANY)
    return pl.pallas_call(
        kernel,
        out_shape=[jax.ShapeDtypeStruct(shape, dtype) for shape, dtype in outputs],
        in_specs=specs,
        out_specs=[VMEM] * len(outputs),
        scratch_shapes=list(scratch),
        compiler_params=pltpu.CompilerParams(vmem_limit_bytes=size << 20),
        cost_estimate=pl.CostEstimate(flops=flops, bytes_accessed=4 << 20, transcendentals=0),
        name=name,
    )(*inputs)


def traded(value, axis):
    return lax.all_to_all(value, axis, split_axis=0, concat_axis=0)


def total(value):
    return jnp.sum(value.astype(F32), axis=0)


def local(image_embeds, text_features, projection, pair_step, pair_col):
    x = lax.axis_index("x")
    places = (RIGHT_AT, RIGHT2_AT, LEFT2_AT, ACROSS_AT)
    place = [lax.axis_index(DP)] + [position_of(x, at) for at in places]
    place = jnp.stack(place + [lax.axis_index(OUTER), lax.axis_index(("zh", "z1"))]).astype(jnp.int32)
    image = image_embeds[0]
    features = text_features[0]
    right = shifted(image, RIGHT)
    left = shifted(image, LEFT)
    other = lax.ppermute(features, "yl", [(0, 1), (1, 0)])

    full = (ROWS, E)
    table = (8, ROWS)
    unit, inverse, texts, acc, steps, cols = call(
        first_kernel,
        (place, features, projection, image, pair_step, pair_col),
        ((full, F32), ((ROWS, 128), F32), (full, BF16), (full, F32), (table, jnp.int32), (table, jnp.int32)),
        1 << 30, 48, "hidden_and_own", range(1, 6),
        (
            pltpu.VMEM((ROWS, D), BF16), pltpu.VMEM((D, E), BF16), pltpu.VMEM(full, BF16),
            pltpu.VMEM(pair_step.shape, jnp.int32), pltpu.VMEM(pair_col.shape, jnp.int32), pltpu.SemaphoreType.DMA((5,)),
        ),
    )
    right, left, acc = lax.optimization_barrier((right, left, acc))
    right2 = shifted(right, RIGHT2)
    left2 = shifted(left, LEFT2)
    across = shifted(right, ACROSS)
    turned, pick = call(
        order_kernel, (features, other), (((2, D, ROWS), BF16), ((E, 4 * PICK), BF16)), 1 << 30, 32, "order"
    )
    opposite = lax.ppermute(turned, "c", [(0, 1), (1, 0)])
    (acc,) = call(near_kernel, (place, right, left, steps, cols, texts, acc), ((full, F32),), 1 << 30, 24, "near_pairs")
    for at, block, name in ((2, right2, "far_right"), (4, across, "far_across")):
        (acc,) = call(
            functools.partial(far_kernel, at), (place, block, steps, cols, texts, acc), ((full, F32),), 1 << 28, 24, name
        )
    grad, columns = call(
        last_kernel,
        (place, left2, steps, cols, texts, acc, unit, inverse, pick),
        ((full, BF16), ((4, ROWS, PICK), BF16)),
        1 << 30, 32, "far_left",
    )
    columns = traded(columns, OUTER)
    (both,) = call(
        partial_kernel, (place, columns, turned, opposite), (((SHARDS, WIDTH), BF16),), 1 << 30, 32, "partial"
    )
    rows = total(traded(both.reshape(16, 8, WIDTH), SIDE)).astype(BF16)
    near = lax.ppermute(rows, "z1", [(0, 1), (1, 0)])
    (grad_text,) = call(text_kernel, (grad, projection), ((full, BF16),), 1 << 30, 24, "grad_text")
    rows = (rows.astype(F32) + near.astype(F32)).astype(BF16)
    rows = traded(jnp.broadcast_to(rows[None], (4, 8, WIDTH)), "zh")
    block, square = call(block_kernel, (place, rows), (((RB, CB), F32), ((64, 8, 128), F32)), 1 << 20, 16, "block")
    square = traded(square, NEAR)
    (block,) = call(clip_kernel, (square, block), (((RB, CB), F32),), 1 << 20, 16, "clip")
    return (grad_text[None], block)


def solution(mesh):
    split = Mesh(mesh.devices.reshape(SHAPE), AXES)
    placed = (
        P(OUTER, DP, None),
        P(OUTER, DP, None),
        P(),
        P(OUTER, None),
        P(OUTER, None),
    )
    return jax.shard_map(
        local,
        mesh=split,
        in_specs=placed,
        out_specs=(P(OUTER, DP, None), P(DP, OUTER)),
        check_vma=False,
    )
```

time: 142 us -> 155 us (1.092)
  waiting for transfers between devices: 13.7 us -> 24.9 us
  blocking collectives: 61.9 us -> 51.1 us
  starting transfers between devices: 40.2 us -> 50.1 us
  Pallas kernels: 18.2 us -> 21.8 us
  local copies, waits for them, and re-layouts: 5.8 us -> 4.04 us
    all_to_all x3, blocking collectives: 61.9 us -> 51.1 us  [traded(): return lax.all_to_all(value, axis, split_axis=0, concat_axis=0)]
    all_to_all x0 -> x1, starting transfers between devices: none -> 9.93 us  [traded(): return lax.all_to_all(value, axis, split_axis=0, concat_axis=0)]
    all_to_all x0 -> x1, waiting for transfers between devices: none -> 7.94 us  [traded(): return lax.all_to_all(value, axis, split_axis=0, concat_axis=0)]
    pallas_call x8 -> x10, Pallas kernels: 18.2 us -> 21.8 us  [call(): pl.pallas_call(kernel, out_shape=[jax.ShapeDtypeStruct(shape, dtype) for...]
    ppermute x5, waiting for transfers between devices: 9.54 us -> 12.8 us  [shifted(): return lax.ppermute(value, DP, pairs)]
    ppermute x5, starting transfers between devices: 33.5 us -> 31.6 us  [shifted(): return lax.ppermute(value, DP, pairs)]
    ppermute x2 -> x3, starting transfers between devices: 6.76 us -> 8.56 us  [the longest x1 4.33 us: local(): opposite = lax.ppermute(turned, 'c', [(0, 1), (1, 0)])]
    unnamed x18 -> x10, local copies, waits for them, and re-layouts: 5.7 us -> 3.94 us
  transfers between devices with their start and end apart: 7 -> 9, of which waited for: 4 -> 5; matrix products, arithmetic and copies ran while one was open for 0% -> 0% of each run, Pallas kernels for 9% -> 11%
where the time goes in v5:
time: 155 us; the launch traced here: 154 us
  blocking collectives  51.1 us (33%)
  starting transfers between devices  50.1 us (32%)
  waiting for transfers between devices  24.9 us (16%)
  Pallas kernels  21.8 us (14%)
  local copies, waits for them, and re-layouts  4.04 us (3%)
    all_to_all x3, blocking collectives, traded(): return lax.all_to_all(value, axis, split_axis=0, concat_axis=0)  51.1 us
    ppermute x5, starting transfers between devices, shifted(): return lax.ppermute(value, DP, pairs)  31.6 us
    pallas_call x10, Pallas kernels, call(): pl.pallas_call(kernel, out_shape=[jax.ShapeDtypeStruct(shape, dtype) for...  21.8 us
    ppermute x5, waiting for transfers between devices, shifted(): return lax.ppermute(value, DP, pairs)  12.8 us
    all_to_all x1, starting transfers between devices, traded(): return lax.all_to_all(value, axis, split_axis=0, concat_axis=0)  9.93 us
    all_to_all x1, waiting for transfers between devices, traded(): return lax.all_to_all(value, axis, split_axis=0, concat_axis=0)  7.94 us
    ppermute x1, starting transfers between devices, local(): opposite = lax.ppermute(turned, 'c', [(0, 1), (1, 0)])  4.33 us
    ppermute x1, waiting for transfers between devices, local(): near = lax.ppermute(rows, 'z1', [(0, 1), (1, 0)])  4.2 us
  transfers between devices with their start and end apart: 9, of which 5 were waited for; matrix products, arithmetic and copies ran while one was open for 0% of the time, Pallas kernels for 11%

profile of v5, /device:TPU:1, one launch (start us, length us, event | category | flops | bytes accessed | tf_op | source)
XLA Modules:
  0.0 154.0 jit_solution(15709473699212586996)
XLA Ops:
  0.6 16.8 %collective-permute-start.1 = (bf16[256,1152]{1,0:T(8,128)(2,1)}, bf16[256,1152]{1,0:T(8,128)(2,1)S(1)}, u32[]{:S(2)}, u32[]{:S(2)}) collective-permute-start(bf16[256,1152]{1,0:T(8,128)(2,1)} %bitcast.12), channel_id=1, source_target_pairs={{0,508},{4,0},{8,4},{12,8},{16,12},{20,16},{24,20},{28,24},{32,28}... | collective-permute-start | bytes 1769480 | tf_op jit(solution)/shard_map/ppermute | solution.py:54
  17.4 1.9 %collective-permute-start = (bf16[256,1152]{1,0:T(8,128)(2,1)}, bf16[256,1152]{1,0:T(8,128)(2,1)S(1)}, u32[]{:S(2)}, u32[]{:S(2)}) collective-permute-start(bf16[256,1152]{1,0:T(8,128)(2,1)} %bitcast.13), channel_id=1, source_target_pairs={{0,4},{4,8},{8,12},{12,0},{16,20},{20,24},{24,28},{28,16},{32,36},... | collective-permute-start | bytes 1769480 | tf_op jit(solution)/shard_map/ppermute | solution.py:54
  19.3 2.3 %collective-permute-start.5 = (bf16[256,1152]{1,0:T(8,128)(2,1)}, bf16[256,1152]{1,0:T(8,128)(2,1)S(1)}, u32[]{:S(2)}, u32[]{:S(2)}) collective-permute-start(bf16[256,1152]{1,0:T(8,128)(2,1)} %bitcast.15), channel_id=1, source_target_pairs={{0,2},{2,0},{1,3},{3,1},{4,6},{6,4},{5,7},{7,5},{8,10},{10,8},{9,1... | collective-permute-start | bytes 1769480 | tf_op jit(solution)/shard_map/ppermute | solution.py:228
  25.7 4.8 %hidden_and_own.1 = (f32[256,1152]{1,0:T(8,128)S(1)}, f32[256,128]{1,0:T(8,128)S(1)}, bf16[256,1152]{1,0:T(8,128)(2,1)S(1)}, f32[256,1152]{1,0:T(8,128)S(1)}, s3...) custom-call(s32[7]{0:T(128)S(1)} %stack.31.place_ref, bf16[256,1152]{1,0:T(8,128)(2,1)S(1)} %bitcast.16, ...), custom_call_target="tpu_custom_call" | custom-call | flops 1073741824 | bytes 4194304 | tf_op jit(solution)/shard_map/hidden_and_own/pallas_call | solution.py:199
  30.5 4.1 %collective-permute-done.right_ref = bf16[256,1152]{1,0:T(8,128)(2,1)S(1)} collective-permute-done((bf16[256,1152]{1,0:T(8,128)(2,1)}, bf16[256,1152]{1,0:T(8,128)(2,1)S(1)}, u32[]{:S(2)}, u32[]{:S(2)}) %collective-permute-start) | collective-permute-done | bytes 589856 | tf_op jit(solution)/shard_map/ppermute | solution.py:54
  34.6 1.9 %collective-permute-start.4 = (bf16[256,1152]{1,0:T(8,128)(2,1)S(1)}, bf16[256,1152]{1,0:T(8,128)(2,1)S(1)}, u32[]{:S(2)}, u32[]{:S(2)}) collective-permute-start(bf16[256,1152]{1,0:T(8,128)(2,1)S(1)} %collective-permute-done.right_ref), channel_id=1, source_target_pairs={{0,4},{4,8},{8,12},{12,16},{16,20},{20,24},{24,28},{28,32},{32,36}... | collective-permute-start | bytes 1769480 | tf_op jit(solution)/shard_map/ppermute | solution.py:54
  36.5 1.9 %collective-permute-start.3 = (bf16[256,1152]{1,0:T(8,128)(2,1)S(1)}, bf16[256,1152]{1,0:T(8,128)(2,1)S(1)}, u32[]{:S(2)}, u32[]{:S(2)}) collective-permute-start(bf16[256,1152]{1,0:T(8,128)(2,1)S(1)} %collective-permute-done.right_ref), channel_id=1, source_target_pairs={{0,16},{4,500},{8,504},{12,508},{16,32},{20,4},{24,8},{28,12},{32,... | collective-permute-start | bytes 1769480 | tf_op jit(solution)/shard_map/ppermute | solution.py:54
  38.5 9.1 %collective-permute-start.2 = (bf16[256,1152]{1,0:T(8,128)(2,1)S(1)}, bf16[256,1152]{1,0:T(8,128)(2,1)S(1)}, u32[]{:S(2)}, u32[]{:S(2)}) collective-permute-start(bf16[256,1152]{1,0:T(8,128)(2,1)S(1)} %collective-permute-done.1.left_ref), channel_id=1, source_target_pairs={{0,508},{4,0},{8,20},{12,8},{16,12},{20,16},{24,36},{28,24},{32,28... | collective-permute-start | bytes 1769480 | tf_op jit(solution)/shard_map/ppermute | solution.py:54
  47.6 2.2 %order.1 = (bf16[2,1152,256]{2,1,0:T(8,128)(2,1)S(1)}, bf16[1152,1536]{1,0:T(8,128)(2,1)S(1)}) custom-call(bf16[256,1152]{1,0:T(8,128)(2,1)S(1)} %bitcast.17, bf16[256,1152]{1,0:T(8,128)(2,1)S(1)} %collective-permute-done.5.other_ref), custom_call_target="tpu_custom_call" | custom-call | flops 1073741824 | bytes 4194304 | tf_op jit(solution)/shard_map/order/pallas_call | solution.py:199
  49.7 4.3 %collective-permute-start.6 = (bf16[2,1152,256]{2,1,0:T(8,128)(2,1)S(1)}, bf16[2,1152,256]{2,1,0:T(8,128)(2,1)S(1)}, u32[]{:S(2)}, u32[]{:S(2)}) collective-permute-start(bf16[2,1152,256]{2,1,0:T(8,128)(2,1)S(1)} %get-tuple-element.29.turned_ref), channel_id=1, source_target_pairs={{0,1},{1,0},{2,3},{3,2},{4,5},{5,4},{6,7},{7,6},{8,9},{9,8},{10,11... | collective-permute-start | bytes 3538952 | tf_op jit(solution)/shard_map/ppermute | solution.py:249
  54.1 2.3 %near_pairs.1.acc_ref = f32[256,1152]{1,0:T(8,128)S(1)} custom-call(s32[7]{0:T(128)S(1)} %stack.31.place_ref, bf16[256,1152]{1,0:T(8,128)(2,1)S(1)} %collective-permute-done.right_ref, bf16[256,1152]{1,0:T(8,128)(2,1)S(1)} %collective-permute-done.1.left_ref, s32[8,256]{1,0:T(8,128)S(1)} %get-tuple-element.19.step_ref, ...), custom_call_target="tpu_custom_call" | custom-call | flops 1073741824 | bytes 4194304 | tf_op jit(solution)/shard_map/near_pairs/pallas_call | solution.py:199
  56.4 7.2 %collective-permute-done.4.image_ref = bf16[256,1152]{1,0:T(8,128)(2,1)S(1)} collective-permute-done((bf16[256,1152]{1,0:T(8,128)(2,1)S(1)}, bf16[256,1152]{1,0:T(8,128)(2,1)S(1)}, u32[]{:S(2)}, u32[]{:S(2)}) %collective-permute-start.4) | collective-permute-done | bytes 589856 | tf_op jit(solution)/shard_map/ppermute | solution.py:54
  63.5 1.6 %far_right.1.acc_ref = f32[256,1152]{1,0:T(8,128)S(1)} custom-call(s32[7]{0:T(128)S(1)} %stack.31.place_ref, bf16[256,1152]{1,0:T(8,128)(2,1)S(1)} %collective-permute-done.4.image_ref, s32[8,256]{1,0:T(8,128)S(1)} %get-tuple-element.19.step_ref, s32[8,256]{1,0:T(8,128)S(1)} %get-tuple-element.20.col_ref, bf16[256,1152]{1,0:T(8,128)(2,1)S(1)} %get-tuple-element.21.text_ref, ...), custom_call_target="tpu_custom_call" | custom-call | flops 268435456 | bytes 4194304 | tf_op jit(solution)/shard_map/far_right/pallas_call | solution.py:199
  66.7 1.6 %far_across.1.acc_ref = f32[256,1152]{1,0:T(8,128)S(1)} custom-call(s32[7]{0:T(128)S(1)} %stack.31.place_ref, bf16[256,1152]{1,0:T(8,128)(2,1)S(1)} %collective-permute-done.3.image_ref, s32[8,256]{1,0:T(8,128)S(1)} %get-tuple-element.19.step_ref, s32[8,256]{1,0:T(8,128)S(1)} %get-tuple-element.20.col_ref, bf16[256,1152]{1,0:T(8,128)(2,1)S(1)} %get-tuple-element.21.text_ref, ...), custom_call_target="tpu_custom_call" | custom-call | flops 268435456 | bytes 4194304 | tf_op jit(solution)/shard_map/far_across/pallas_call | solution.py:199
  68.3 3.4 %far_left.1 = (bf16[256,1152]{1,0:T(8,128)(2,1)S(1)}, bf16[4,256,384]{2,1,0:T(8,128)(2,1)S(1)}) custom-call(s32[7]{0:T(128)S(1)} %stack.31.place_ref, bf16[256,1152]{1,0:T(8,128)(2,1)S(1)} %collective-permute-done.2.left_ref, s32[8,256]{1,0:T(8,128)S(1)} %get-tuple-element.19.step_ref, s32[8,256]{1,0:T(8,128)S(1)} %get-tuple-element.20.col_ref, ...), custom_call_target="tpu_custom_call" | custom-call | flops 1073741824 | bytes 4194304 | tf_op jit(solution)/shard_map/far_left/pallas_call | solution.py:199
  71.7 16.8 %all_to_all.20.came_ref = bf16[4,256,384]{2,1,0:T(8,128)(2,1)S(1)} all-to-all(bf16[4,256,384]{2,1,0:T(8,128)(2,1)S(1)} %get-tuple-element.28), channel_id=1, replica_groups=mesh['yh'=2,'zh'=4,'z1'=2,'z0'=2,'x'=4,'yl'=2,'c'=2] {'yl','c'}, dimensions={0} | all-to-all | bytes 1572864 | tf_op jit(solution)/shard_map/all_to_all | solution.py:212
  88.5 1.9 %partial.1 = bf16[128,2688]{1,0:T(8,128)(2,1)S(1)} custom-call(s32[7]{0:T(128)S(1)} %stack.31.place_ref, bf16[4,256,384]{2,1,0:T(8,128)(2,1)S(1)} %all_to_all.20.came_ref, bf16[2,1152,256]{2,1,0:T(8,128)(2,1)S(1)} %get-tuple-element.29.turned_ref, bf16[2,1152,256]{2,1,0:T(8,128)(2,1)S(1)} %collective-permute-done.6.across_ref), custom_call_target="tpu_custom_call" | custom-call | flops 1073741824 | bytes 4194304 | tf_op jit(solution)/shard_map/partial/pallas_call | solution.py:199
  90.4 15.5 %all_to_all.21 = bf16[16,8,2688]{2,1,0:T(8,128)(2,1)} all-to-all(bf16[16,8,2688]{2,1,0:T(8,128)(2,1)S(1)} %bitcast.11), channel_id=1, replica_groups=mesh['yh'=2,'zh'=4,'z1'=2,'z0'=2,'x'=4,'yl'=2,'c'=2] {'yh','x','z0'}, dimensions={0} | all-to-all | bytes 1376256 | tf_op jit(solution)/shard_map/all_to_all | solution.py:212
  107.1 1.9 %collective-permute-start.7 = (bf16[8,2688]{1,0:T(8,128)(2,1)S(1)}, bf16[8,2688]{1,0:T(8,128)(2,1)S(1)}, u32[]{:S(2)}, u32[]{:S(2)}) collective-permute-start(bf16[8,2688]{1,0:T(8,128)(2,1)S(1)} %reduce_sum.12), channel_id=1, source_target_pairs={{0,32},{32,0},{1,33},{33,1},{2,34},{34,2},{3,35},{35,3},{4,36},{36... | collective-permute-start | bytes 129032 | tf_op jit(solution)/shard_map/ppermute | solution.py:266
  109.1 4.2 %collective-permute-done.7 = bf16[8,2688]{1,0:T(8,128)(2,1)S(1)} collective-permute-done((bf16[8,2688]{1,0:T(8,128)(2,1)S(1)}, bf16[8,2688]{1,0:T(8,128)(2,1)S(1)}, u32[]{:S(2)}, u32[]{:S(2)}) %collective-permute-start.7) | collective-permute-done | bytes 43040 | tf_op jit(solution)/shard_map/ppermute | solution.py:266
  113.3 18.8 %all_to_all.22.came_ref = bf16[4,8,2688]{2,1,0:T(8,128)(2,1)S(1)} all-to-all(bf16[4,8,2688]{2,1,0:T(8,128)(2,1)S(1)} %broadcast_in_dim.10), channel_id=1, replica_groups=mesh['yh'=2,'zh'=4,'z1'=2,'z0'=2,'x'=4,'yl'=2,'c'=2] {'zh'}, dimensions={0} | all-to-all | bytes 344064 | tf_op jit(solution)/shard_map/all_to_all | solution.py:212
  133.5 9.9 %all-to-all-start.3 = ((f32[64,8,128]{2,1,0:T(8,128)}), f32[64,8,128]{2,1,0:T(8,128)S(1)}, u32[]{:S(2)}, u32[]{:S(2)}) async-start(f32[64,8,128]{2,1,0:T(8,128)} %get-tuple-element.30), calls=%async_computation.3 | async-start | bytes 524288 | tf_op jit(solution)/shard_map/all_to_all | solution.py:212
  143.4 1.9 %grad_text.1 = bf16[256,1152]{1,0:T(8,128)(2,1)} custom-call(bf16[256,1152]{1,0:T(8,128)(2,1)S(1)} %get-tuple-element.27.grad_ref, bf16[1152,1152]{1,0:T(8,128)(2,1)S(1)} %copy-done), custom_call_target="tpu_custom_call" | custom-call | flops 1073741824 | bytes 4194304 | tf_op jit(solution)/shard_map/grad_text/pallas_call | solution.py:199
  145.3 7.9 %all-to-all-done.3.square_ref = f32[64,8,128]{2,1,0:T(8,128)S(1)} async-done(((f32[64,8,128]{2,1,0:T(8,128)}), f32[64,8,128]{2,1,0:T(8,128)S(1)}, u32[]{:S(2)}, u32[]{:S(2)}) %all-to-all-start.3) | async-done | bytes 262176 | tf_op jit(solution)/shard_map/all_to_all | solution.py:212
  (21 shorter events, 8.9 us)
Async XLA Ops:
  0.6 29.9 %collective-permute-start.1 = (bf16[256,1152]{1,0:T(8,128)(2,1)}, bf16[256,1152]{1,0:T(8,128)(2,1)S(1)}, u32[]{:S(2)}, u32[]{:S(2)}) collective-permute-start(bf16[256,1152]{1,0:T(8,128)(2,1)} %bitcast.12), channel_id=1, source_target_pairs={{0,508},{4,0},{8,4},{12,8},{16,12},{20,16},{24,20},{28,24},{32,28}... | collective-permute-start | bytes 1769480 | tf_op jit(solution)/shard_map/ppermute | solution.py:54
  17.4 17.2 %collective-permute-start = (bf16[256,1152]{1,0:T(8,128)(2,1)}, bf16[256,1152]{1,0:T(8,128)(2,1)S(1)}, u32[]{:S(2)}, u32[]{:S(2)}) collective-permute-start(bf16[256,1152]{1,0:T(8,128)(2,1)} %bitcast.13), channel_id=1, source_target_pairs={{0,4},{4,8},{8,12},{12,0},{16,20},{20,24},{24,28},{28,16},{32,36},... | collective-permute-start | bytes 1769480 | tf_op jit(solution)/shard_map/ppermute | solution.py:54
  19.3 28.2 %collective-permute-start.5 = (bf16[256,1152]{1,0:T(8,128)(2,1)}, bf16[256,1152]{1,0:T(8,128)(2,1)S(1)}, u32[]{:S(2)}, u32[]{:S(2)}) collective-permute-start(bf16[256,1152]{1,0:T(8,128)(2,1)} %bitcast.15), channel_id=1, source_target_pairs={{0,2},{2,0},{1,3},{3,1},{4,6},{6,4},{5,7},{7,5},{8,10},{10,8},{9,1... | collective-permute-start | bytes 1769480 | tf_op jit(solution)/shard_map/ppermute | solution.py:228
  21.8 1.1 copy-start.1
  22.8 1.1 copy-start.2
  23.9 0.9 copy-start.3
  24.8 0.9 copy-start.4
  34.6 28.9 %collective-permute-start.4 = (bf16[256,1152]{1,0:T(8,128)(2,1)S(1)}, bf16[256,1152]{1,0:T(8,128)(2,1)S(1)}, u32[]{:S(2)}, u32[]{:S(2)}) collective-permute-start(bf16[256,1152]{1,0:T(8,128)(2,1)S(1)} %collective-permute-done.right_ref), channel_id=1, source_target_pairs={{0,4},{4,8},{8,12},{12,16},{16,20},{20,24},{24,28},{28,32},{32,36}... | collective-permute-start | bytes 1769480 | tf_op jit(solution)/shard_map/ppermute | solution.py:54
  36.5 30.2 %collective-permute-start.3 = (bf16[256,1152]{1,0:T(8,128)(2,1)S(1)}, bf16[256,1152]{1,0:T(8,128)(2,1)S(1)}, u32[]{:S(2)}, u32[]{:S(2)}) collective-permute-start(bf16[256,1152]{1,0:T(8,128)(2,1)S(1)} %collective-permute-done.right_ref), channel_id=1, source_target_pairs={{0,16},{4,500},{8,504},{12,508},{16,32},{20,4},{24,8},{28,12},{32,... | collective-permute-start | bytes 1769480 | tf_op jit(solution)/shard_map/ppermute | solution.py:54
  38.5 29.9 %collective-permute-start.2 = (bf16[256,1152]{1,0:T(8,128)(2,1)S(1)}, bf16[256,1152]{1,0:T(8,128)(2,1)S(1)}, u32[]{:S(2)}, u32[]{:S(2)}) collective-permute-start(bf16[256,1152]{1,0:T(8,128)(2,1)S(1)} %collective-permute-done.1.left_ref), channel_id=1, source_target_pairs={{0,508},{4,0},{8,20},{12,8},{16,12},{20,16},{24,36},{28,24},{32,28... | collective-permute-start | bytes 1769480 | tf_op jit(solution)/shard_map/ppermute | solution.py:54
  49.7 38.7 %collective-permute-start.6 = (bf16[2,1152,256]{2,1,0:T(8,128)(2,1)S(1)}, bf16[2,1152,256]{2,1,0:T(8,128)(2,1)S(1)}, u32[]{:S(2)}, u32[]{:S(2)}) collective-permute-start(bf16[2,1152,256]{2,1,0:T(8,128)(2,1)S(1)} %get-tuple-element.29.turned_ref), channel_id=1, source_target_pairs={{0,1},{1,0},{2,3},{3,2},{4,5},{5,4},{6,7},{7,6},{8,9},{9,8},{10,11... | collective-permute-start | bytes 3538952 | tf_op jit(solution)/shard_map/ppermute | solution.py:249
  90.4 53.0 %copy-start = (bf16[1152,1152]{1,0:T(8,128)(2,1)S(1)}, bf16[1152,1152]{1,0:T(8,128)(2,1)}, u32[]{:S(2)}) copy-start(bf16[1152,1152]{1,0:T(8,128)(2,1)} %proj_ref.1) | copy-start | bytes 7962628
  107.1 6.1 %collective-permute-start.7 = (bf16[8,2688]{1,0:T(8,128)(2,1)S(1)}, bf16[8,2688]{1,0:T(8,128)(2,1)S(1)}, u32[]{:S(2)}, u32[]{:S(2)}) collective-permute-start(bf16[8,2688]{1,0:T(8,128)(2,1)S(1)} %reduce_sum.12), channel_id=1, source_target_pairs={{0,32},{32,0},{1,33},{33,1},{2,34},{34,2},{3,35},{35,3},{4,36},{36... | collective-permute-start | bytes 129032 | tf_op jit(solution)/shard_map/ppermute | solution.py:266
  133.5 19.8 %all-to-all-start.3 = ((f32[64,8,128]{2,1,0:T(8,128)}), f32[64,8,128]{2,1,0:T(8,128)S(1)}, u32[]{:S(2)}, u32[]{:S(2)}) async-start(f32[64,8,128]{2,1,0:T(8,128)} %get-tuple-element.30), calls=%async_computation.3 | async-start | bytes 524288 | tf_op jit(solution)/shard_map/all_to_all | solution.py:212

commit v6 on v5

--- a/solution.py
+++ b/solution.py
@@ -21,15 +21,14 @@
 AXES = ("yh", "zh", "z1", "z0", "x", "yl", "c")
 DP = ("yh", "zh", "z1", "z0", "x")
 OUTER = ("yl", "c")
-SIDE = ("yh", "x", "z0")
-NEAR = ("yh", "x", "z0", "yl", "c")
+NEAR = ("yh", "yl", "x", "z0")
 RB = 9
 CB = 288
 MAIN = 256
 REST = 32
 SPLIT = RB * MAIN
 WIDTH = 2688
-PICK = MAIN + 128
+PICK = 2 * MAIN + 2 * 128
 
 F32 = jnp.float32
 BF16 = jnp.bfloat16
@@ -119,20 +118,26 @@
     out_ref[...] = total + pair_grad(step_ref, col_ref, texts, left_ref[...], 3)
 
 
-def order_kernel(feat_ref, other_ref, turned_ref, pick_ref):
+def column_of(lane, core):
+    tail = lane - 2 * MAIN
+    pair = jnp.where(lane < 2 * MAIN, lane >> 8, tail >> 7)
+    inside = jnp.where(lane < 2 * MAIN, lane & (MAIN - 1), MAIN + (lane & (REST - 1)))
+    return CB * (2 * pair + core) + inside
+
+
+def order_kernel(place_ref, feat_ref, turned_ref, there_ref, here_ref):
     spot = lax.broadcasted_iota(jnp.int32, (D, 1), 0)
     within, peer = spot >> 7, spot & (SHARDS - 1)
     yh, x, z0, z = peer >> 6, (peer >> 4) & 3, (peer >> 3) & 1, peer & 7
     source = RB * (64 * yh + 8 * z + 4 * z0 + x) + within
     lanes = lax.broadcasted_iota(jnp.int32, (D, D), 1)
     order = jnp.where(lanes == source, 1.0, 0.0).astype(BF16)
-    turned_ref[0] = dot_t(order, feat_ref[...]).astype(BF16)
-    turned_ref[1] = dot_t(order, other_ref[...]).astype(BF16)
+    turned_ref[...] = dot_t(order, feat_ref[...]).astype(BF16)
+    core = place_ref[5]
     lane = lax.broadcasted_iota(jnp.int32, (1, PICK), 1)
-    column = jnp.where(lane < MAIN, lane, MAIN + (lane & (REST - 1)))
     rows = lax.broadcasted_iota(jnp.int32, (E, PICK), 0)
-    for block in range(4):
-        pick_ref[:, block * PICK : (block + 1) * PICK] = jnp.where(rows == column + CB * block, 1.0, 0.0).astype(BF16)
+    there_ref[...] = jnp.where(rows == column_of(lane, 1 - core), 1.0, 0.0).astype(BF16)
+    here_ref[...] = jnp.where(rows == column_of(lane, core), 1.0, 0.0).astype(BF16)
 
 
 def far_kernel(at, place_ref, image_ref, step_ref, col_ref, text_ref, acc_ref, out_ref):
@@ -149,23 +154,33 @@
     radial = jnp.sum(unit * total, axis=-1, keepdims=True)
     grad = (inv_ref[:, :1] * (total - unit * radial)).astype(BF16)
     grad_ref[...] = grad
-    for block in range(4):
-        out_ref[block] = dot(grad, pick_ref[:, block * PICK : (block + 1) * PICK]).astype(BF16)
-
-
-def partial_kernel(place_ref, came_ref, turned_ref, across_ref, out_ref):
-    me = place_ref[5]
-    parts = [came_ref[me ^ flip] for flip in range(4)]
+    out_ref[...] = dot(grad, pick_ref[...]).astype(BF16)
+
+
+def own_kernel(grad_ref, pick_ref, out_ref):
+    out_ref[...] = dot(grad_ref[...], pick_ref[...]).astype(BF16)
+
+
+def partial_kernel(own_ref, came_ref, turned_ref, opposite_ref, out_ref):
+    half = SHARDS // 2
     group = lax.broadcasted_iota(jnp.int32, (SHARDS, 128), 1) // REST
-    rest = [jnp.zeros((SHARDS, 128), F32) for _ in range(3)]
+    rest = [[jnp.zeros((SHARDS, 128), F32) for _ in range(3)] for _ in range(2)]
+
+    def put(pair, lanes, value):
+        value = value.astype(BF16)
+        for yh in range(2):
+            out_ref[yh, pair, :, lanes] = value[yh * half : (yh + 1) * half]
+
     for r in range(RB):
         rows = slice(r * SHARDS, (r + 1) * SHARDS)
-        block = dot(turned_ref[0, rows, :], parts[0]) + dot(across_ref[0, rows, :], parts[1])
-        block = block + dot(turned_ref[1, rows, :], parts[2]) + dot(across_ref[1, rows, :], parts[3])
-        out_ref[:, r * MAIN : (r + 1) * MAIN] = block[:, :MAIN].astype(BF16)
-        rest[r // 4] = jnp.where(group == r % 4, block[:, MAIN:], rest[r // 4])
-    for t in range(3):
-        out_ref[:, SPLIT + t * 128 : SPLIT + (t + 1) * 128] = rest[t].astype(BF16)
+        block = dot(turned_ref[rows, :], own_ref[...]) + dot(opposite_ref[rows, :], came_ref[...])
+        for pair in range(2):
+            put(pair, slice(r * MAIN, (r + 1) * MAIN), block[:, pair * MAIN : (pair + 1) * MAIN])
+            tail = block[:, 2 * MAIN + pair * 128 : 2 * MAIN + (pair + 1) * 128]
+            rest[pair][r // 4] = jnp.where(group == r % 4, tail, rest[pair][r // 4])
+    for pair in range(2):
+        for t in range(3):
+            put(pair, slice(SPLIT + t * 128, SPLIT + (t + 1) * 128), rest[pair][t])
 
 
 def text_kernel(grad_ref, proj_ref, out_ref):
@@ -220,12 +235,14 @@
     x = lax.axis_index("x")
     places = (RIGHT_AT, RIGHT2_AT, LEFT2_AT, ACROSS_AT)
     place = [lax.axis_index(DP)] + [position_of(x, at) for at in places]
-    place = jnp.stack(place + [lax.axis_index(OUTER), lax.axis_index(("zh", "z1"))]).astype(jnp.int32)
+    place = jnp.stack(place + [lax.axis_index("c"), lax.axis_index(("zh", "z1"))]).astype(jnp.int32)
     image = image_embeds[0]
     features = text_features[0]
     right = shifted(image, RIGHT)
     left = shifted(image, LEFT)
-    other = lax.ppermute(features, "yl", [(0, 1), (1, 0)])
+    right2 = shifted(right, RIGHT2)
+    left2 = shifted(left, LEFT2)
+    across = shifted(right, ACROSS)
 
     full = (ROWS, E)
     table = (8, ROWS)
@@ -239,14 +256,11 @@
             pltpu.VMEM(pair_step.shape, jnp.int32), pltpu.VMEM(pair_col.shape, jnp.int32), pltpu.SemaphoreType.DMA((5,)),
         ),
     )
-    right, left, acc = lax.optimization_barrier((right, left, acc))
-    right2 = shifted(right, RIGHT2)
-    left2 = shifted(left, LEFT2)
-    across = shifted(right, ACROSS)
-    turned, pick = call(
-        order_kernel, (features, other), (((2, D, ROWS), BF16), ((E, 4 * PICK), BF16)), 1 << 30, 32, "order"
-    )
-    opposite = lax.ppermute(turned, "c", [(0, 1), (1, 0)])
+    turned, pick_there, pick_here = call(
+        order_kernel, (place, features), (((D, ROWS), BF16), ((E, PICK), BF16), ((E, PICK), BF16)), 1 << 30, 32, "order"
+    )
+    swap = [(0, 1), (1, 0)]
+    opposite = lax.ppermute(turned, "c", swap)
     (acc,) = call(near_kernel, (place, right, left, steps, cols, texts, acc), ((full, F32),), 1 << 30, 24, "near_pairs")
     for at, block, name in ((2, right2, "far_right"), (4, across, "far_across")):
         (acc,) = call(
@@ -254,21 +268,22 @@
         )
     grad, columns = call(
         last_kernel,
-        (place, left2, steps, cols, texts, acc, unit, inverse, pick),
-        ((full, BF16), ((4, ROWS, PICK), BF16)),
+        (place, left2, steps, cols, texts, acc, unit, inverse, pick_there),
+        ((full, BF16), ((ROWS, PICK), BF16)),
         1 << 30, 32, "far_left",
     )
-    columns = traded(columns, OUTER)
+    columns = lax.ppermute(columns, "c", swap)
+    (own,) = call(own_kernel, (grad, pick_here), (((ROWS, PICK), BF16),), 1 << 28, 24, "own_columns")
     (both,) = call(
-        partial_kernel, (place, columns, turned, opposite), (((SHARDS, WIDTH), BF16),), 1 << 30, 32, "partial"
-    )
-    rows = total(traded(both.reshape(16, 8, WIDTH), SIDE)).astype(BF16)
-    near = lax.ppermute(rows, "z1", [(0, 1), (1, 0)])
+        partial_kernel, (own, columns, turned, opposite), (((2, 2, SHARDS // 2, WIDTH), BF16),), 1 << 30, 32, "partial"
+    )
+    rows = total(traded(both.reshape(32, 8, WIDTH), NEAR)).astype(BF16)
+    near = lax.ppermute(rows, "z1", swap)
     (grad_text,) = call(text_kernel, (grad, projection), ((full, BF16),), 1 << 30, 24, "grad_text")
     rows = (rows.astype(F32) + near.astype(F32)).astype(BF16)
     rows = traded(jnp.broadcast_to(rows[None], (4, 8, WIDTH)), "zh")
     block, square = call(block_kernel, (place, rows), (((RB, CB), F32), ((64, 8, 128), F32)), 1 << 20, 16, "block")
-    square = traded(square, NEAR)
+    square = traded(square, NEAR + ("c",))
     (block,) = call(clip_kernel, (square, block), (((RB, CB), F32),), 1 << 20, 16, "clip")
     return (grad_text[None], block)
 

time: 155 us -> 142 us (0.916)
  blocking collectives: 51.1 us -> 43 us
  waiting for transfers between devices: 24.9 us -> 20.2 us
  starting transfers between devices: 50.1 us -> 53.7 us
  local copies, waits for them, and re-layouts: 4.04 us -> 1.89 us
    all_to_all x3 -> x2, blocking collectives: 51.1 us -> 43 us  [traded(): return lax.all_to_all(value, axis, split_axis=0, concat_axis=0)]
    ppermute x5, waiting for transfers between devices: 12.8 us -> 7.26 us  [shifted(): return lax.ppermute(value, DP, pairs)]
    unnamed x10 -> x14, local copies, waits for them, and re-layouts: 3.94 us -> 1.79 us
    ppermute x3, starting transfers between devices: 8.56 us -> 10.6 us  [the longest x1 4.66 us: local(): columns = lax.ppermute(columns, 'c', swap)]
    ppermute x5, starting transfers between devices: 31.6 us -> 33.5 us  [shifted(): return lax.ppermute(value, DP, pairs)]
    pallas_call x10 -> x11, Pallas kernels: 21.8 us -> 20.4 us  [call(): pl.pallas_call(kernel, out_shape=[jax.ShapeDtypeStruct(shape, dtype) for...]
  transfers between devices with their start and end apart: 9 -> 9, of which waited for: 5 -> 5; matrix products, arithmetic and copies ran while one was open for 0% -> 0% of each run, Pallas kernels for 11% -> 13%
where the time goes in v6:
time: 142 us
  starting transfers between devices  53.7 us (38%)
  blocking collectives  43 us (30%)
  Pallas kernels  20.4 us (14%)
  waiting for transfers between devices  20.2 us (14%)
  local copies, waits for them, and re-layouts  1.89 us (1%)
  other arithmetic  1.7 us (1%)
    all_to_all x2, blocking collectives, traded(): return lax.all_to_all(value, axis, split_axis=0, concat_axis=0)  43 us
    ppermute x5, starting transfers between devices, shifted(): return lax.ppermute(value, DP, pairs)  33.5 us
    pallas_call x11, Pallas kernels, call(): pl.pallas_call(kernel, out_shape=[jax.ShapeDtypeStruct(shape, dtype) for...  20.4 us
    all_to_all x1, starting transfers between devices, traded(): return lax.all_to_all(value, axis, split_axis=0, concat_axis=0)  9.57 us
    all_to_all x1, waiting for transfers between devices, traded(): return lax.all_to_all(value, axis, split_axis=0, concat_axis=0)  8.13 us
    ppermute x5, waiting for transfers between devices, shifted(): return lax.ppermute(value, DP, pairs)  7.26 us
    ppermute x1, starting transfers between devices, local(): columns = lax.ppermute(columns, 'c', swap)  4.66 us
    ppermute x1, waiting for transfers between devices, local(): near = lax.ppermute(rows, 'z1', swap)  4.2 us
  transfers between devices with their start and end apart: 9, of which 5 were waited for; matrix products, arithmetic and copies ran while one was open for 0% of the time, Pallas kernels for 13%

profile of v6, /device:TPU:1, one launch (start us, length us, event | category | flops | bytes accessed | tf_op | source)
XLA Modules:
  0.0 141.8 jit_solution(10558210120405488460)
XLA Ops:
  0.6 4.0 %collective-permute-start.2 = (bf16[256,1152]{1,0:T(8,128)(2,1)}, bf16[256,1152]{1,0:T(8,128)(2,1)S(1)}, u32[]{:S(2)}, u32[]{:S(2)}) collective-permute-start(bf16[256,1152]{1,0:T(8,128)(2,1)} %bitcast.12), channel_id=1, source_target_pairs={{0,4},{4,8},{8,12},{12,0},{16,20},{20,24},{24,28},{28,16},{32,36},... | collective-permute-start | bytes 1769480 | tf_op jit(solution)/shard_map/ppermute | solution.py:53
  4.6 14.9 %collective-permute-start = (bf16[256,1152]{1,0:T(8,128)(2,1)}, bf16[256,1152]{1,0:T(8,128)(2,1)S(1)}, u32[]{:S(2)}, u32[]{:S(2)}) collective-permute-start(bf16[256,1152]{1,0:T(8,128)(2,1)} %bitcast.13), channel_id=1, source_target_pairs={{0,508},{4,0},{8,4},{12,8},{16,12},{20,16},{24,20},{28,24},{32,28}... | collective-permute-start | bytes 1769480 | tf_op jit(solution)/shard_map/ppermute | solution.py:53
  19.5 1.9 %collective-permute-start.4 = (bf16[256,1152]{1,0:T(8,128)(2,1)S(1)}, bf16[256,1152]{1,0:T(8,128)(2,1)S(1)}, u32[]{:S(2)}, u32[]{:S(2)}) collective-permute-start(bf16[256,1152]{1,0:T(8,128)(2,1)S(1)} %collective-permute-done.2.right_ref), channel_id=1, source_target_pairs={{0,4},{4,8},{8,12},{12,16},{16,20},{20,24},{24,28},{28,32},{32,36}... | collective-permute-start | bytes 1769480 | tf_op jit(solution)/shard_map/ppermute | solution.py:53
  21.5 3.0 %collective-permute-start.3 = (bf16[256,1152]{1,0:T(8,128)(2,1)S(1)}, bf16[256,1152]{1,0:T(8,128)(2,1)S(1)}, u32[]{:S(2)}, u32[]{:S(2)}) collective-permute-start(bf16[256,1152]{1,0:T(8,128)(2,1)S(1)} %collective-permute-done.2.right_ref), channel_id=1, source_target_pairs={{0,16},{4,500},{8,504},{12,508},{16,32},{20,4},{24,8},{28,12},{32,... | collective-permute-start | bytes 1769480 | tf_op jit(solution)/shard_map/ppermute | solution.py:53
  24.4 7.1 %collective-permute-done.left_ref = bf16[256,1152]{1,0:T(8,128)(2,1)S(1)} collective-permute-done((bf16[256,1152]{1,0:T(8,128)(2,1)}, bf16[256,1152]{1,0:T(8,128)(2,1)S(1)}, u32[]{:S(2)}, u32[]{:S(2)}) %collective-permute-start) | collective-permute-done | bytes 589856 | tf_op jit(solution)/shard_map/ppermute | solution.py:53
  31.5 9.7 %collective-permute-start.1 = (bf16[256,1152]{1,0:T(8,128)(2,1)S(1)}, bf16[256,1152]{1,0:T(8,128)(2,1)S(1)}, u32[]{:S(2)}, u32[]{:S(2)}) collective-permute-start(bf16[256,1152]{1,0:T(8,128)(2,1)S(1)} %collective-permute-done.left_ref), channel_id=1, source_target_pairs={{0,508},{4,0},{8,20},{12,8},{16,12},{20,16},{24,36},{28,24},{32,28... | collective-permute-start | bytes 1769480 | tf_op jit(solution)/shard_map/ppermute | solution.py:53
  41.3 1.1 copy-done.2
  42.4 2.4 %order.1 = (bf16[1152,256]{1,0:T(8,128)(2,1)S(1)}, bf16[1152,768]{1,0:T(8,128)(2,1)S(1)}, bf16[1152,768]{1,0:T(8,128)(2,1)S(1)}) custom-call(s32[7]{0:T(128)S(1)} %stack.31.place_ref, bf16[256,1152]{1,0:T(8,128)(2,1)S(1)} %bitcast.15), custom_call_target="tpu_custom_call" | custom-call | flops 1073741824 | bytes 4194304 | tf_op jit(solution)/shard_map/order/pallas_call | solution.py:214
  44.8 4.1 %collective-permute-start.6 = (bf16[1152,256]{1,0:T(8,128)(2,1)S(1)}, bf16[1152,256]{1,0:T(8,128)(2,1)S(1)}, u32[]{:S(2)}, u32[]{:S(2)}) collective-permute-start(bf16[1152,256]{1,0:T(8,128)(2,1)S(1)} %get-tuple-element.25.turned_ref), channel_id=1, source_target_pairs={{0,1},{1,0},{2,3},{3,2},{4,5},{5,4},{6,7},{7,6},{8,9},{9,8},{10,11... | collective-permute-start | bytes 1769480 | tf_op jit(solution)/shard_map/ppermute | solution.py:263
  48.9 4.8 %hidden_and_own.1 = (f32[256,1152]{1,0:T(8,128)S(1)}, f32[256,128]{1,0:T(8,128)S(1)}, bf16[256,1152]{1,0:T(8,128)(2,1)S(1)}, f32[256,1152]{1,0:T(8,128)S(1)}, s3...) custom-call(s32[7]{0:T(128)S(1)} %stack.31.place_ref, bf16[256,1152]{1,0:T(8,128)(2,1)S(1)} %bitcast.16, ...), custom_call_target="tpu_custom_call" | custom-call | flops 1073741824 | bytes 4194304 | tf_op jit(solution)/shard_map/hidden_and_own/pallas_call | solution.py:214
  53.7 2.3 %near_pairs.1.acc_ref = f32[256,1152]{1,0:T(8,128)S(1)} custom-call(s32[7]{0:T(128)S(1)} %stack.31.place_ref, bf16[256,1152]{1,0:T(8,128)(2,1)S(1)} %collective-permute-done.2.right_ref, bf16[256,1152]{1,0:T(8,128)(2,1)S(1)} %collective-permute-done.left_ref, s32[8,256]{1,0:T(8,128)S(1)} %get-tuple-element.15.step_ref, ...), custom_call_target="tpu_custom_call" | custom-call | flops 1073741824 | bytes 4194304 | tf_op jit(solution)/shard_map/near_pairs/pallas_call | solution.py:214
  56.0 1.6 %far_right.1.acc_ref = f32[256,1152]{1,0:T(8,128)S(1)} custom-call(s32[7]{0:T(128)S(1)} %stack.31.place_ref, bf16[256,1152]{1,0:T(8,128)(2,1)S(1)} %collective-permute-done.4.image_ref, s32[8,256]{1,0:T(8,128)S(1)} %get-tuple-element.15.step_ref, s32[8,256]{1,0:T(8,128)S(1)} %get-tuple-element.16.col_ref, bf16[256,1152]{1,0:T(8,128)(2,1)S(1)} %get-tuple-element.17.text_ref, ...), custom_call_target="tpu_custom_call" | custom-call | flops 268435456 | bytes 4194304 | tf_op jit(solution)/shard_map/far_right/pallas_call | solution.py:214
  57.9 1.6 %far_across.1.acc_ref = f32[256,1152]{1,0:T(8,128)S(1)} custom-call(s32[7]{0:T(128)S(1)} %stack.31.place_ref, bf16[256,1152]{1,0:T(8,128)(2,1)S(1)} %collective-permute-done.3.image_ref, s32[8,256]{1,0:T(8,128)S(1)} %get-tuple-element.15.step_ref, s32[8,256]{1,0:T(8,128)S(1)} %get-tuple-element.16.col_ref, bf16[256,1152]{1,0:T(8,128)(2,1)S(1)} %get-tuple-element.17.text_ref, ...), custom_call_target="tpu_custom_call" | custom-call | flops 268435456 | bytes 4194304 | tf_op jit(solution)/shard_map/far_across/pallas_call | solution.py:214
  59.5 2.6 %far_left.1 = (bf16[256,1152]{1,0:T(8,128)(2,1)S(1)}, bf16[256,768]{1,0:T(8,128)(2,1)S(1)}) custom-call(s32[7]{0:T(128)S(1)} %stack.31.place_ref, bf16[256,1152]{1,0:T(8,128)(2,1)S(1)} %collective-permute-done.1.left_ref, s32[8,256]{1,0:T(8,128)S(1)} %get-tuple-element.15.step_ref, s32[8,256]{1,0:T(8,128)S(1)} %get-tuple-element.16.col_ref, ...), custom_call_target="tpu_custom_call" | custom-call | flops 1073741824 | bytes 4194304 | tf_op jit(solution)/shard_map/far_left/pallas_call | solution.py:214
  62.1 4.7 %collective-permute-start.5 = (bf16[256,768]{1,0:T(8,128)(2,1)S(1)}, bf16[256,768]{1,0:T(8,128)(2,1)S(1)}, u32[]{:S(2)}, u32[]{:S(2)}) collective-permute-start(bf16[256,768]{1,0:T(8,128)(2,1)S(1)} %get-tuple-element.24), channel_id=1, source_target_pairs={{0,1},{1,0},{2,3},{3,2},{4,5},{5,4},{6,7},{7,6},{8,9},{9,8},{10,11... | collective-permute-start | bytes 1179656 | tf_op jit(solution)/shard_map/ppermute | solution.py:275
  68.1 1.1 partial.1
  69.2 24.5 %all_to_all.15 = bf16[32,8,2688]{2,1,0:T(8,128)(2,1)} all-to-all(bf16[32,8,2688]{2,1,0:T(8,128)(2,1)S(1)} %bitcast.11), channel_id=1, replica_groups=mesh['yh'=2,'zh'=4,'z1'=2,'z0'=2,'x'=4,'yl'=2,'c'=2] {'yh','yl','x','z0'}, dimensions={0} | all-to-all | bytes 2752512 | tf_op jit(solution)/shard_map/all_to_all | solution.py:227
  93.7 1.7 %reduce_sum.12 = bf16[8,2688]{1,0:T(8,128)(2,1)S(1)} reduce(bf16[32,8,2688]{2,1,0:T(8,128)(2,1)} %all_to_all.15, bf16[]{:T(256)} %constant.43.clone.1), dimensions={0}, to_apply=%region_0.1 | reduce | flops 666624 | bytes 1419266 | tf_op jit(solution)/shard_map/reduce_sum | solution.py:231
  95.4 1.9 %collective-permute-start.7 = (bf16[8,2688]{1,0:T(8,128)(2,1)S(1)}, bf16[8,2688]{1,0:T(8,128)(2,1)S(1)}, u32[]{:S(2)}, u32[]{:S(2)}) collective-permute-start(bf16[8,2688]{1,0:T(8,128)(2,1)S(1)} %reduce_sum.12), channel_id=1, source_target_pairs={{0,32},{32,0},{1,33},{33,1},{2,34},{34,2},{3,35},{35,3},{4,36},{36... | collective-permute-start | bytes 129032 | tf_op jit(solution)/shard_map/ppermute | solution.py:281
  97.3 4.2 %collective-permute-done.7 = bf16[8,2688]{1,0:T(8,128)(2,1)S(1)} collective-permute-done((bf16[8,2688]{1,0:T(8,128)(2,1)S(1)}, bf16[8,2688]{1,0:T(8,128)(2,1)S(1)}, u32[]{:S(2)}, u32[]{:S(2)}) %collective-permute-start.7) | collective-permute-done | bytes 43040 | tf_op jit(solution)/shard_map/ppermute | solution.py:281
  101.6 18.5 %all_to_all.16.came_ref = bf16[4,8,2688]{2,1,0:T(8,128)(2,1)S(1)} all-to-all(bf16[4,8,2688]{2,1,0:T(8,128)(2,1)S(1)} %broadcast_in_dim.10), channel_id=1, replica_groups=mesh['yh'=2,'zh'=4,'z1'=2,'z0'=2,'x'=4,'yl'=2,'c'=2] {'zh'}, dimensions={0} | all-to-all | bytes 344064 | tf_op jit(solution)/shard_map/all_to_all | solution.py:227
  121.5 9.6 %all-to-all-start.2 = ((f32[64,8,128]{2,1,0:T(8,128)}), f32[64,8,128]{2,1,0:T(8,128)S(1)}, u32[]{:S(2)}, u32[]{:S(2)}) async-start(f32[64,8,128]{2,1,0:T(8,128)} %copy-done.4), calls=%async_computation.2 | async-start | bytes 524288 | tf_op jit(solution)/shard_map/all_to_all | solution.py:227
  131.0 1.8 %grad_text.1 = bf16[256,1152]{1,0:T(8,128)(2,1)} custom-call(bf16[256,1152]{1,0:T(8,128)(2,1)S(1)} %get-tuple-element.22.grad_ref, bf16[1152,1152]{1,0:T(8,128)(2,1)S(1)} %copy-done), custom_call_target="tpu_custom_call" | custom-call | flops 1073741824 | bytes 4194304 | tf_op jit(solution)/shard_map/grad_text/pallas_call | solution.py:214
  132.9 8.1 %all-to-all-done.2.square_ref = f32[64,8,128]{2,1,0:T(8,128)S(1)} async-done(((f32[64,8,128]{2,1,0:T(8,128)}), f32[64,8,128]{2,1,0:T(8,128)S(1)}, u32[]{:S(2)}, u32[]{:S(2)}) %all-to-all-start.2) | async-done | bytes 262176 | tf_op jit(solution)/shard_map/all_to_all | solution.py:227
  (25 shorter events, 3.8 us)
Async XLA Ops:
  0.6 18.9 %collective-permute-start.2 = (bf16[256,1152]{1,0:T(8,128)(2,1)}, bf16[256,1152]{1,0:T(8,128)(2,1)S(1)}, u32[]{:S(2)}, u32[]{:S(2)}) collective-permute-start(bf16[256,1152]{1,0:T(8,128)(2,1)} %bitcast.12), channel_id=1, source_target_pairs={{0,4},{4,8},{8,12},{12,0},{16,20},{20,24},{24,28},{28,16},{32,36},... | collective-permute-start | bytes 1769480 | tf_op jit(solution)/shard_map/ppermute | solution.py:53
  4.6 26.9 %collective-permute-start = (bf16[256,1152]{1,0:T(8,128)(2,1)}, bf16[256,1152]{1,0:T(8,128)(2,1)S(1)}, u32[]{:S(2)}, u32[]{:S(2)}) collective-permute-start(bf16[256,1152]{1,0:T(8,128)(2,1)} %bitcast.13), channel_id=1, source_target_pairs={{0,508},{4,0},{8,4},{12,8},{16,12},{20,16},{24,20},{28,24},{32,28}... | collective-permute-start | bytes 1769480 | tf_op jit(solution)/shard_map/ppermute | solution.py:53
  19.5 36.5 %collective-permute-start.4 = (bf16[256,1152]{1,0:T(8,128)(2,1)S(1)}, bf16[256,1152]{1,0:T(8,128)(2,1)S(1)}, u32[]{:S(2)}, u32[]{:S(2)}) collective-permute-start(bf16[256,1152]{1,0:T(8,128)(2,1)S(1)} %collective-permute-done.2.right_ref), channel_id=1, source_target_pairs={{0,4},{4,8},{8,12},{12,16},{16,20},{20,24},{24,28},{28,32},{32,36}... | collective-permute-start | bytes 1769480 | tf_op jit(solution)/shard_map/ppermute | solution.py:53
  21.5 36.4 %collective-permute-start.3 = (bf16[256,1152]{1,0:T(8,128)(2,1)S(1)}, bf16[256,1152]{1,0:T(8,128)(2,1)S(1)}, u32[]{:S(2)}, u32[]{:S(2)}) collective-permute-start(bf16[256,1152]{1,0:T(8,128)(2,1)S(1)} %collective-permute-done.2.right_ref), channel_id=1, source_target_pairs={{0,16},{4,500},{8,504},{12,508},{16,32},{20,4},{24,8},{28,12},{32,... | collective-permute-start | bytes 1769480 | tf_op jit(solution)/shard_map/ppermute | solution.py:53
  31.5 28.0 %collective-permute-start.1 = (bf16[256,1152]{1,0:T(8,128)(2,1)S(1)}, bf16[256,1152]{1,0:T(8,128)(2,1)S(1)}, u32[]{:S(2)}, u32[]{:S(2)}) collective-permute-start(bf16[256,1152]{1,0:T(8,128)(2,1)S(1)} %collective-permute-done.left_ref), channel_id=1, source_target_pairs={{0,508},{4,0},{8,20},{12,8},{16,12},{20,16},{24,36},{28,24},{32,28... | collective-permute-start | bytes 1769480 | tf_op jit(solution)/shard_map/ppermute | solution.py:53
  41.3 1.1 copy-start.2
  42.4 6.5 %copy-start.1 = (bf16[1,256,1152]{2,1,0:T(8,128)(2,1)S(1)}, bf16[1,256,1152]{2,1,0:T(8,128)(2,1)}, u32[]{:S(2)}) copy-start(bf16[1,256,1152]{2,1,0:T(8,128)(2,1)} %param.5) | copy-start | bytes 1769476
  42.4 6.5 %copy-start.3 = (bf16[1,256,1152]{2,1,0:T(8,128)(2,1)S(1)}, bf16[1,256,1152]{2,1,0:T(8,128)(2,1)}, u32[]{:S(2)}) copy-start(bf16[1,256,1152]{2,1,0:T(8,128)(2,1)} %param.6) | copy-start | bytes 1769476
  42.4 6.5 %copy-start.5 = (s32[1,32768]{1,0:T(1,128)S(1)}, s32[1,32768]{1,0:T(1,128)}, u32[]{:S(2)}) copy-start(s32[1,32768]{1,0:T(1,128)} %step_hbm.1) | copy-start | bytes 393220
  42.4 6.5 %copy-start.6 = (s32[1,32768]{1,0:T(1,128)S(1)}, s32[1,32768]{1,0:T(1,128)}, u32[]{:S(2)}) copy-start(s32[1,32768]{1,0:T(1,128)} %col_hbm.1) | copy-start | bytes 393220
  44.8 22.6 %collective-permute-start.6 = (bf16[1152,256]{1,0:T(8,128)(2,1)S(1)}, bf16[1152,256]{1,0:T(8,128)(2,1)S(1)}, u32[]{:S(2)}, u32[]{:S(2)}) collective-permute-start(bf16[1152,256]{1,0:T(8,128)(2,1)S(1)} %get-tuple-element.25.turned_ref), channel_id=1, source_target_pairs={{0,1},{1,0},{2,3},{3,2},{4,5},{5,4},{6,7},{7,6},{8,9},{9,8},{10,11... | collective-permute-start | bytes 1769480 | tf_op jit(solution)/shard_map/ppermute | solution.py:263
  62.1 6.0 %collective-permute-start.5 = (bf16[256,768]{1,0:T(8,128)(2,1)S(1)}, bf16[256,768]{1,0:T(8,128)(2,1)S(1)}, u32[]{:S(2)}, u32[]{:S(2)}) collective-permute-start(bf16[256,768]{1,0:T(8,128)(2,1)S(1)} %get-tuple-element.24), channel_id=1, source_target_pairs={{0,1},{1,0},{2,3},{3,2},{4,5},{5,4},{6,7},{7,6},{8,9},{9,8},{10,11... | collective-permute-start | bytes 1179656 | tf_op jit(solution)/shard_map/ppermute | solution.py:275
  93.7 37.3 %copy-start = (bf16[1152,1152]{1,0:T(8,128)(2,1)S(1)}, bf16[1152,1152]{1,0:T(8,128)(2,1)}, u32[]{:S(2)}) copy-start(bf16[1152,1152]{1,0:T(8,128)(2,1)} %proj_ref.1) | copy-start | bytes 7962628
  95.4 6.1 %collective-permute-start.7 = (bf16[8,2688]{1,0:T(8,128)(2,1)S(1)}, bf16[8,2688]{1,0:T(8,128)(2,1)S(1)}, u32[]{:S(2)}, u32[]{:S(2)}) collective-permute-start(bf16[8,2688]{1,0:T(8,128)(2,1)S(1)} %reduce_sum.12), channel_id=1, source_target_pairs={{0,32},{32,0},{1,33},{33,1},{2,34},{34,2},{3,35},{35,3},{4,36},{36... | collective-permute-start | bytes 129032 | tf_op jit(solution)/shard_map/ppermute | solution.py:281
  120.7 0.7 copy-start.4
  121.5 19.6 %all-to-all-start.2 = ((f32[64,8,128]{2,1,0:T(8,128)}), f32[64,8,128]{2,1,0:T(8,128)S(1)}, u32[]{:S(2)}, u32[]{:S(2)}) async-start(f32[64,8,128]{2,1,0:T(8,128)} %copy-done.4), calls=%async_computation.2 | async-start | bytes 524288 | tf_op jit(solution)/shard_map/all_to_all | solution.py:227

commit v7 on v6

--- a/solution.py
+++ b/solution.py
@@ -157,8 +157,9 @@
     out_ref[...] = dot(grad, pick_ref[...]).astype(BF16)
 
 
-def own_kernel(grad_ref, pick_ref, out_ref):
+def own_kernel(grad_ref, pick_ref, proj_ref, out_ref, text_ref):
     out_ref[...] = dot(grad_ref[...], pick_ref[...]).astype(BF16)
+    text_ref[...] = dot_t(grad_ref[...], proj_ref[...]).astype(BF16)
 
 
 def partial_kernel(own_ref, came_ref, turned_ref, opposite_ref, out_ref):
@@ -181,10 +182,6 @@
     for pair in range(2):
         for t in range(3):
             put(pair, slice(SPLIT + t * 128, SPLIT + (t + 1) * 128), rest[pair][t])
-
-
-def text_kernel(grad_ref, proj_ref, out_ref):
-    out_ref[...] = dot_t(grad_ref[...], proj_ref[...]).astype(BF16)
 
 
 def block_kernel(place_ref, came_ref, block_ref, square_ref):
@@ -273,13 +270,14 @@
         1 << 30, 32, "far_left",
     )
     columns = lax.ppermute(columns, "c", swap)
-    (own,) = call(own_kernel, (grad, pick_here), (((ROWS, PICK), BF16),), 1 << 28, 24, "own_columns")
+    own, grad_text = call(
+        own_kernel, (grad, pick_here, projection), (((ROWS, PICK), BF16), (full, BF16)), 1 << 28, 24, "own_columns"
+    )
     (both,) = call(
         partial_kernel, (own, columns, turned, opposite), (((2, 2, SHARDS // 2, WIDTH), BF16),), 1 << 30, 32, "partial"
     )
     rows = total(traded(both.reshape(32, 8, WIDTH), NEAR)).astype(BF16)
     near = lax.ppermute(rows, "z1", swap)
-    (grad_text,) = call(text_kernel, (grad, projection), ((full, BF16),), 1 << 30, 24, "grad_text")
     rows = (rows.astype(F32) + near.astype(F32)).astype(BF16)
     rows = traded(jnp.broadcast_to(rows[None], (4, 8, WIDTH)), "zh")
     block, square = call(block_kernel, (place, rows), (((RB, CB), F32), ((64, 8, 128), F32)), 1 << 20, 16, "block")

time: 142 us -> 141 us (level)
  blocking collectives: 43 us -> 62.4 us
  starting transfers between devices: 53.7 us -> 44.1 us
  waiting for transfers between devices: 20.2 us -> 11 us
  other arithmetic: 1.7 us -> 0.21 us
    all_to_all x2 -> x3, blocking collectives: 43 us -> 62.4 us  [traded(): return lax.all_to_all(value, axis, split_axis=0, concat_axis=0)]
    all_to_all x1 -> x0, starting transfers between devices: 9.57 us -> none  [traded(): return lax.all_to_all(value, axis, split_axis=0, concat_axis=0)]
    all_to_all x1 -> x0, waiting for transfers between devices: 8.13 us -> none  [traded(): return lax.all_to_all(value, axis, split_axis=0, concat_axis=0)]
    reduce_sum x1, other arithmetic: 1.69 us -> 0.2 us  [total(): return jnp.sum(value.astype(F32), axis=0)]
    pallas_call x11 -> x10, Pallas kernels: 20.4 us -> 20.2 us  [call(): pl.pallas_call(kernel, out_shape=[jax.ShapeDtypeStruct(shape, dtype) for...]
  transfers between devices with their start and end apart: 9 -> 8, of which waited for: 5 -> 3; matrix products, arithmetic and copies ran while one was open for 0% -> 0% of each run, Pallas kernels for 13% -> 13%
where the time goes in v7:
time: 141 us; the launch traced here: 140 us
  blocking collectives  62.4 us (44%)
  starting transfers between devices  44.1 us (31%)
  Pallas kernels  20.2 us (14%)
  waiting for transfers between devices  11 us (8%)
    all_to_all x3, blocking collectives, traded(): return lax.all_to_all(value, axis, split_axis=0, concat_axis=0)  62.4 us
    ppermute x5, starting transfers between devices, shifted(): return lax.ppermute(value, DP, pairs)  33.5 us
    pallas_call x10, Pallas kernels, call(): pl.pallas_call(kernel, out_shape=[jax.ShapeDtypeStruct(shape, dtype) for...  20.2 us
    ppermute x5, waiting for transfers between devices, shifted(): return lax.ppermute(value, DP, pairs)  7.26 us
    ppermute x1, starting transfers between devices, local(): columns = lax.ppermute(columns, 'c', swap)  4.66 us
    ppermute x1, starting transfers between devices, local(): opposite = lax.ppermute(turned, 'c', swap)  4.05 us
    ppermute x1, waiting for transfers between devices, local(): near = lax.ppermute(rows, 'z1', swap)  3.75 us
  transfers between devices with their start and end apart: 8, of which 3 were waited for; matrix products, arithmetic and copies ran while one was open for 0% of the time, Pallas kernels for 13%

profile of v7, /device:TPU:1, one launch (start us, length us, event | category | flops | bytes accessed | tf_op | source)
XLA Modules:
  0.0 140.0 jit_solution(2010792961837860603)
XLA Ops:
  0.6 4.0 %collective-permute-start.2 = (bf16[256,1152]{1,0:T(8,128)(2,1)}, bf16[256,1152]{1,0:T(8,128)(2,1)S(1)}, u32[]{:S(2)}, u32[]{:S(2)}) collective-permute-start(bf16[256,1152]{1,0:T(8,128)(2,1)} %bitcast.12), channel_id=1, source_target_pairs={{0,4},{4,8},{8,12},{12,0},{16,20},{20,24},{24,28},{28,16},{32,36},... | collective-permute-start | bytes 1769480 | tf_op jit(solution)/shard_map/ppermute | solution.py:53
  4.6 14.9 %collective-permute-start = (bf16[256,1152]{1,0:T(8,128)(2,1)}, bf16[256,1152]{1,0:T(8,128)(2,1)S(1)}, u32[]{:S(2)}, u32[]{:S(2)}) collective-permute-start(bf16[256,1152]{1,0:T(8,128)(2,1)} %bitcast.13), channel_id=1, source_target_pairs={{0,508},{4,0},{8,4},{12,8},{16,12},{20,16},{24,20},{28,24},{32,28}... | collective-permute-start | bytes 1769480 | tf_op jit(solution)/shard_map/ppermute | solution.py:53
  19.5 1.9 %collective-permute-start.4 = (bf16[256,1152]{1,0:T(8,128)(2,1)S(1)}, bf16[256,1152]{1,0:T(8,128)(2,1)S(1)}, u32[]{:S(2)}, u32[]{:S(2)}) collective-permute-start(bf16[256,1152]{1,0:T(8,128)(2,1)S(1)} %collective-permute-done.2.right_ref), channel_id=1, source_target_pairs={{0,4},{4,8},{8,12},{12,16},{16,20},{20,24},{24,28},{28,32},{32,36}... | collective-permute-start | bytes 1769480 | tf_op jit(solution)/shard_map/ppermute | solution.py:53
  21.5 3.0 %collective-permute-start.3 = (bf16[256,1152]{1,0:T(8,128)(2,1)S(1)}, bf16[256,1152]{1,0:T(8,128)(2,1)S(1)}, u32[]{:S(2)}, u32[]{:S(2)}) collective-permute-start(bf16[256,1152]{1,0:T(8,128)(2,1)S(1)} %collective-permute-done.2.right_ref), channel_id=1, source_target_pairs={{0,16},{4,500},{8,504},{12,508},{16,32},{20,4},{24,8},{28,12},{32,... | collective-permute-start | bytes 1769480 | tf_op jit(solution)/shard_map/ppermute | solution.py:53
  24.4 7.1 %collective-permute-done.left_ref = bf16[256,1152]{1,0:T(8,128)(2,1)S(1)} collective-permute-done((bf16[256,1152]{1,0:T(8,128)(2,1)}, bf16[256,1152]{1,0:T(8,128)(2,1)S(1)}, u32[]{:S(2)}, u32[]{:S(2)}) %collective-permute-start) | collective-permute-done | bytes 589856 | tf_op jit(solution)/shard_map/ppermute | solution.py:53
  31.5 9.7 %collective-permute-start.1 = (bf16[256,1152]{1,0:T(8,128)(2,1)S(1)}, bf16[256,1152]{1,0:T(8,128)(2,1)S(1)}, u32[]{:S(2)}, u32[]{:S(2)}) collective-permute-start(bf16[256,1152]{1,0:T(8,128)(2,1)S(1)} %collective-permute-done.left_ref), channel_id=1, source_target_pairs={{0,508},{4,0},{8,20},{12,8},{16,12},{20,16},{24,36},{28,24},{32,28... | collective-permute-start | bytes 1769480 | tf_op jit(solution)/shard_map/ppermute | solution.py:53
  41.3 1.1 copy-done.2
  42.4 2.4 %order.1 = (bf16[1152,256]{1,0:T(8,128)(2,1)S(1)}, bf16[1152,768]{1,0:T(8,128)(2,1)S(1)}, bf16[1152,768]{1,0:T(8,128)(2,1)S(1)}) custom-call(s32[7]{0:T(128)S(1)} %stack.31.place_ref, bf16[256,1152]{1,0:T(8,128)(2,1)S(1)} %bitcast.15), custom_call_target="tpu_custom_call" | custom-call | flops 1073741824 | bytes 4194304 | tf_op jit(solution)/shard_map/order/pallas_call | solution.py:211
  44.8 4.1 %collective-permute-start.6 = (bf16[1152,256]{1,0:T(8,128)(2,1)S(1)}, bf16[1152,256]{1,0:T(8,128)(2,1)S(1)}, u32[]{:S(2)}, u32[]{:S(2)}) collective-permute-start(bf16[1152,256]{1,0:T(8,128)(2,1)S(1)} %get-tuple-element.29.turned_ref), channel_id=1, source_target_pairs={{0,1},{1,0},{2,3},{3,2},{4,5},{5,4},{6,7},{7,6},{8,9},{9,8},{10,11... | collective-permute-start | bytes 1769480 | tf_op jit(solution)/shard_map/ppermute | solution.py:260
  48.9 4.8 %hidden_and_own.1 = (f32[256,1152]{1,0:T(8,128)S(1)}, f32[256,128]{1,0:T(8,128)S(1)}, bf16[256,1152]{1,0:T(8,128)(2,1)S(1)}, f32[256,1152]{1,0:T(8,128)S(1)}, s3...) custom-call(s32[7]{0:T(128)S(1)} %stack.31.place_ref, bf16[256,1152]{1,0:T(8,128)(2,1)S(1)} %bitcast.16, ...), custom_call_target="tpu_custom_call" | custom-call | flops 1073741824 | bytes 4194304 | tf_op jit(solution)/shard_map/hidden_and_own/pallas_call | solution.py:211
  53.7 2.3 %near_pairs.1.acc_ref = f32[256,1152]{1,0:T(8,128)S(1)} custom-call(s32[7]{0:T(128)S(1)} %stack.31.place_ref, bf16[256,1152]{1,0:T(8,128)(2,1)S(1)} %collective-permute-done.2.right_ref, bf16[256,1152]{1,0:T(8,128)(2,1)S(1)} %collective-permute-done.left_ref, s32[8,256]{1,0:T(8,128)S(1)} %get-tuple-element.17.step_ref, ...), custom_call_target="tpu_custom_call" | custom-call | flops 1073741824 | bytes 4194304 | tf_op jit(solution)/shard_map/near_pairs/pallas_call | solution.py:211
  56.0 1.6 %far_right.1.acc_ref = f32[256,1152]{1,0:T(8,128)S(1)} custom-call(s32[7]{0:T(128)S(1)} %stack.31.place_ref, bf16[256,1152]{1,0:T(8,128)(2,1)S(1)} %collective-permute-done.4.image_ref, s32[8,256]{1,0:T(8,128)S(1)} %get-tuple-element.17.step_ref, s32[8,256]{1,0:T(8,128)S(1)} %get-tuple-element.18.col_ref, bf16[256,1152]{1,0:T(8,128)(2,1)S(1)} %get-tuple-element.19.text_ref, ...), custom_call_target="tpu_custom_call" | custom-call | flops 268435456 | bytes 4194304 | tf_op jit(solution)/shard_map/far_right/pallas_call | solution.py:211
  57.9 1.6 %far_across.1.acc_ref = f32[256,1152]{1,0:T(8,128)S(1)} custom-call(s32[7]{0:T(128)S(1)} %stack.31.place_ref, bf16[256,1152]{1,0:T(8,128)(2,1)S(1)} %collective-permute-done.3.image_ref, s32[8,256]{1,0:T(8,128)S(1)} %get-tuple-element.17.step_ref, s32[8,256]{1,0:T(8,128)S(1)} %get-tuple-element.18.col_ref, bf16[256,1152]{1,0:T(8,128)(2,1)S(1)} %get-tuple-element.19.text_ref, ...), custom_call_target="tpu_custom_call" | custom-call | flops 268435456 | bytes 4194304 | tf_op jit(solution)/shard_map/far_across/pallas_call | solution.py:211
  59.5 2.6 %far_left.1 = (bf16[256,1152]{1,0:T(8,128)(2,1)S(1)}, bf16[256,768]{1,0:T(8,128)(2,1)S(1)}) custom-call(s32[7]{0:T(128)S(1)} %stack.31.place_ref, bf16[256,1152]{1,0:T(8,128)(2,1)S(1)} %collective-permute-done.1.left_ref, s32[8,256]{1,0:T(8,128)S(1)} %get-tuple-element.17.step_ref, s32[8,256]{1,0:T(8,128)S(1)} %get-tuple-element.18.col_ref, ...), custom_call_target="tpu_custom_call" | custom-call | flops 1073741824 | bytes 4194304 | tf_op jit(solution)/shard_map/far_left/pallas_call | solution.py:211
  62.1 4.7 %collective-permute-start.5 = (bf16[256,768]{1,0:T(8,128)(2,1)S(1)}, bf16[256,768]{1,0:T(8,128)(2,1)S(1)}, u32[]{:S(2)}, u32[]{:S(2)}) collective-permute-start(bf16[256,768]{1,0:T(8,128)(2,1)S(1)} %get-tuple-element.28), channel_id=1, source_target_pairs={{0,1},{1,0},{2,3},{3,2},{4,5},{5,4},{6,7},{7,6},{8,9},{9,8},{10,11... | collective-permute-start | bytes 1179656 | tf_op jit(solution)/shard_map/ppermute | solution.py:272
  66.8 2.3 %own_columns.1 = (bf16[256,768]{1,0:T(8,128)(2,1)S(1)}, bf16[256,1152]{1,0:T(8,128)(2,1)}) custom-call(bf16[256,1152]{1,0:T(8,128)(2,1)S(1)} %get-tuple-element.24.grad_ref, bf16[1152,768]{1,0:T(8,128)(2,1)S(1)} %get-tuple-element.25.pick_ref, bf16[1152,1152]{1,0:T(8,128)(2,1)S(1)} %copy-done), custom_call_target="tpu_custom_call" | custom-call | flops 268435456 | bytes 4194304 | tf_op jit(solution)/shard_map/own_columns/pallas_call | solution.py:211
  69.1 1.1 partial.1
  70.2 24.2 %all_to_all.15 = bf16[32,8,2688]{2,1,0:T(8,128)(2,1)S(1)} all-to-all(bf16[32,8,2688]{2,1,0:T(8,128)(2,1)S(1)} %bitcast.11), channel_id=1, replica_groups=mesh['yh'=2,'zh'=4,'z1'=2,'z0'=2,'x'=4,'yl'=2,'c'=2] {'yh','yl','x','z0'}, dimensions={0} | all-to-all | bytes 2752512 | tf_op jit(solution)/shard_map/all_to_all | solution.py:224
  94.6 1.9 %collective-permute-start.7 = (bf16[8,2688]{1,0:T(8,128)(2,1)S(1)}, bf16[8,2688]{1,0:T(8,128)(2,1)S(1)}, u32[]{:S(2)}, u32[]{:S(2)}) collective-permute-start(bf16[8,2688]{1,0:T(8,128)(2,1)S(1)} %reduce_sum.12), channel_id=1, source_target_pairs={{0,32},{32,0},{1,33},{33,1},{2,34},{34,2},{3,35},{35,3},{4,36},{36... | collective-permute-start | bytes 129032 | tf_op jit(solution)/shard_map/ppermute | solution.py:280
  96.5 3.8 %collective-permute-done.7 = bf16[8,2688]{1,0:T(8,128)(2,1)S(1)} collective-permute-done((bf16[8,2688]{1,0:T(8,128)(2,1)S(1)}, bf16[8,2688]{1,0:T(8,128)(2,1)S(1)}, u32[]{:S(2)}, u32[]{:S(2)}) %collective-permute-start.7) | collective-permute-done | bytes 43040 | tf_op jit(solution)/shard_map/ppermute | solution.py:280
  100.3 19.4 %all_to_all.16.came_ref = bf16[4,8,2688]{2,1,0:T(8,128)(2,1)S(1)} all-to-all(bf16[4,8,2688]{2,1,0:T(8,128)(2,1)S(1)} %broadcast_in_dim.10), channel_id=1, replica_groups=mesh['yh'=2,'zh'=4,'z1'=2,'z0'=2,'x'=4,'yl'=2,'c'=2] {'zh'}, dimensions={0} | all-to-all | bytes 344064 | tf_op jit(solution)/shard_map/all_to_all | solution.py:224
  119.7 0.7 block.1
  120.4 18.8 %all_to_all.17.square_ref = f32[64,8,128]{2,1,0:T(8,128)S(1)} all-to-all(f32[64,8,128]{2,1,0:T(8,128)S(1)} %get-tuple-element.30), channel_id=1, replica_groups=mesh['yh'=2,'zh'=4,'z1'=2,'z0'=2,'x'=4,'yl'=2,'c'=2] {'yh','yl','x','z0'..., dimensions={0} | all-to-all | bytes 524288 | tf_op jit(solution)/shard_map/all_to_all | solution.py:224
  139.2 0.8 clip.1
  (21 shorter events, 0.5 us)
Async XLA Ops:
  0.6 18.9 %collective-permute-start.2 = (bf16[256,1152]{1,0:T(8,128)(2,1)}, bf16[256,1152]{1,0:T(8,128)(2,1)S(1)}, u32[]{:S(2)}, u32[]{:S(2)}) collective-permute-start(bf16[256,1152]{1,0:T(8,128)(2,1)} %bitcast.12), channel_id=1, source_target_pairs={{0,4},{4,8},{8,12},{12,0},{16,20},{20,24},{24,28},{28,16},{32,36},... | collective-permute-start | bytes 1769480 | tf_op jit(solution)/shard_map/ppermute | solution.py:53
  4.6 26.9 %collective-permute-start = (bf16[256,1152]{1,0:T(8,128)(2,1)}, bf16[256,1152]{1,0:T(8,128)(2,1)S(1)}, u32[]{:S(2)}, u32[]{:S(2)}) collective-permute-start(bf16[256,1152]{1,0:T(8,128)(2,1)} %bitcast.13), channel_id=1, source_target_pairs={{0,508},{4,0},{8,4},{12,8},{16,12},{20,16},{24,20},{28,24},{32,28}... | collective-permute-start | bytes 1769480 | tf_op jit(solution)/shard_map/ppermute | solution.py:53
  19.5 36.5 %collective-permute-start.4 = (bf16[256,1152]{1,0:T(8,128)(2,1)S(1)}, bf16[256,1152]{1,0:T(8,128)(2,1)S(1)}, u32[]{:S(2)}, u32[]{:S(2)}) collective-permute-start(bf16[256,1152]{1,0:T(8,128)(2,1)S(1)} %collective-permute-done.2.right_ref), channel_id=1, source_target_pairs={{0,4},{4,8},{8,12},{12,16},{16,20},{20,24},{24,28},{28,32},{32,36}... | collective-permute-start | bytes 1769480 | tf_op jit(solution)/shard_map/ppermute | solution.py:53
  21.5 36.4 %collective-permute-start.3 = (bf16[256,1152]{1,0:T(8,128)(2,1)S(1)}, bf16[256,1152]{1,0:T(8,128)(2,1)S(1)}, u32[]{:S(2)}, u32[]{:S(2)}) collective-permute-start(bf16[256,1152]{1,0:T(8,128)(2,1)S(1)} %collective-permute-done.2.right_ref), channel_id=1, source_target_pairs={{0,16},{4,500},{8,504},{12,508},{16,32},{20,4},{24,8},{28,12},{32,... | collective-permute-start | bytes 1769480 | tf_op jit(solution)/shard_map/ppermute | solution.py:53
  31.5 28.0 %collective-permute-start.1 = (bf16[256,1152]{1,0:T(8,128)(2,1)S(1)}, bf16[256,1152]{1,0:T(8,128)(2,1)S(1)}, u32[]{:S(2)}, u32[]{:S(2)}) collective-permute-start(bf16[256,1152]{1,0:T(8,128)(2,1)S(1)} %collective-permute-done.left_ref), channel_id=1, source_target_pairs={{0,508},{4,0},{8,20},{12,8},{16,12},{20,16},{24,36},{28,24},{32,28... | collective-permute-start | bytes 1769480 | tf_op jit(solution)/shard_map/ppermute | solution.py:53
  41.3 1.1 copy-start.2
  42.4 6.5 %copy-start.1 = (bf16[1,256,1152]{2,1,0:T(8,128)(2,1)S(1)}, bf16[1,256,1152]{2,1,0:T(8,128)(2,1)}, u32[]{:S(2)}) copy-start(bf16[1,256,1152]{2,1,0:T(8,128)(2,1)} %param.5) | copy-start | bytes 1769476
  42.4 6.5 %copy-start.3 = (bf16[1,256,1152]{2,1,0:T(8,128)(2,1)S(1)}, bf16[1,256,1152]{2,1,0:T(8,128)(2,1)}, u32[]{:S(2)}) copy-start(bf16[1,256,1152]{2,1,0:T(8,128)(2,1)} %param.6) | copy-start | bytes 1769476
  42.4 6.5 %copy-start.4 = (s32[1,32768]{1,0:T(1,128)S(1)}, s32[1,32768]{1,0:T(1,128)}, u32[]{:S(2)}) copy-start(s32[1,32768]{1,0:T(1,128)} %step_hbm.1) | copy-start | bytes 393220
  42.4 6.5 %copy-start.5 = (s32[1,32768]{1,0:T(1,128)S(1)}, s32[1,32768]{1,0:T(1,128)}, u32[]{:S(2)}) copy-start(s32[1,32768]{1,0:T(1,128)} %col_hbm.1) | copy-start | bytes 393220
  44.8 24.3 %collective-permute-start.6 = (bf16[1152,256]{1,0:T(8,128)(2,1)S(1)}, bf16[1152,256]{1,0:T(8,128)(2,1)S(1)}, u32[]{:S(2)}, u32[]{:S(2)}) collective-permute-start(bf16[1152,256]{1,0:T(8,128)(2,1)S(1)} %get-tuple-element.29.turned_ref), channel_id=1, source_target_pairs={{0,1},{1,0},{2,3},{3,2},{4,5},{5,4},{6,7},{7,6},{8,9},{9,8},{10,11... | collective-permute-start | bytes 1769480 | tf_op jit(solution)/shard_map/ppermute | solution.py:260
  59.5 7.3 %copy-start = (bf16[1152,1152]{1,0:T(8,128)(2,1)S(1)}, bf16[1152,1152]{1,0:T(8,128)(2,1)}, u32[]{:S(2)}) copy-start(bf16[1152,1152]{1,0:T(8,128)(2,1)} %proj_ref.1) | copy-start | bytes 7962628
  62.1 7.0 %collective-permute-start.5 = (bf16[256,768]{1,0:T(8,128)(2,1)S(1)}, bf16[256,768]{1,0:T(8,128)(2,1)S(1)}, u32[]{:S(2)}, u32[]{:S(2)}) collective-permute-start(bf16[256,768]{1,0:T(8,128)(2,1)S(1)} %get-tuple-element.28), channel_id=1, source_target_pairs={{0,1},{1,0},{2,3},{3,2},{4,5},{5,4},{6,7},{7,6},{8,9},{9,8},{10,11... | collective-permute-start | bytes 1179656 | tf_op jit(solution)/shard_map/ppermute | solution.py:272
  94.6 5.7 %collective-permute-start.7 = (bf16[8,2688]{1,0:T(8,128)(2,1)S(1)}, bf16[8,2688]{1,0:T(8,128)(2,1)S(1)}, u32[]{:S(2)}, u32[]{:S(2)}) collective-permute-start(bf16[8,2688]{1,0:T(8,128)(2,1)S(1)} %reduce_sum.12), channel_id=1, source_target_pairs={{0,32},{32,0},{1,33},{33,1},{2,34},{34,2},{3,35},{35,3},{4,36},{36... | collective-permute-start | bytes 129032 | tf_op jit(solution)/shard_map/ppermute | solution.py:280

commit v8 on v7

--- a/solution.py
+++ b/solution.py
@@ -259,7 +259,7 @@
     swap = [(0, 1), (1, 0)]
     opposite = lax.ppermute(turned, "c", swap)
     (acc,) = call(near_kernel, (place, right, left, steps, cols, texts, acc), ((full, F32),), 1 << 30, 24, "near_pairs")
-    for at, block, name in ((2, right2, "far_right"), (4, across, "far_across")):
+    for at, block, name in ((4, across, "far_across"), (2, right2, "far_right")):
         (acc,) = call(
             functools.partial(far_kernel, at), (place, block, steps, cols, texts, acc), ((full, F32),), 1 << 28, 24, name
         )

time: 141 us -> 139 us (0.986)
  waiting for transfers between devices: 11 us -> 4.22 us
  starting transfers between devices: 44.1 us -> 50.4 us
    ppermute x5, waiting for transfers between devices: 7.26 us -> 0.01 us  [shifted(): return lax.ppermute(value, DP, pairs)]
    ppermute x5, starting transfers between devices: 33.5 us -> 40.5 us  [shifted(): return lax.ppermute(value, DP, pairs)]
    ppermute x1, starting transfers between devices: 4.66 us -> 3.08 us  [local(): columns = lax.ppermute(columns, 'c', swap)]
  transfers between devices with their start and end apart: 8 -> 8, of which waited for: 3 -> 1; matrix products, arithmetic and copies ran while one was open for 0% -> 0% of each run, Pallas kernels for 13% -> 13%
where the time goes in v8:
time: 139 us
  blocking collectives  61.8 us (44%)
  starting transfers between devices  50.4 us (36%)
  Pallas kernels  20.2 us (15%)
  waiting for transfers between devices  4.22 us (3%)
    all_to_all x3, blocking collectives, traded(): return lax.all_to_all(value, axis, split_axis=0, concat_axis=0)  61.8 us
    ppermute x5, starting transfers between devices, shifted(): return lax.ppermute(value, DP, pairs)  40.5 us
    pallas_call x10, Pallas kernels, call(): pl.pallas_call(kernel, out_shape=[jax.ShapeDtypeStruct(shape, dtype) for...  20.2 us
    ppermute x1, starting transfers between devices, local(): opposite = lax.ppermute(turned, 'c', swap)  4.84 us
    ppermute x1, waiting for transfers between devices, local(): near = lax.ppermute(rows, 'z1', swap)  4.2 us
    ppermute x1, starting transfers between devices, local(): columns = lax.ppermute(columns, 'c', swap)  3.08 us
  transfers between devices with their start and end apart: 8, of which 1 were waited for; matrix products, arithmetic and copies ran while one was open for 0% of the time, Pallas kernels for 13%

profile of v8, /device:TPU:1, one launch (start us, length us, event | category | flops | bytes accessed | tf_op | source)
XLA Modules:
  0.0 138.9 jit_solution(10605191207457655090)
XLA Ops:
  0.6 4.0 %collective-permute-start.2 = (bf16[256,1152]{1,0:T(8,128)(2,1)}, bf16[256,1152]{1,0:T(8,128)(2,1)S(1)}, u32[]{:S(2)}, u32[]{:S(2)}) collective-permute-start(bf16[256,1152]{1,0:T(8,128)(2,1)} %bitcast.12), channel_id=1, source_target_pairs={{0,4},{4,8},{8,12},{12,0},{16,20},{20,24},{24,28},{28,16},{32,36},... | collective-permute-start | bytes 1769480 | tf_op jit(solution)/shard_map/ppermute | solution.py:53
  4.6 14.9 %collective-permute-start = (bf16[256,1152]{1,0:T(8,128)(2,1)}, bf16[256,1152]{1,0:T(8,128)(2,1)S(1)}, u32[]{:S(2)}, u32[]{:S(2)}) collective-permute-start(bf16[256,1152]{1,0:T(8,128)(2,1)} %bitcast.13), channel_id=1, source_target_pairs={{0,508},{4,0},{8,4},{12,8},{16,12},{20,16},{24,20},{28,24},{32,28}... | collective-permute-start | bytes 1769480 | tf_op jit(solution)/shard_map/ppermute | solution.py:53
  19.5 3.0 %collective-permute-start.4 = (bf16[256,1152]{1,0:T(8,128)(2,1)S(1)}, bf16[256,1152]{1,0:T(8,128)(2,1)S(1)}, u32[]{:S(2)}, u32[]{:S(2)}) collective-permute-start(bf16[256,1152]{1,0:T(8,128)(2,1)S(1)} %collective-permute-done.2.right_ref), channel_id=1, source_target_pairs={{0,16},{4,500},{8,504},{12,508},{16,32},{20,4},{24,8},{28,12},{32,... | collective-permute-start | bytes 1769480 | tf_op jit(solution)/shard_map/ppermute | solution.py:53
  22.5 12.1 %collective-permute-start.3 = (bf16[256,1152]{1,0:T(8,128)(2,1)S(1)}, bf16[256,1152]{1,0:T(8,128)(2,1)S(1)}, u32[]{:S(2)}, u32[]{:S(2)}) collective-permute-start(bf16[256,1152]{1,0:T(8,128)(2,1)S(1)} %collective-permute-done.2.right_ref), channel_id=1, source_target_pairs={{0,4},{4,8},{8,12},{12,16},{16,20},{20,24},{24,28},{28,32},{32,36}... | collective-permute-start | bytes 1769480 | tf_op jit(solution)/shard_map/ppermute | solution.py:53
  34.6 6.6 %collective-permute-start.1 = (bf16[256,1152]{1,0:T(8,128)(2,1)S(1)}, bf16[256,1152]{1,0:T(8,128)(2,1)S(1)}, u32[]{:S(2)}, u32[]{:S(2)}) collective-permute-start(bf16[256,1152]{1,0:T(8,128)(2,1)S(1)} %collective-permute-done.left_ref), channel_id=1, source_target_pairs={{0,508},{4,0},{8,20},{12,8},{16,12},{20,16},{24,36},{28,24},{32,28... | collective-permute-start | bytes 1769480 | tf_op jit(solution)/shard_map/ppermute | solution.py:53
  41.3 1.1 copy-done.2
  42.4 2.4 %order.1 = (bf16[1152,256]{1,0:T(8,128)(2,1)S(1)}, bf16[1152,768]{1,0:T(8,128)(2,1)S(1)}, bf16[1152,768]{1,0:T(8,128)(2,1)S(1)}) custom-call(s32[7]{0:T(128)S(1)} %stack.31.place_ref, bf16[256,1152]{1,0:T(8,128)(2,1)S(1)} %bitcast.15), custom_call_target="tpu_custom_call" | custom-call | flops 1073741824 | bytes 4194304 | tf_op jit(solution)/shard_map/order/pallas_call | solution.py:211
  44.8 4.8 %collective-permute-start.6 = (bf16[1152,256]{1,0:T(8,128)(2,1)S(1)}, bf16[1152,256]{1,0:T(8,128)(2,1)S(1)}, u32[]{:S(2)}, u32[]{:S(2)}) collective-permute-start(bf16[1152,256]{1,0:T(8,128)(2,1)S(1)} %get-tuple-element.29.turned_ref), channel_id=1, source_target_pairs={{0,1},{1,0},{2,3},{3,2},{4,5},{5,4},{6,7},{7,6},{8,9},{9,8},{10,11... | collective-permute-start | bytes 1769480 | tf_op jit(solution)/shard_map/ppermute | solution.py:260
  49.7 4.8 %hidden_and_own.1 = (f32[256,1152]{1,0:T(8,128)S(1)}, f32[256,128]{1,0:T(8,128)S(1)}, bf16[256,1152]{1,0:T(8,128)(2,1)S(1)}, f32[256,1152]{1,0:T(8,128)S(1)}, s3...) custom-call(s32[7]{0:T(128)S(1)} %stack.31.place_ref, bf16[256,1152]{1,0:T(8,128)(2,1)S(1)} %bitcast.16, ...), custom_call_target="tpu_custom_call" | custom-call | flops 1073741824 | bytes 4194304 | tf_op jit(solution)/shard_map/hidden_and_own/pallas_call | solution.py:211
  54.5 2.3 %near_pairs.1.acc_ref = f32[256,1152]{1,0:T(8,128)S(1)} custom-call(s32[7]{0:T(128)S(1)} %stack.31.place_ref, bf16[256,1152]{1,0:T(8,128)(2,1)S(1)} %collective-permute-done.2.right_ref, bf16[256,1152]{1,0:T(8,128)(2,1)S(1)} %collective-permute-done.left_ref, s32[8,256]{1,0:T(8,128)S(1)} %get-tuple-element.17.step_ref, ...), custom_call_target="tpu_custom_call" | custom-call | flops 1073741824 | bytes 4194304 | tf_op jit(solution)/shard_map/near_pairs/pallas_call | solution.py:211
  56.8 1.6 %far_across.1.acc_ref = f32[256,1152]{1,0:T(8,128)S(1)} custom-call(s32[7]{0:T(128)S(1)} %stack.31.place_ref, bf16[256,1152]{1,0:T(8,128)(2,1)S(1)} %collective-permute-done.4.image_ref, s32[8,256]{1,0:T(8,128)S(1)} %get-tuple-element.17.step_ref, s32[8,256]{1,0:T(8,128)S(1)} %get-tuple-element.18.col_ref, bf16[256,1152]{1,0:T(8,128)(2,1)S(1)} %get-tuple-element.19.text_ref, ...), custom_call_target="tpu_custom_call" | custom-call | flops 268435456 | bytes 4194304 | tf_op jit(solution)/shard_map/far_across/pallas_call | solution.py:211
  58.5 1.6 %far_right.1.acc_ref = f32[256,1152]{1,0:T(8,128)S(1)} custom-call(s32[7]{0:T(128)S(1)} %stack.31.place_ref, bf16[256,1152]{1,0:T(8,128)(2,1)S(1)} %collective-permute-done.3.image_ref, s32[8,256]{1,0:T(8,128)S(1)} %get-tuple-element.17.step_ref, s32[8,256]{1,0:T(8,128)S(1)} %get-tuple-element.18.col_ref, bf16[256,1152]{1,0:T(8,128)(2,1)S(1)} %get-tuple-element.19.text_ref, ...), custom_call_target="tpu_custom_call" | custom-call | flops 268435456 | bytes 4194304 | tf_op jit(solution)/shard_map/far_right/pallas_call | solution.py:211
  60.1 2.6 %far_left.1 = (bf16[256,1152]{1,0:T(8,128)(2,1)S(1)}, bf16[256,768]{1,0:T(8,128)(2,1)S(1)}) custom-call(s32[7]{0:T(128)S(1)} %stack.31.place_ref, bf16[256,1152]{1,0:T(8,128)(2,1)S(1)} %collective-permute-done.1.left_ref, s32[8,256]{1,0:T(8,128)S(1)} %get-tuple-element.17.step_ref, s32[8,256]{1,0:T(8,128)S(1)} %get-tuple-element.18.col_ref, ...), custom_call_target="tpu_custom_call" | custom-call | flops 1073741824 | bytes 4194304 | tf_op jit(solution)/shard_map/far_left/pallas_call | solution.py:211
  62.7 3.1 %collective-permute-start.5 = (bf16[256,768]{1,0:T(8,128)(2,1)S(1)}, bf16[256,768]{1,0:T(8,128)(2,1)S(1)}, u32[]{:S(2)}, u32[]{:S(2)}) collective-permute-start(bf16[256,768]{1,0:T(8,128)(2,1)S(1)} %get-tuple-element.28), channel_id=1, source_target_pairs={{0,1},{1,0},{2,3},{3,2},{4,5},{5,4},{6,7},{7,6},{8,9},{9,8},{10,11... | collective-permute-start | bytes 1179656 | tf_op jit(solution)/shard_map/ppermute | solution.py:272
  65.8 2.3 %own_columns.1 = (bf16[256,768]{1,0:T(8,128)(2,1)S(1)}, bf16[256,1152]{1,0:T(8,128)(2,1)}) custom-call(bf16[256,1152]{1,0:T(8,128)(2,1)S(1)} %get-tuple-element.24.grad_ref, bf16[1152,768]{1,0:T(8,128)(2,1)S(1)} %get-tuple-element.25.pick_ref, bf16[1152,1152]{1,0:T(8,128)(2,1)S(1)} %copy-done), custom_call_target="tpu_custom_call" | custom-call | flops 268435456 | bytes 4194304 | tf_op jit(solution)/shard_map/own_columns/pallas_call | solution.py:211
  68.1 1.1 partial.1
  69.2 24.2 %all_to_all.15 = bf16[32,8,2688]{2,1,0:T(8,128)(2,1)S(1)} all-to-all(bf16[32,8,2688]{2,1,0:T(8,128)(2,1)S(1)} %bitcast.11), channel_id=1, replica_groups=mesh['yh'=2,'zh'=4,'z1'=2,'z0'=2,'x'=4,'yl'=2,'c'=2] {'yh','yl','x','z0'}, dimensions={0} | all-to-all | bytes 2752512 | tf_op jit(solution)/shard_map/all_to_all | solution.py:224
  93.4 0.2 reduce_sum.12
  93.6 1.9 %collective-permute-start.7 = (bf16[8,2688]{1,0:T(8,128)(2,1)S(1)}, bf16[8,2688]{1,0:T(8,128)(2,1)S(1)}, u32[]{:S(2)}, u32[]{:S(2)}) collective-permute-start(bf16[8,2688]{1,0:T(8,128)(2,1)S(1)} %reduce_sum.12), channel_id=1, source_target_pairs={{0,32},{32,0},{1,33},{33,1},{2,34},{34,2},{3,35},{35,3},{4,36},{36... | collective-permute-start | bytes 129032 | tf_op jit(solution)/shard_map/ppermute | solution.py:280
  95.5 4.2 %collective-permute-done.7 = bf16[8,2688]{1,0:T(8,128)(2,1)S(1)} collective-permute-done((bf16[8,2688]{1,0:T(8,128)(2,1)S(1)}, bf16[8,2688]{1,0:T(8,128)(2,1)S(1)}, u32[]{:S(2)}, u32[]{:S(2)}) %collective-permute-start.7) | collective-permute-done | bytes 43040 | tf_op jit(solution)/shard_map/ppermute | solution.py:280
  99.8 18.8 %all_to_all.16.came_ref = bf16[4,8,2688]{2,1,0:T(8,128)(2,1)S(1)} all-to-all(bf16[4,8,2688]{2,1,0:T(8,128)(2,1)S(1)} %broadcast_in_dim.10), channel_id=1, replica_groups=mesh['yh'=2,'zh'=4,'z1'=2,'z0'=2,'x'=4,'yl'=2,'c'=2] {'zh'}, dimensions={0} | all-to-all | bytes 344064 | tf_op jit(solution)/shard_map/all_to_all | solution.py:224
  118.6 0.7 block.1
  119.2 18.8 %all_to_all.17.square_ref = f32[64,8,128]{2,1,0:T(8,128)S(1)} all-to-all(f32[64,8,128]{2,1,0:T(8,128)S(1)} %get-tuple-element.30), channel_id=1, replica_groups=mesh['yh'=2,'zh'=4,'z1'=2,'z0'=2,'x'=4,'yl'=2,'c'=2] {'yh','yl','x','z0'..., dimensions={0} | all-to-all | bytes 524288 | tf_op jit(solution)/shard_map/all_to_all | solution.py:224
  138.1 0.8 clip.1
  (21 shorter events, 0.2 us)
Async XLA Ops:
  0.6 18.9 %collective-permute-start.2 = (bf16[256,1152]{1,0:T(8,128)(2,1)}, bf16[256,1152]{1,0:T(8,128)(2,1)S(1)}, u32[]{:S(2)}, u32[]{:S(2)}) collective-permute-start(bf16[256,1152]{1,0:T(8,128)(2,1)} %bitcast.12), channel_id=1, source_target_pairs={{0,4},{4,8},{8,12},{12,0},{16,20},{20,24},{24,28},{28,16},{32,36},... | collective-permute-start | bytes 1769480 | tf_op jit(solution)/shard_map/ppermute | solution.py:53
  4.6 30.1 %collective-permute-start = (bf16[256,1152]{1,0:T(8,128)(2,1)}, bf16[256,1152]{1,0:T(8,128)(2,1)S(1)}, u32[]{:S(2)}, u32[]{:S(2)}) collective-permute-start(bf16[256,1152]{1,0:T(8,128)(2,1)} %bitcast.13), channel_id=1, source_target_pairs={{0,508},{4,0},{8,4},{12,8},{16,12},{20,16},{24,20},{28,24},{32,28}... | collective-permute-start | bytes 1769480 | tf_op jit(solution)/shard_map/ppermute | solution.py:53
  19.5 37.3 %collective-permute-start.4 = (bf16[256,1152]{1,0:T(8,128)(2,1)S(1)}, bf16[256,1152]{1,0:T(8,128)(2,1)S(1)}, u32[]{:S(2)}, u32[]{:S(2)}) collective-permute-start(bf16[256,1152]{1,0:T(8,128)(2,1)S(1)} %collective-permute-done.2.right_ref), channel_id=1, source_target_pairs={{0,16},{4,500},{8,504},{12,508},{16,32},{20,4},{24,8},{28,12},{32,... | collective-permute-start | bytes 1769480 | tf_op jit(solution)/shard_map/ppermute | solution.py:53
  22.5 35.9 %collective-permute-start.3 = (bf16[256,1152]{1,0:T(8,128)(2,1)S(1)}, bf16[256,1152]{1,0:T(8,128)(2,1)S(1)}, u32[]{:S(2)}, u32[]{:S(2)}) collective-permute-start(bf16[256,1152]{1,0:T(8,128)(2,1)S(1)} %collective-permute-done.2.right_ref), channel_id=1, source_target_pairs={{0,4},{4,8},{8,12},{12,16},{16,20},{20,24},{24,28},{28,32},{32,36}... | collective-permute-start | bytes 1769480 | tf_op jit(solution)/shard_map/ppermute | solution.py:53
  34.6 25.4 %collective-permute-start.1 = (bf16[256,1152]{1,0:T(8,128)(2,1)S(1)}, bf16[256,1152]{1,0:T(8,128)(2,1)S(1)}, u32[]{:S(2)}, u32[]{:S(2)}) collective-permute-start(bf16[256,1152]{1,0:T(8,128)(2,1)S(1)} %collective-permute-done.left_ref), channel_id=1, source_target_pairs={{0,508},{4,0},{8,20},{12,8},{16,12},{20,16},{24,36},{28,24},{32,28... | collective-permute-start | bytes 1769480 | tf_op jit(solution)/shard_map/ppermute | solution.py:53
  41.3 1.1 copy-start.2
  42.4 7.3 %copy-start.1 = (bf16[1,256,1152]{2,1,0:T(8,128)(2,1)S(1)}, bf16[1,256,1152]{2,1,0:T(8,128)(2,1)}, u32[]{:S(2)}) copy-start(bf16[1,256,1152]{2,1,0:T(8,128)(2,1)} %param.5) | copy-start | bytes 1769476
  42.4 7.3 %copy-start.3 = (bf16[1,256,1152]{2,1,0:T(8,128)(2,1)S(1)}, bf16[1,256,1152]{2,1,0:T(8,128)(2,1)}, u32[]{:S(2)}) copy-start(bf16[1,256,1152]{2,1,0:T(8,128)(2,1)} %param.6) | copy-start | bytes 1769476
  42.4 7.3 %copy-start.4 = (s32[1,32768]{1,0:T(1,128)S(1)}, s32[1,32768]{1,0:T(1,128)}, u32[]{:S(2)}) copy-start(s32[1,32768]{1,0:T(1,128)} %step_hbm.1) | copy-start | bytes 393220
  42.4 7.3 %copy-start.5 = (s32[1,32768]{1,0:T(1,128)S(1)}, s32[1,32768]{1,0:T(1,128)}, u32[]{:S(2)}) copy-start(s32[1,32768]{1,0:T(1,128)} %col_hbm.1) | copy-start | bytes 393220
  44.8 23.3 %collective-permute-start.6 = (bf16[1152,256]{1,0:T(8,128)(2,1)S(1)}, bf16[1152,256]{1,0:T(8,128)(2,1)S(1)}, u32[]{:S(2)}, u32[]{:S(2)}) collective-permute-start(bf16[1152,256]{1,0:T(8,128)(2,1)S(1)} %get-tuple-element.29.turned_ref), channel_id=1, source_target_pairs={{0,1},{1,0},{2,3},{3,2},{4,5},{5,4},{6,7},{7,6},{8,9},{9,8},{10,11... | collective-permute-start | bytes 1769480 | tf_op jit(solution)/shard_map/ppermute | solution.py:260
  60.1 5.7 %copy-start = (bf16[1152,1152]{1,0:T(8,128)(2,1)S(1)}, bf16[1152,1152]{1,0:T(8,128)(2,1)}, u32[]{:S(2)}) copy-start(bf16[1152,1152]{1,0:T(8,128)(2,1)} %proj_ref.1) | copy-start | bytes 7962628
  62.7 5.4 %collective-permute-start.5 = (bf16[256,768]{1,0:T(8,128)(2,1)S(1)}, bf16[256,768]{1,0:T(8,128)(2,1)S(1)}, u32[]{:S(2)}, u32[]{:S(2)}) collective-permute-start(bf16[256,768]{1,0:T(8,128)(2,1)S(1)} %get-tuple-element.28), channel_id=1, source_target_pairs={{0,1},{1,0},{2,3},{3,2},{4,5},{5,4},{6,7},{7,6},{8,9},{9,8},{10,11... | collective-permute-start | bytes 1179656 | tf_op jit(solution)/shard_map/ppermute | solution.py:272
  93.6 6.1 %collective-permute-start.7 = (bf16[8,2688]{1,0:T(8,128)(2,1)S(1)}, bf16[8,2688]{1,0:T(8,128)(2,1)S(1)}, u32[]{:S(2)}, u32[]{:S(2)}) collective-permute-start(bf16[8,2688]{1,0:T(8,128)(2,1)S(1)} %reduce_sum.12), channel_id=1, source_target_pairs={{0,32},{32,0},{1,33},{33,1},{2,34},{34,2},{3,35},{35,3},{4,36},{36... | collective-permute-start | bytes 129032 | tf_op jit(solution)/shard_map/ppermute | solution.py:280

commit v9 on v8

--- a/solution.py
+++ b/solution.py
@@ -237,9 +237,6 @@
     features = text_features[0]
     right = shifted(image, RIGHT)
     left = shifted(image, LEFT)
-    right2 = shifted(right, RIGHT2)
-    left2 = shifted(left, LEFT2)
-    across = shifted(right, ACROSS)
 
     full = (ROWS, E)
     table = (8, ROWS)
@@ -253,6 +250,10 @@
             pltpu.VMEM(pair_step.shape, jnp.int32), pltpu.VMEM(pair_col.shape, jnp.int32), pltpu.SemaphoreType.DMA((5,)),
         ),
     )
+    right, acc = lax.optimization_barrier((right, acc))
+    right2 = shifted(right, RIGHT2)
+    left2 = shifted(left, LEFT2)
+    across = shifted(right, ACROSS)
     turned, pick_there, pick_here = call(
         order_kernel, (place, features), (((D, ROWS), BF16), ((E, PICK), BF16), ((E, PICK), BF16)), 1 << 30, 32, "order"
     )

time: 139 us -> 139 us (level)
  starting transfers between devices: 50.4 us -> 42.8 us
  waiting for transfers between devices: 4.22 us -> 11.6 us
  local copies, waits for them, and re-layouts: 1.19 us -> 4.04 us
  blocking collectives: 61.8 us -> 59.2 us
    ppermute x5, starting transfers between devices: 40.5 us -> 31.8 us  [shifted(): return lax.ppermute(value, DP, pairs)]
    ppermute x5, waiting for transfers between devices: 0.01 us -> 7.42 us  [shifted(): return lax.ppermute(value, DP, pairs)]
    unnamed x12 -> x10, local copies, waits for them, and re-layouts: 1.09 us -> 3.94 us
    all_to_all x3, blocking collectives: 61.8 us -> 59.2 us  [traded(): return lax.all_to_all(value, axis, split_axis=0, concat_axis=0)]
  transfers between devices with their start and end apart: 8 -> 8, of which waited for: 1 -> 3; matrix products, arithmetic and copies ran while one was open for 0% -> 0% of each run, Pallas kernels for 13% -> 13%
where the time goes in v9:
time: 139 us
  blocking collectives  59.2 us (43%)
  starting transfers between devices  42.8 us (31%)
  Pallas kernels  20.2 us (15%)
  waiting for transfers between devices  11.6 us (8%)
  local copies, waits for them, and re-layouts  4.04 us (3%)
    all_to_all x3, blocking collectives, traded(): return lax.all_to_all(value, axis, split_axis=0, concat_axis=0)  59.2 us
    ppermute x5, starting transfers between devices, shifted(): return lax.ppermute(value, DP, pairs)  31.8 us
    pallas_call x10, Pallas kernels, call(): pl.pallas_call(kernel, out_shape=[jax.ShapeDtypeStruct(shape, dtype) for...  20.2 us
    ppermute x5, waiting for transfers between devices, shifted(): return lax.ppermute(value, DP, pairs)  7.42 us
    ppermute x1, starting transfers between devices, local(): opposite = lax.ppermute(turned, 'c', swap)  4.72 us
    ppermute x1, starting transfers between devices, local(): columns = lax.ppermute(columns, 'c', swap)  4.36 us
    ppermute x1, waiting for transfers between devices, local(): near = lax.ppermute(rows, 'z1', swap)  4.2 us
    unnamed x10, local copies, waits for them, and re-layouts  3.94 us
  transfers between devices with their start and end apart: 8, of which 3 were waited for; matrix products, arithmetic and copies ran while one was open for 0% of the time, Pallas kernels for 13%

profile of v9, /device:TPU:1, one launch (start us, length us, event | category | flops | bytes accessed | tf_op | source)
XLA Modules:
  0.0 138.9 jit_solution(6136936777446594172)
XLA Ops:
  0.6 4.0 %collective-permute-start.2 = (bf16[256,1152]{1,0:T(8,128)(2,1)}, bf16[256,1152]{1,0:T(8,128)(2,1)S(1)}, u32[]{:S(2)}, u32[]{:S(2)}) collective-permute-start(bf16[256,1152]{1,0:T(8,128)(2,1)} %bitcast.12), channel_id=1, source_target_pairs={{0,4},{4,8},{8,12},{12,0},{16,20},{20,24},{24,28},{28,16},{32,36},... | collective-permute-start | bytes 1769480 | tf_op jit(solution)/shard_map/ppermute | solution.py:53
  4.6 14.9 %collective-permute-start = (bf16[256,1152]{1,0:T(8,128)(2,1)}, bf16[256,1152]{1,0:T(8,128)(2,1)S(1)}, u32[]{:S(2)}, u32[]{:S(2)}) collective-permute-start(bf16[256,1152]{1,0:T(8,128)(2,1)} %bitcast.13), channel_id=1, source_target_pairs={{0,508},{4,0},{8,4},{12,8},{16,12},{20,16},{24,20},{28,24},{32,28}... | collective-permute-start | bytes 1769480 | tf_op jit(solution)/shard_map/ppermute | solution.py:53
  19.7 1.1 copy-done.1
  20.7 1.1 copy-done.2
  23.6 4.8 %hidden_and_own.1 = (f32[256,1152]{1,0:T(8,128)S(1)}, f32[256,128]{1,0:T(8,128)S(1)}, bf16[256,1152]{1,0:T(8,128)(2,1)S(1)}, f32[256,1152]{1,0:T(8,128)S(1)}, s3...) custom-call(s32[7]{0:T(128)S(1)} %stack.31.place_ref, bf16[256,1152]{1,0:T(8,128)(2,1)S(1)} %bitcast.15, ...), custom_call_target="tpu_custom_call" | custom-call | flops 1073741824 | bytes 4194304 | tf_op jit(solution)/shard_map/hidden_and_own/pallas_call | solution.py:211
  28.4 1.9 %collective-permute-start.4 = (bf16[256,1152]{1,0:T(8,128)(2,1)S(1)}, bf16[256,1152]{1,0:T(8,128)(2,1)S(1)}, u32[]{:S(2)}, u32[]{:S(2)}) collective-permute-start(bf16[256,1152]{1,0:T(8,128)(2,1)S(1)} %collective-permute-done.2.right_ref), channel_id=1, source_target_pairs={{0,16},{4,500},{8,504},{12,508},{16,32},{20,4},{24,8},{28,12},{32,... | collective-permute-start | bytes 1769480 | tf_op jit(solution)/shard_map/ppermute | solution.py:53
  30.3 4.3 %collective-permute-start.3 = (bf16[256,1152]{1,0:T(8,128)(2,1)S(1)}, bf16[256,1152]{1,0:T(8,128)(2,1)S(1)}, u32[]{:S(2)}, u32[]{:S(2)}) collective-permute-start(bf16[256,1152]{1,0:T(8,128)(2,1)S(1)} %collective-permute-done.2.right_ref), channel_id=1, source_target_pairs={{0,4},{4,8},{8,12},{12,16},{16,20},{20,24},{24,28},{28,32},{32,36}... | collective-permute-start | bytes 1769480 | tf_op jit(solution)/shard_map/ppermute | solution.py:53
  34.6 6.7 %collective-permute-start.1 = (bf16[256,1152]{1,0:T(8,128)(2,1)S(1)}, bf16[256,1152]{1,0:T(8,128)(2,1)S(1)}, u32[]{:S(2)}, u32[]{:S(2)}) collective-permute-start(bf16[256,1152]{1,0:T(8,128)(2,1)S(1)} %collective-permute-done.left_ref), channel_id=1, source_target_pairs={{0,508},{4,0},{8,20},{12,8},{16,12},{20,16},{24,36},{28,24},{32,28... | collective-permute-start | bytes 1769480 | tf_op jit(solution)/shard_map/ppermute | solution.py:53
  41.3 2.4 %order.1 = (bf16[1152,256]{1,0:T(8,128)(2,1)S(1)}, bf16[1152,768]{1,0:T(8,128)(2,1)S(1)}, bf16[1152,768]{1,0:T(8,128)(2,1)S(1)}) custom-call(s32[7]{0:T(128)S(1)} %stack.31.place_ref, bf16[256,1152]{1,0:T(8,128)(2,1)S(1)} %bitcast.16), custom_call_target="tpu_custom_call" | custom-call | flops 1073741824 | bytes 4194304 | tf_op jit(solution)/shard_map/order/pallas_call | solution.py:211
  43.8 4.7 %collective-permute-start.6 = (bf16[1152,256]{1,0:T(8,128)(2,1)S(1)}, bf16[1152,256]{1,0:T(8,128)(2,1)S(1)}, u32[]{:S(2)}, u32[]{:S(2)}) collective-permute-start(bf16[1152,256]{1,0:T(8,128)(2,1)S(1)} %get-tuple-element.33.turned_ref), channel_id=1, source_target_pairs={{0,1},{1,0},{2,3},{3,2},{4,5},{5,4},{6,7},{7,6},{8,9},{9,8},{10,11... | collective-permute-start | bytes 1769480 | tf_op jit(solution)/shard_map/ppermute | solution.py:261
  48.5 2.3 %near_pairs.1.acc_ref = f32[256,1152]{1,0:T(8,128)S(1)} custom-call(s32[7]{0:T(128)S(1)} %stack.31.place_ref, bf16[256,1152]{1,0:T(8,128)(2,1)S(1)} %collective-permute-done.2.right_ref, bf16[256,1152]{1,0:T(8,128)(2,1)S(1)} %collective-permute-done.left_ref, s32[8,256]{1,0:T(8,128)S(1)} %get-tuple-element.19.step_ref, ...), custom_call_target="tpu_custom_call" | custom-call | flops 1073741824 | bytes 4194304 | tf_op jit(solution)/shard_map/near_pairs/pallas_call | solution.py:211
  50.8 4.4 %collective-permute-done.4.image_ref = bf16[256,1152]{1,0:T(8,128)(2,1)S(1)} collective-permute-done((bf16[256,1152]{1,0:T(8,128)(2,1)S(1)}, bf16[256,1152]{1,0:T(8,128)(2,1)S(1)}, u32[]{:S(2)}, u32[]{:S(2)}) %collective-permute-start.4) | collective-permute-done | bytes 589856 | tf_op jit(solution)/shard_map/ppermute | solution.py:53
  55.2 1.6 %far_across.1.acc_ref = f32[256,1152]{1,0:T(8,128)S(1)} custom-call(s32[7]{0:T(128)S(1)} %stack.31.place_ref, bf16[256,1152]{1,0:T(8,128)(2,1)S(1)} %collective-permute-done.4.image_ref, s32[8,256]{1,0:T(8,128)S(1)} %get-tuple-element.19.step_ref, s32[8,256]{1,0:T(8,128)S(1)} %get-tuple-element.20.col_ref, bf16[256,1152]{1,0:T(8,128)(2,1)S(1)} %get-tuple-element.21.text_ref, ...), custom_call_target="tpu_custom_call" | custom-call | flops 268435456 | bytes 4194304 | tf_op jit(solution)/shard_map/far_across/pallas_call | solution.py:211
  56.8 3.0 %collective-permute-done.3.image_ref = bf16[256,1152]{1,0:T(8,128)(2,1)S(1)} collective-permute-done((bf16[256,1152]{1,0:T(8,128)(2,1)S(1)}, bf16[256,1152]{1,0:T(8,128)(2,1)S(1)}, u32[]{:S(2)}, u32[]{:S(2)}) %collective-permute-start.3) | collective-permute-done | bytes 589856 | tf_op jit(solution)/shard_map/ppermute | solution.py:53
  59.8 1.6 %far_right.1.acc_ref = f32[256,1152]{1,0:T(8,128)S(1)} custom-call(s32[7]{0:T(128)S(1)} %stack.31.place_ref, bf16[256,1152]{1,0:T(8,128)(2,1)S(1)} %collective-permute-done.3.image_ref, s32[8,256]{1,0:T(8,128)S(1)} %get-tuple-element.19.step_ref, s32[8,256]{1,0:T(8,128)S(1)} %get-tuple-element.20.col_ref, bf16[256,1152]{1,0:T(8,128)(2,1)S(1)} %get-tuple-element.21.text_ref, ...), custom_call_target="tpu_custom_call" | custom-call | flops 268435456 | bytes 4194304 | tf_op jit(solution)/shard_map/far_right/pallas_call | solution.py:211
  61.5 2.6 %far_left.1 = (bf16[256,1152]{1,0:T(8,128)(2,1)S(1)}, bf16[256,768]{1,0:T(8,128)(2,1)S(1)}) custom-call(s32[7]{0:T(128)S(1)} %stack.31.place_ref, bf16[256,1152]{1,0:T(8,128)(2,1)S(1)} %collective-permute-done.1.left_ref, s32[8,256]{1,0:T(8,128)S(1)} %get-tuple-element.19.step_ref, s32[8,256]{1,0:T(8,128)S(1)} %get-tuple-element.20.col_ref, ...), custom_call_target="tpu_custom_call" | custom-call | flops 1073741824 | bytes 4194304 | tf_op jit(solution)/shard_map/far_left/pallas_call | solution.py:211
  64.1 4.4 %collective-permute-start.5 = (bf16[256,768]{1,0:T(8,128)(2,1)S(1)}, bf16[256,768]{1,0:T(8,128)(2,1)S(1)}, u32[]{:S(2)}, u32[]{:S(2)}) collective-permute-start(bf16[256,768]{1,0:T(8,128)(2,1)S(1)} %get-tuple-element.32), channel_id=1, source_target_pairs={{0,1},{1,0},{2,3},{3,2},{4,5},{5,4},{6,7},{7,6},{8,9},{9,8},{10,11... | collective-permute-start | bytes 1179656 | tf_op jit(solution)/shard_map/ppermute | solution.py:273
  68.4 2.3 %own_columns.1 = (bf16[256,768]{1,0:T(8,128)(2,1)S(1)}, bf16[256,1152]{1,0:T(8,128)(2,1)}) custom-call(bf16[256,1152]{1,0:T(8,128)(2,1)S(1)} %get-tuple-element.28.grad_ref, bf16[1152,768]{1,0:T(8,128)(2,1)S(1)} %get-tuple-element.29.pick_ref, bf16[1152,1152]{1,0:T(8,128)(2,1)S(1)} %copy-done), custom_call_target="tpu_custom_call" | custom-call | flops 268435456 | bytes 4194304 | tf_op jit(solution)/shard_map/own_columns/pallas_call | solution.py:211
  70.8 1.1 partial.1
  71.9 24.2 %all_to_all.15 = bf16[32,8,2688]{2,1,0:T(8,128)(2,1)S(1)} all-to-all(bf16[32,8,2688]{2,1,0:T(8,128)(2,1)S(1)} %bitcast.11), channel_id=1, replica_groups=mesh['yh'=2,'zh'=4,'z1'=2,'z0'=2,'x'=4,'yl'=2,'c'=2] {'yh','yl','x','z0'}, dimensions={0} | all-to-all | bytes 2752512 | tf_op jit(solution)/shard_map/all_to_all | solution.py:224
  96.3 1.9 %collective-permute-start.7 = (bf16[8,2688]{1,0:T(8,128)(2,1)S(1)}, bf16[8,2688]{1,0:T(8,128)(2,1)S(1)}, u32[]{:S(2)}, u32[]{:S(2)}) collective-permute-start(bf16[8,2688]{1,0:T(8,128)(2,1)S(1)} %reduce_sum.12), channel_id=1, source_target_pairs={{0,32},{32,0},{1,33},{33,1},{2,34},{34,2},{3,35},{35,3},{4,36},{36... | collective-permute-start | bytes 129032 | tf_op jit(solution)/shard_map/ppermute | solution.py:281
  98.2 4.2 %collective-permute-done.7 = bf16[8,2688]{1,0:T(8,128)(2,1)S(1)} collective-permute-done((bf16[8,2688]{1,0:T(8,128)(2,1)S(1)}, bf16[8,2688]{1,0:T(8,128)(2,1)S(1)}, u32[]{:S(2)}, u32[]{:S(2)}) %collective-permute-start.7) | collective-permute-done | bytes 43040 | tf_op jit(solution)/shard_map/ppermute | solution.py:281
  102.4 16.1 %all_to_all.16.came_ref = bf16[4,8,2688]{2,1,0:T(8,128)(2,1)S(1)} all-to-all(bf16[4,8,2688]{2,1,0:T(8,128)(2,1)S(1)} %broadcast_in_dim.10), channel_id=1, replica_groups=mesh['yh'=2,'zh'=4,'z1'=2,'z0'=2,'x'=4,'yl'=2,'c'=2] {'zh'}, dimensions={0} | all-to-all | bytes 344064 | tf_op jit(solution)/shard_map/all_to_all | solution.py:224
  119.3 18.8 %all_to_all.17.square_ref = f32[64,8,128]{2,1,0:T(8,128)S(1)} all-to-all(f32[64,8,128]{2,1,0:T(8,128)S(1)} %get-tuple-element.34), channel_id=1, replica_groups=mesh['yh'=2,'zh'=4,'z1'=2,'z0'=2,'x'=4,'yl'=2,'c'=2] {'yh','yl','x','z0'..., dimensions={0} | all-to-all | bytes 524288 | tf_op jit(solution)/shard_map/all_to_all | solution.py:224
  (19 shorter events, 3.6 us)
Async XLA Ops:
  0.6 27.8 %collective-permute-start.2 = (bf16[256,1152]{1,0:T(8,128)(2,1)}, bf16[256,1152]{1,0:T(8,128)(2,1)S(1)}, u32[]{:S(2)}, u32[]{:S(2)}) collective-permute-start(bf16[256,1152]{1,0:T(8,128)(2,1)} %bitcast.12), channel_id=1, source_target_pairs={{0,4},{4,8},{8,12},{12,0},{16,20},{20,24},{24,28},{28,16},{32,36},... | collective-permute-start | bytes 1769480 | tf_op jit(solution)/shard_map/ppermute | solution.py:53
  4.6 30.1 %collective-permute-start = (bf16[256,1152]{1,0:T(8,128)(2,1)}, bf16[256,1152]{1,0:T(8,128)(2,1)S(1)}, u32[]{:S(2)}, u32[]{:S(2)}) collective-permute-start(bf16[256,1152]{1,0:T(8,128)(2,1)} %bitcast.13), channel_id=1, source_target_pairs={{0,508},{4,0},{8,4},{12,8},{16,12},{20,16},{24,20},{28,24},{32,28}... | collective-permute-start | bytes 1769480 | tf_op jit(solution)/shard_map/ppermute | solution.py:53
  19.6 1.1 copy-start.1
  20.7 1.1 copy-start.2
  21.8 0.9 copy-start.3
  22.7 0.9 copy-start.4
  28.4 26.8 %collective-permute-start.4 = (bf16[256,1152]{1,0:T(8,128)(2,1)S(1)}, bf16[256,1152]{1,0:T(8,128)(2,1)S(1)}, u32[]{:S(2)}, u32[]{:S(2)}) collective-permute-start(bf16[256,1152]{1,0:T(8,128)(2,1)S(1)} %collective-permute-done.2.right_ref), channel_id=1, source_target_pairs={{0,16},{4,500},{8,504},{12,508},{16,32},{20,4},{24,8},{28,12},{32,... | collective-permute-start | bytes 1769480 | tf_op jit(solution)/shard_map/ppermute | solution.py:53
  30.3 29.5 %collective-permute-start.3 = (bf16[256,1152]{1,0:T(8,128)(2,1)S(1)}, bf16[256,1152]{1,0:T(8,128)(2,1)S(1)}, u32[]{:S(2)}, u32[]{:S(2)}) collective-permute-start(bf16[256,1152]{1,0:T(8,128)(2,1)S(1)} %collective-permute-done.2.right_ref), channel_id=1, source_target_pairs={{0,4},{4,8},{8,12},{12,16},{16,20},{20,24},{24,28},{28,32},{32,36}... | collective-permute-start | bytes 1769480 | tf_op jit(solution)/shard_map/ppermute | solution.py:53
  34.6 26.8 %collective-permute-start.1 = (bf16[256,1152]{1,0:T(8,128)(2,1)S(1)}, bf16[256,1152]{1,0:T(8,128)(2,1)S(1)}, u32[]{:S(2)}, u32[]{:S(2)}) collective-permute-start(bf16[256,1152]{1,0:T(8,128)(2,1)S(1)} %collective-permute-done.left_ref), channel_id=1, source_target_pairs={{0,508},{4,0},{8,20},{12,8},{16,12},{20,16},{24,36},{28,24},{32,28... | collective-permute-start | bytes 1769480 | tf_op jit(solution)/shard_map/ppermute | solution.py:53
  43.8 27.0 %collective-permute-start.6 = (bf16[1152,256]{1,0:T(8,128)(2,1)S(1)}, bf16[1152,256]{1,0:T(8,128)(2,1)S(1)}, u32[]{:S(2)}, u32[]{:S(2)}) collective-permute-start(bf16[1152,256]{1,0:T(8,128)(2,1)S(1)} %get-tuple-element.33.turned_ref), channel_id=1, source_target_pairs={{0,1},{1,0},{2,3},{3,2},{4,5},{5,4},{6,7},{7,6},{8,9},{9,8},{10,11... | collective-permute-start | bytes 1769480 | tf_op jit(solution)/shard_map/ppermute | solution.py:261
  61.5 7.0 %copy-start = (bf16[1152,1152]{1,0:T(8,128)(2,1)S(1)}, bf16[1152,1152]{1,0:T(8,128)(2,1)}, u32[]{:S(2)}) copy-start(bf16[1152,1152]{1,0:T(8,128)(2,1)} %proj_ref.1) | copy-start | bytes 7962628
  64.1 6.7 %collective-permute-start.5 = (bf16[256,768]{1,0:T(8,128)(2,1)S(1)}, bf16[256,768]{1,0:T(8,128)(2,1)S(1)}, u32[]{:S(2)}, u32[]{:S(2)}) collective-permute-start(bf16[256,768]{1,0:T(8,128)(2,1)S(1)} %get-tuple-element.32), channel_id=1, source_target_pairs={{0,1},{1,0},{2,3},{3,2},{4,5},{5,4},{6,7},{7,6},{8,9},{9,8},{10,11... | collective-permute-start | bytes 1179656 | tf_op jit(solution)/shard_map/ppermute | solution.py:273
  96.3 6.1 %collective-permute-start.7 = (bf16[8,2688]{1,0:T(8,128)(2,1)S(1)}, bf16[8,2688]{1,0:T(8,128)(2,1)S(1)}, u32[]{:S(2)}, u32[]{:S(2)}) collective-permute-start(bf16[8,2688]{1,0:T(8,128)(2,1)S(1)} %reduce_sum.12), channel_id=1, source_target_pairs={{0,32},{32,0},{1,33},{33,1},{2,34},{34,2},{3,35},{35,3},{4,36},{36... | collective-permute-start | bytes 129032 | tf_op jit(solution)/shard_map/ppermute | solution.py:281

commit v10 on v8

--- a/solution.py
+++ b/solution.py
@@ -277,9 +277,7 @@
         partial_kernel, (own, columns, turned, opposite), (((2, 2, SHARDS // 2, WIDTH), BF16),), 1 << 30, 32, "partial"
     )
     rows = total(traded(both.reshape(32, 8, WIDTH), NEAR)).astype(BF16)
-    near = lax.ppermute(rows, "z1", swap)
-    rows = (rows.astype(F32) + near.astype(F32)).astype(BF16)
-    rows = traded(jnp.broadcast_to(rows[None], (4, 8, WIDTH)), "zh")
+    rows = traded(jnp.broadcast_to(rows[None], (8, 8, WIDTH)), ("zh", "z1"))
     block, square = call(block_kernel, (place, rows), (((RB, CB), F32), ((64, 8, 128), F32)), 1 << 20, 16, "block")
     square = traded(square, NEAR + ("c",))
     (block,) = call(clip_kernel, (square, block), (((RB, CB), F32),), 1 << 20, 16, "clip")

time: 139 us -> 141 us (1.014)
  blocking collectives: 61.8 us -> 69.5 us
  waiting for transfers between devices: 4.22 us -> 0.02 us
  starting transfers between devices: 50.4 us -> 48.5 us
    all_to_all x3, blocking collectives: 61.8 us -> 69.5 us  [traded(): return lax.all_to_all(value, axis, split_axis=0, concat_axis=0)]
    ppermute x1 -> x0, waiting for transfers between devices: 4.2 us -> none  [local(): near = lax.ppermute(rows, 'z1', swap)]
    ppermute x1 -> x0, starting transfers between devices: 1.92 us -> none  [local(): near = lax.ppermute(rows, 'z1', swap)]
  transfers between devices with their start and end apart: 8 -> 7, of which waited for: 1 -> 0; matrix products, arithmetic and copies ran while one was open for 0% -> 0% of each run, Pallas kernels for 13% -> 13%
where the time goes in v10:
time: 141 us; the launch traced here: 140 us
  blocking collectives  69.5 us (49%)
  starting transfers between devices  48.5 us (34%)
  Pallas kernels  20.2 us (14%)
    all_to_all x3, blocking collectives, traded(): return lax.all_to_all(value, axis, split_axis=0, concat_axis=0)  69.5 us
    ppermute x5, starting transfers between devices, shifted(): return lax.ppermute(value, DP, pairs)  40.5 us
    pallas_call x10, Pallas kernels, call(): pl.pallas_call(kernel, out_shape=[jax.ShapeDtypeStruct(shape, dtype) for...  20.2 us
    ppermute x1, starting transfers between devices, local(): opposite = lax.ppermute(turned, 'c', swap)  4.84 us
    ppermute x1, starting transfers between devices, local(): columns = lax.ppermute(columns, 'c', swap)  3.08 us
  transfers between devices with their start and end apart: 7, of which 0 were waited for; matrix products, arithmetic and copies ran while one was open for 0% of the time, Pallas kernels for 13%

profile of v10, /device:TPU:1, one launch (start us, length us, event | category | flops | bytes accessed | tf_op | source)
XLA Modules:
  0.0 140.4 jit_solution(4677091233185726277)
XLA Ops:
  0.6 4.0 %collective-permute-start.2 = (bf16[256,1152]{1,0:T(8,128)(2,1)}, bf16[256,1152]{1,0:T(8,128)(2,1)S(1)}, u32[]{:S(2)}, u32[]{:S(2)}) collective-permute-start(bf16[256,1152]{1,0:T(8,128)(2,1)} %bitcast.12), channel_id=1, source_target_pairs={{0,4},{4,8},{8,12},{12,0},{16,20},{20,24},{24,28},{28,16},{32,36},... | collective-permute-start | bytes 1769480 | tf_op jit(solution)/shard_map/ppermute | solution.py:53
  4.6 14.9 %collective-permute-start = (bf16[256,1152]{1,0:T(8,128)(2,1)}, bf16[256,1152]{1,0:T(8,128)(2,1)S(1)}, u32[]{:S(2)}, u32[]{:S(2)}) collective-permute-start(bf16[256,1152]{1,0:T(8,128)(2,1)} %bitcast.13), channel_id=1, source_target_pairs={{0,508},{4,0},{8,4},{12,8},{16,12},{20,16},{24,20},{28,24},{32,28}... | collective-permute-start | bytes 1769480 | tf_op jit(solution)/shard_map/ppermute | solution.py:53
  19.5 3.0 %collective-permute-start.4 = (bf16[256,1152]{1,0:T(8,128)(2,1)S(1)}, bf16[256,1152]{1,0:T(8,128)(2,1)S(1)}, u32[]{:S(2)}, u32[]{:S(2)}) collective-permute-start(bf16[256,1152]{1,0:T(8,128)(2,1)S(1)} %collective-permute-done.2.right_ref), channel_id=1, source_target_pairs={{0,16},{4,500},{8,504},{12,508},{16,32},{20,4},{24,8},{28,12},{32,... | collective-permute-start | bytes 1769480 | tf_op jit(solution)/shard_map/ppermute | solution.py:53
  22.5 12.1 %collective-permute-start.3 = (bf16[256,1152]{1,0:T(8,128)(2,1)S(1)}, bf16[256,1152]{1,0:T(8,128)(2,1)S(1)}, u32[]{:S(2)}, u32[]{:S(2)}) collective-permute-start(bf16[256,1152]{1,0:T(8,128)(2,1)S(1)} %collective-permute-done.2.right_ref), channel_id=1, source_target_pairs={{0,4},{4,8},{8,12},{12,16},{16,20},{20,24},{24,28},{28,32},{32,36}... | collective-permute-start | bytes 1769480 | tf_op jit(solution)/shard_map/ppermute | solution.py:53
  34.6 6.6 %collective-permute-start.1 = (bf16[256,1152]{1,0:T(8,128)(2,1)S(1)}, bf16[256,1152]{1,0:T(8,128)(2,1)S(1)}, u32[]{:S(2)}, u32[]{:S(2)}) collective-permute-start(bf16[256,1152]{1,0:T(8,128)(2,1)S(1)} %collective-permute-done.left_ref), channel_id=1, source_target_pairs={{0,508},{4,0},{8,20},{12,8},{16,12},{20,16},{24,36},{28,24},{32,28... | collective-permute-start | bytes 1769480 | tf_op jit(solution)/shard_map/ppermute | solution.py:53
  41.3 0.1 stack.31.place_ref
  41.3 1.1 copy-done.2
  42.4 2.4 %order.1 = (bf16[1152,256]{1,0:T(8,128)(2,1)S(1)}, bf16[1152,768]{1,0:T(8,128)(2,1)S(1)}, bf16[1152,768]{1,0:T(8,128)(2,1)S(1)}) custom-call(s32[7]{0:T(128)S(1)} %stack.31.place_ref, bf16[256,1152]{1,0:T(8,128)(2,1)S(1)} %bitcast.15), custom_call_target="tpu_custom_call" | custom-call | flops 1073741824 | bytes 4194304 | tf_op jit(solution)/shard_map/order/pallas_call | solution.py:211
  44.8 4.8 %collective-permute-start.6 = (bf16[1152,256]{1,0:T(8,128)(2,1)S(1)}, bf16[1152,256]{1,0:T(8,128)(2,1)S(1)}, u32[]{:S(2)}, u32[]{:S(2)}) collective-permute-start(bf16[1152,256]{1,0:T(8,128)(2,1)S(1)} %get-tuple-element.29.turned_ref), channel_id=1, source_target_pairs={{0,1},{1,0},{2,3},{3,2},{4,5},{5,4},{6,7},{7,6},{8,9},{9,8},{10,11... | collective-permute-start | bytes 1769480 | tf_op jit(solution)/shard_map/ppermute | solution.py:260
  49.7 4.8 %hidden_and_own.1 = (f32[256,1152]{1,0:T(8,128)S(1)}, f32[256,128]{1,0:T(8,128)S(1)}, bf16[256,1152]{1,0:T(8,128)(2,1)S(1)}, f32[256,1152]{1,0:T(8,128)S(1)}, s3...) custom-call(s32[7]{0:T(128)S(1)} %stack.31.place_ref, bf16[256,1152]{1,0:T(8,128)(2,1)S(1)} %bitcast.16, ...), custom_call_target="tpu_custom_call" | custom-call | flops 1073741824 | bytes 4194304 | tf_op jit(solution)/shard_map/hidden_and_own/pallas_call | solution.py:211
  54.5 2.3 %near_pairs.1.acc_ref = f32[256,1152]{1,0:T(8,128)S(1)} custom-call(s32[7]{0:T(128)S(1)} %stack.31.place_ref, bf16[256,1152]{1,0:T(8,128)(2,1)S(1)} %collective-permute-done.2.right_ref, bf16[256,1152]{1,0:T(8,128)(2,1)S(1)} %collective-permute-done.left_ref, s32[8,256]{1,0:T(8,128)S(1)} %get-tuple-element.17.step_ref, ...), custom_call_target="tpu_custom_call" | custom-call | flops 1073741824 | bytes 4194304 | tf_op jit(solution)/shard_map/near_pairs/pallas_call | solution.py:211
  56.8 1.6 %far_across.1.acc_ref = f32[256,1152]{1,0:T(8,128)S(1)} custom-call(s32[7]{0:T(128)S(1)} %stack.31.place_ref, bf16[256,1152]{1,0:T(8,128)(2,1)S(1)} %collective-permute-done.4.image_ref, s32[8,256]{1,0:T(8,128)S(1)} %get-tuple-element.17.step_ref, s32[8,256]{1,0:T(8,128)S(1)} %get-tuple-element.18.col_ref, bf16[256,1152]{1,0:T(8,128)(2,1)S(1)} %get-tuple-element.19.text_ref, ...), custom_call_target="tpu_custom_call" | custom-call | flops 268435456 | bytes 4194304 | tf_op jit(solution)/shard_map/far_across/pallas_call | solution.py:211
  58.5 1.6 %far_right.1.acc_ref = f32[256,1152]{1,0:T(8,128)S(1)} custom-call(s32[7]{0:T(128)S(1)} %stack.31.place_ref, bf16[256,1152]{1,0:T(8,128)(2,1)S(1)} %collective-permute-done.3.image_ref, s32[8,256]{1,0:T(8,128)S(1)} %get-tuple-element.17.step_ref, s32[8,256]{1,0:T(8,128)S(1)} %get-tuple-element.18.col_ref, bf16[256,1152]{1,0:T(8,128)(2,1)S(1)} %get-tuple-element.19.text_ref, ...), custom_call_target="tpu_custom_call" | custom-call | flops 268435456 | bytes 4194304 | tf_op jit(solution)/shard_map/far_right/pallas_call | solution.py:211
  60.1 0.0 copy-start
  60.1 2.6 %far_left.1 = (bf16[256,1152]{1,0:T(8,128)(2,1)S(1)}, bf16[256,768]{1,0:T(8,128)(2,1)S(1)}) custom-call(s32[7]{0:T(128)S(1)} %stack.31.place_ref, bf16[256,1152]{1,0:T(8,128)(2,1)S(1)} %collective-permute-done.1.left_ref, s32[8,256]{1,0:T(8,128)S(1)} %get-tuple-element.17.step_ref, s32[8,256]{1,0:T(8,128)S(1)} %get-tuple-element.18.col_ref, ...), custom_call_target="tpu_custom_call" | custom-call | flops 1073741824 | bytes 4194304 | tf_op jit(solution)/shard_map/far_left/pallas_call | solution.py:211
  62.7 3.1 %collective-permute-start.5 = (bf16[256,768]{1,0:T(8,128)(2,1)S(1)}, bf16[256,768]{1,0:T(8,128)(2,1)S(1)}, u32[]{:S(2)}, u32[]{:S(2)}) collective-permute-start(bf16[256,768]{1,0:T(8,128)(2,1)S(1)} %get-tuple-element.28), channel_id=1, source_target_pairs={{0,1},{1,0},{2,3},{3,2},{4,5},{5,4},{6,7},{7,6},{8,9},{9,8},{10,11... | collective-permute-start | bytes 1179656 | tf_op jit(solution)/shard_map/ppermute | solution.py:272
  65.8 2.3 %own_columns.1 = (bf16[256,768]{1,0:T(8,128)(2,1)S(1)}, bf16[256,1152]{1,0:T(8,128)(2,1)}) custom-call(bf16[256,1152]{1,0:T(8,128)(2,1)S(1)} %get-tuple-element.24.grad_ref, bf16[1152,768]{1,0:T(8,128)(2,1)S(1)} %get-tuple-element.25.pick_ref, bf16[1152,1152]{1,0:T(8,128)(2,1)S(1)} %copy-done), custom_call_target="tpu_custom_call" | custom-call | flops 268435456 | bytes 4194304 | tf_op jit(solution)/shard_map/own_columns/pallas_call | solution.py:211
  68.1 1.1 partial.1
  69.2 24.2 %all_to_all.15 = bf16[32,8,2688]{2,1,0:T(8,128)(2,1)S(1)} all-to-all(bf16[32,8,2688]{2,1,0:T(8,128)(2,1)S(1)} %bitcast.11), channel_id=1, replica_groups=mesh['yh'=2,'zh'=4,'z1'=2,'z0'=2,'x'=4,'yl'=2,'c'=2] {'yh','yl','x','z0'}, dimensions={0} | all-to-all | bytes 2752512 | tf_op jit(solution)/shard_map/all_to_all | solution.py:224
  93.4 0.2 reduce_sum.12
  93.7 25.0 %all_to_all.16.came_ref = bf16[8,8,2688]{2,1,0:T(8,128)(2,1)S(1)} all-to-all(bf16[8,8,2688]{2,1,0:T(8,128)(2,1)S(1)} %broadcast_in_dim.10), channel_id=1, replica_groups=mesh['yh'=2,'zh'=4,'z1'=2,'z0'=2,'x'=4,'yl'=2,'c'=2] {'zh','z1'}, dimensions={0} | all-to-all | bytes 688128 | tf_op jit(solution)/shard_map/all_to_all | solution.py:224
  118.7 0.7 block.1
  119.4 20.2 %all_to_all.17.square_ref = f32[64,8,128]{2,1,0:T(8,128)S(1)} all-to-all(f32[64,8,128]{2,1,0:T(8,128)S(1)} %get-tuple-element.30), channel_id=1, replica_groups=mesh['yh'=2,'zh'=4,'z1'=2,'z0'=2,'x'=4,'yl'=2,'c'=2] {'yh','yl','x','z0'..., dimensions={0} | all-to-all | bytes 524288 | tf_op jit(solution)/shard_map/all_to_all | solution.py:224
  139.6 0.8 clip.1
  (18 shorter events, 0.1 us)
Async XLA Ops:
  0.6 18.9 %collective-permute-start.2 = (bf16[256,1152]{1,0:T(8,128)(2,1)}, bf16[256,1152]{1,0:T(8,128)(2,1)S(1)}, u32[]{:S(2)}, u32[]{:S(2)}) collective-permute-start(bf16[256,1152]{1,0:T(8,128)(2,1)} %bitcast.12), channel_id=1, source_target_pairs={{0,4},{4,8},{8,12},{12,0},{16,20},{20,24},{24,28},{28,16},{32,36},... | collective-permute-start | bytes 1769480 | tf_op jit(solution)/shard_map/ppermute | solution.py:53
  4.6 30.1 %collective-permute-start = (bf16[256,1152]{1,0:T(8,128)(2,1)}, bf16[256,1152]{1,0:T(8,128)(2,1)S(1)}, u32[]{:S(2)}, u32[]{:S(2)}) collective-permute-start(bf16[256,1152]{1,0:T(8,128)(2,1)} %bitcast.13), channel_id=1, source_target_pairs={{0,508},{4,0},{8,4},{12,8},{16,12},{20,16},{24,20},{28,24},{32,28}... | collective-permute-start | bytes 1769480 | tf_op jit(solution)/shard_map/ppermute | solution.py:53
  19.5 37.3 %collective-permute-start.4 = (bf16[256,1152]{1,0:T(8,128)(2,1)S(1)}, bf16[256,1152]{1,0:T(8,128)(2,1)S(1)}, u32[]{:S(2)}, u32[]{:S(2)}) collective-permute-start(bf16[256,1152]{1,0:T(8,128)(2,1)S(1)} %collective-permute-done.2.right_ref), channel_id=1, source_target_pairs={{0,16},{4,500},{8,504},{12,508},{16,32},{20,4},{24,8},{28,12},{32,... | collective-permute-start | bytes 1769480 | tf_op jit(solution)/shard_map/ppermute | solution.py:53
  22.5 35.9 %collective-permute-start.3 = (bf16[256,1152]{1,0:T(8,128)(2,1)S(1)}, bf16[256,1152]{1,0:T(8,128)(2,1)S(1)}, u32[]{:S(2)}, u32[]{:S(2)}) collective-permute-start(bf16[256,1152]{1,0:T(8,128)(2,1)S(1)} %collective-permute-done.2.right_ref), channel_id=1, source_target_pairs={{0,4},{4,8},{8,12},{12,16},{16,20},{20,24},{24,28},{28,32},{32,36}... | collective-permute-start | bytes 1769480 | tf_op jit(solution)/shard_map/ppermute | solution.py:53
  34.6 25.4 %collective-permute-start.1 = (bf16[256,1152]{1,0:T(8,128)(2,1)S(1)}, bf16[256,1152]{1,0:T(8,128)(2,1)S(1)}, u32[]{:S(2)}, u32[]{:S(2)}) collective-permute-start(bf16[256,1152]{1,0:T(8,128)(2,1)S(1)} %collective-permute-done.left_ref), channel_id=1, source_target_pairs={{0,508},{4,0},{8,20},{12,8},{16,12},{20,16},{24,36},{28,24},{32,28... | collective-permute-start | bytes 1769480 | tf_op jit(solution)/shard_map/ppermute | solution.py:53
  41.3 1.1 copy-start.2
  42.4 7.3 %copy-start.1 = (bf16[1,256,1152]{2,1,0:T(8,128)(2,1)S(1)}, bf16[1,256,1152]{2,1,0:T(8,128)(2,1)}, u32[]{:S(2)}) copy-start(bf16[1,256,1152]{2,1,0:T(8,128)(2,1)} %param.5) | copy-start | bytes 1769476
  42.4 7.3 %copy-start.3 = (bf16[1,256,1152]{2,1,0:T(8,128)(2,1)S(1)}, bf16[1,256,1152]{2,1,0:T(8,128)(2,1)}, u32[]{:S(2)}) copy-start(bf16[1,256,1152]{2,1,0:T(8,128)(2,1)} %param.6) | copy-start | bytes 1769476
  42.4 7.3 %copy-start.4 = (s32[1,32768]{1,0:T(1,128)S(1)}, s32[1,32768]{1,0:T(1,128)}, u32[]{:S(2)}) copy-start(s32[1,32768]{1,0:T(1,128)} %step_hbm.1) | copy-start | bytes 393220
  42.4 7.3 %copy-start.5 = (s32[1,32768]{1,0:T(1,128)S(1)}, s32[1,32768]{1,0:T(1,128)}, u32[]{:S(2)}) copy-start(s32[1,32768]{1,0:T(1,128)} %col_hbm.1) | copy-start | bytes 393220
  44.8 23.3 %collective-permute-start.6 = (bf16[1152,256]{1,0:T(8,128)(2,1)S(1)}, bf16[1152,256]{1,0:T(8,128)(2,1)S(1)}, u32[]{:S(2)}, u32[]{:S(2)}) collective-permute-start(bf16[1152,256]{1,0:T(8,128)(2,1)S(1)} %get-tuple-element.29.turned_ref), channel_id=1, source_target_pairs={{0,1},{1,0},{2,3},{3,2},{4,5},{5,4},{6,7},{7,6},{8,9},{9,8},{10,11... | collective-permute-start | bytes 1769480 | tf_op jit(solution)/shard_map/ppermute | solution.py:260
  60.1 5.7 %copy-start = (bf16[1152,1152]{1,0:T(8,128)(2,1)S(1)}, bf16[1152,1152]{1,0:T(8,128)(2,1)}, u32[]{:S(2)}) copy-start(bf16[1152,1152]{1,0:T(8,128)(2,1)} %proj_ref.1) | copy-start | bytes 7962628
  62.7 5.4 %collective-permute-start.5 = (bf16[256,768]{1,0:T(8,128)(2,1)S(1)}, bf16[256,768]{1,0:T(8,128)(2,1)S(1)}, u32[]{:S(2)}, u32[]{:S(2)}) collective-permute-start(bf16[256,768]{1,0:T(8,128)(2,1)S(1)} %get-tuple-element.28), channel_id=1, source_target_pairs={{0,1},{1,0},{2,3},{3,2},{4,5},{5,4},{6,7},{7,6},{8,9},{9,8},{10,11... | collective-permute-start | bytes 1179656 | tf_op jit(solution)/shard_map/ppermute | solution.py:272

commit v11 on v8

--- a/solution.py
+++ b/solution.py
@@ -188,8 +188,6 @@
     rows = jnp.sum(came_ref[...].astype(F32), axis=0)
     sums = jnp.sum(rows * rows, axis=0, keepdims=True)
     square = functools.reduce(jnp.add, [sums[:, t * 128 : (t + 1) * 128] for t in range(WIDTH // 128)])
-    lines = lax.broadcasted_iota(jnp.int32, (8, 128), 0)
-    square = jnp.where(lines == 0, jnp.broadcast_to(square, (8, 128)), 0.0)
     square_ref[...] = jnp.broadcast_to(square[None], square_ref.shape)
     mine = lax.broadcasted_iota(jnp.int32, rows.shape, 0) == place_ref[6]
     own = jnp.sum(jnp.where(mine, rows, 0.0), axis=0, keepdims=True)
@@ -280,7 +278,7 @@
     near = lax.ppermute(rows, "z1", swap)
     rows = (rows.astype(F32) + near.astype(F32)).astype(BF16)
     rows = traded(jnp.broadcast_to(rows[None], (4, 8, WIDTH)), "zh")
-    block, square = call(block_kernel, (place, rows), (((RB, CB), F32), ((64, 8, 128), F32)), 1 << 20, 16, "block")
+    block, square = call(block_kernel, (place, rows), (((RB, CB), F32), ((64, 1, 128), F32)), 1 << 20, 16, "block")
     square = traded(square, NEAR + ("c",))
     (block,) = call(clip_kernel, (square, block), (((RB, CB), F32),), 1 << 20, 16, "clip")
     return (grad_text[None], block)

time: 139 us -> 137 us (0.986)
  blocking collectives: 61.8 us -> 59.6 us
    all_to_all x3, blocking collectives: 61.8 us -> 59.6 us  [traded(): return lax.all_to_all(value, axis, split_axis=0, concat_axis=0)]
where the time goes in v11:
time: 137 us
  blocking collectives  59.6 us (44%)
  starting transfers between devices  50.4 us (37%)
  Pallas kernels  20.2 us (15%)
  waiting for transfers between devices  4.22 us (3%)
    all_to_all x3, blocking collectives, traded(): return lax.all_to_all(value, axis, split_axis=0, concat_axis=0)  59.6 us
    ppermute x5, starting transfers between devices, shifted(): return lax.ppermute(value, DP, pairs)  40.5 us
    pallas_call x10, Pallas kernels, call(): pl.pallas_call(kernel, out_shape=[jax.ShapeDtypeStruct(shape, dtype) for...  20.2 us
    ppermute x1, starting transfers between devices, local(): opposite = lax.ppermute(turned, 'c', swap)  4.84 us
    ppermute x1, waiting for transfers between devices, local(): near = lax.ppermute(rows, 'z1', swap)  4.2 us
    ppermute x1, starting transfers between devices, local(): columns = lax.ppermute(columns, 'c', swap)  3.08 us
  transfers between devices with their start and end apart: 8, of which 1 were waited for; matrix products, arithmetic and copies ran while one was open for 0% of the time, Pallas kernels for 13%

profile of v11, /device:TPU:1, one launch (start us, length us, event | category | flops | bytes accessed | tf_op | source)
XLA Modules:
  0.0 136.7 jit_solution(15097702166499816129)
XLA Ops:
  0.6 4.0 %collective-permute-start.2 = (bf16[256,1152]{1,0:T(8,128)(2,1)}, bf16[256,1152]{1,0:T(8,128)(2,1)S(1)}, u32[]{:S(2)}, u32[]{:S(2)}) collective-permute-start(bf16[256,1152]{1,0:T(8,128)(2,1)} %bitcast.12), channel_id=1, source_target_pairs={{0,4},{4,8},{8,12},{12,0},{16,20},{20,24},{24,28},{28,16},{32,36},... | collective-permute-start | bytes 1769480 | tf_op jit(solution)/shard_map/ppermute | solution.py:53
  4.6 14.9 %collective-permute-start = (bf16[256,1152]{1,0:T(8,128)(2,1)}, bf16[256,1152]{1,0:T(8,128)(2,1)S(1)}, u32[]{:S(2)}, u32[]{:S(2)}) collective-permute-start(bf16[256,1152]{1,0:T(8,128)(2,1)} %bitcast.13), channel_id=1, source_target_pairs={{0,508},{4,0},{8,4},{12,8},{16,12},{20,16},{24,20},{28,24},{32,28}... | collective-permute-start | bytes 1769480 | tf_op jit(solution)/shard_map/ppermute | solution.py:53
  19.5 3.0 %collective-permute-start.4 = (bf16[256,1152]{1,0:T(8,128)(2,1)S(1)}, bf16[256,1152]{1,0:T(8,128)(2,1)S(1)}, u32[]{:S(2)}, u32[]{:S(2)}) collective-permute-start(bf16[256,1152]{1,0:T(8,128)(2,1)S(1)} %collective-permute-done.2.right_ref), channel_id=1, source_target_pairs={{0,16},{4,500},{8,504},{12,508},{16,32},{20,4},{24,8},{28,12},{32,... | collective-permute-start | bytes 1769480 | tf_op jit(solution)/shard_map/ppermute | solution.py:53
  22.5 12.1 %collective-permute-start.3 = (bf16[256,1152]{1,0:T(8,128)(2,1)S(1)}, bf16[256,1152]{1,0:T(8,128)(2,1)S(1)}, u32[]{:S(2)}, u32[]{:S(2)}) collective-permute-start(bf16[256,1152]{1,0:T(8,128)(2,1)S(1)} %collective-permute-done.2.right_ref), channel_id=1, source_target_pairs={{0,4},{4,8},{8,12},{12,16},{16,20},{20,24},{24,28},{28,32},{32,36}... | collective-permute-start | bytes 1769480 | tf_op jit(solution)/shard_map/ppermute | solution.py:53
  34.6 6.6 %collective-permute-start.1 = (bf16[256,1152]{1,0:T(8,128)(2,1)S(1)}, bf16[256,1152]{1,0:T(8,128)(2,1)S(1)}, u32[]{:S(2)}, u32[]{:S(2)}) collective-permute-start(bf16[256,1152]{1,0:T(8,128)(2,1)S(1)} %collective-permute-done.left_ref), channel_id=1, source_target_pairs={{0,508},{4,0},{8,20},{12,8},{16,12},{20,16},{24,36},{28,24},{32,28... | collective-permute-start | bytes 1769480 | tf_op jit(solution)/shard_map/ppermute | solution.py:53
  41.3 1.1 copy-done.2
  42.4 2.4 %order.1 = (bf16[1152,256]{1,0:T(8,128)(2,1)S(1)}, bf16[1152,768]{1,0:T(8,128)(2,1)S(1)}, bf16[1152,768]{1,0:T(8,128)(2,1)S(1)}) custom-call(s32[7]{0:T(128)S(1)} %stack.31.place_ref, bf16[256,1152]{1,0:T(8,128)(2,1)S(1)} %bitcast.15), custom_call_target="tpu_custom_call" | custom-call | flops 1073741824 | bytes 4194304 | tf_op jit(solution)/shard_map/order/pallas_call | solution.py:209
  44.8 4.8 %collective-permute-start.6 = (bf16[1152,256]{1,0:T(8,128)(2,1)S(1)}, bf16[1152,256]{1,0:T(8,128)(2,1)S(1)}, u32[]{:S(2)}, u32[]{:S(2)}) collective-permute-start(bf16[1152,256]{1,0:T(8,128)(2,1)S(1)} %get-tuple-element.29.turned_ref), channel_id=1, source_target_pairs={{0,1},{1,0},{2,3},{3,2},{4,5},{5,4},{6,7},{7,6},{8,9},{9,8},{10,11... | collective-permute-start | bytes 1769480 | tf_op jit(solution)/shard_map/ppermute | solution.py:258
  49.7 4.8 %hidden_and_own.1 = (f32[256,1152]{1,0:T(8,128)S(1)}, f32[256,128]{1,0:T(8,128)S(1)}, bf16[256,1152]{1,0:T(8,128)(2,1)S(1)}, f32[256,1152]{1,0:T(8,128)S(1)}, s3...) custom-call(s32[7]{0:T(128)S(1)} %stack.31.place_ref, bf16[256,1152]{1,0:T(8,128)(2,1)S(1)} %bitcast.16, ...), custom_call_target="tpu_custom_call" | custom-call | flops 1073741824 | bytes 4194304 | tf_op jit(solution)/shard_map/hidden_and_own/pallas_call | solution.py:209
  54.5 2.3 %near_pairs.1.acc_ref = f32[256,1152]{1,0:T(8,128)S(1)} custom-call(s32[7]{0:T(128)S(1)} %stack.31.place_ref, bf16[256,1152]{1,0:T(8,128)(2,1)S(1)} %collective-permute-done.2.right_ref, bf16[256,1152]{1,0:T(8,128)(2,1)S(1)} %collective-permute-done.left_ref, s32[8,256]{1,0:T(8,128)S(1)} %get-tuple-element.17.step_ref, ...), custom_call_target="tpu_custom_call" | custom-call | flops 1073741824 | bytes 4194304 | tf_op jit(solution)/shard_map/near_pairs/pallas_call | solution.py:209
  56.8 1.6 %far_across.1.acc_ref = f32[256,1152]{1,0:T(8,128)S(1)} custom-call(s32[7]{0:T(128)S(1)} %stack.31.place_ref, bf16[256,1152]{1,0:T(8,128)(2,1)S(1)} %collective-permute-done.4.image_ref, s32[8,256]{1,0:T(8,128)S(1)} %get-tuple-element.17.step_ref, s32[8,256]{1,0:T(8,128)S(1)} %get-tuple-element.18.col_ref, bf16[256,1152]{1,0:T(8,128)(2,1)S(1)} %get-tuple-element.19.text_ref, ...), custom_call_target="tpu_custom_call" | custom-call | flops 268435456 | bytes 4194304 | tf_op jit(solution)/shard_map/far_across/pallas_call | solution.py:209
  58.5 1.6 %far_right.1.acc_ref = f32[256,1152]{1,0:T(8,128)S(1)} custom-call(s32[7]{0:T(128)S(1)} %stack.31.place_ref, bf16[256,1152]{1,0:T(8,128)(2,1)S(1)} %collective-permute-done.3.image_ref, s32[8,256]{1,0:T(8,128)S(1)} %get-tuple-element.17.step_ref, s32[8,256]{1,0:T(8,128)S(1)} %get-tuple-element.18.col_ref, bf16[256,1152]{1,0:T(8,128)(2,1)S(1)} %get-tuple-element.19.text_ref, ...), custom_call_target="tpu_custom_call" | custom-call | flops 268435456 | bytes 4194304 | tf_op jit(solution)/shard_map/far_right/pallas_call | solution.py:209
  60.1 2.6 %far_left.1 = (bf16[256,1152]{1,0:T(8,128)(2,1)S(1)}, bf16[256,768]{1,0:T(8,128)(2,1)S(1)}) custom-call(s32[7]{0:T(128)S(1)} %stack.31.place_ref, bf16[256,1152]{1,0:T(8,128)(2,1)S(1)} %collective-permute-done.1.left_ref, s32[8,256]{1,0:T(8,128)S(1)} %get-tuple-element.17.step_ref, s32[8,256]{1,0:T(8,128)S(1)} %get-tuple-element.18.col_ref, ...), custom_call_target="tpu_custom_call" | custom-call | flops 1073741824 | bytes 4194304 | tf_op jit(solution)/shard_map/far_left/pallas_call | solution.py:209
  62.7 3.1 %collective-permute-start.5 = (bf16[256,768]{1,0:T(8,128)(2,1)S(1)}, bf16[256,768]{1,0:T(8,128)(2,1)S(1)}, u32[]{:S(2)}, u32[]{:S(2)}) collective-permute-start(bf16[256,768]{1,0:T(8,128)(2,1)S(1)} %get-tuple-element.28), channel_id=1, source_target_pairs={{0,1},{1,0},{2,3},{3,2},{4,5},{5,4},{6,7},{7,6},{8,9},{9,8},{10,11... | collective-permute-start | bytes 1179656 | tf_op jit(solution)/shard_map/ppermute | solution.py:270
  65.8 2.3 %own_columns.1 = (bf16[256,768]{1,0:T(8,128)(2,1)S(1)}, bf16[256,1152]{1,0:T(8,128)(2,1)}) custom-call(bf16[256,1152]{1,0:T(8,128)(2,1)S(1)} %get-tuple-element.24.grad_ref, bf16[1152,768]{1,0:T(8,128)(2,1)S(1)} %get-tuple-element.25.pick_ref, bf16[1152,1152]{1,0:T(8,128)(2,1)S(1)} %copy-done), custom_call_target="tpu_custom_call" | custom-call | flops 268435456 | bytes 4194304 | tf_op jit(solution)/shard_map/own_columns/pallas_call | solution.py:209
  68.1 1.1 partial.1
  69.2 24.2 %all_to_all.15 = bf16[32,8,2688]{2,1,0:T(8,128)(2,1)S(1)} all-to-all(bf16[32,8,2688]{2,1,0:T(8,128)(2,1)S(1)} %bitcast.11), channel_id=1, replica_groups=mesh['yh'=2,'zh'=4,'z1'=2,'z0'=2,'x'=4,'yl'=2,'c'=2] {'yh','yl','x','z0'}, dimensions={0} | all-to-all | bytes 2752512 | tf_op jit(solution)/shard_map/all_to_all | solution.py:222
  93.4 0.2 reduce_sum.12
  93.6 1.9 %collective-permute-start.7 = (bf16[8,2688]{1,0:T(8,128)(2,1)S(1)}, bf16[8,2688]{1,0:T(8,128)(2,1)S(1)}, u32[]{:S(2)}, u32[]{:S(2)}) collective-permute-start(bf16[8,2688]{1,0:T(8,128)(2,1)S(1)} %reduce_sum.12), channel_id=1, source_target_pairs={{0,32},{32,0},{1,33},{33,1},{2,34},{34,2},{3,35},{35,3},{4,36},{36... | collective-permute-start | bytes 129032 | tf_op jit(solution)/shard_map/ppermute | solution.py:278
  95.5 4.2 %collective-permute-done.7 = bf16[8,2688]{1,0:T(8,128)(2,1)S(1)} collective-permute-done((bf16[8,2688]{1,0:T(8,128)(2,1)S(1)}, bf16[8,2688]{1,0:T(8,128)(2,1)S(1)}, u32[]{:S(2)}, u32[]{:S(2)}) %collective-permute-start.7) | collective-permute-done | bytes 43040 | tf_op jit(solution)/shard_map/ppermute | solution.py:278
  99.8 18.8 %all_to_all.16.came_ref = bf16[4,8,2688]{2,1,0:T(8,128)(2,1)S(1)} all-to-all(bf16[4,8,2688]{2,1,0:T(8,128)(2,1)S(1)} %broadcast_in_dim.10), channel_id=1, replica_groups=mesh['yh'=2,'zh'=4,'z1'=2,'z0'=2,'x'=4,'yl'=2,'c'=2] {'zh'}, dimensions={0} | all-to-all | bytes 344064 | tf_op jit(solution)/shard_map/all_to_all | solution.py:222
  118.6 0.7 block.1
  119.2 16.6 %all_to_all.17.square_ref = f32[64,1,128]{2,1,0:T(1,128)S(1)} all-to-all(f32[64,1,128]{2,1,0:T(1,128)S(1)} %get-tuple-element.30), channel_id=1, replica_groups=mesh['yh'=2,'zh'=4,'z1'=2,'z0'=2,'x'=4,'yl'=2,'c'=2] {'yh','yl','x','z0'..., dimensions={0} | all-to-all | bytes 65536 | tf_op jit(solution)/shard_map/all_to_all | solution.py:222
  135.8 0.8 clip.1
  (21 shorter events, 0.2 us)
Async XLA Ops:
  0.6 18.9 %collective-permute-start.2 = (bf16[256,1152]{1,0:T(8,128)(2,1)}, bf16[256,1152]{1,0:T(8,128)(2,1)S(1)}, u32[]{:S(2)}, u32[]{:S(2)}) collective-permute-start(bf16[256,1152]{1,0:T(8,128)(2,1)} %bitcast.12), channel_id=1, source_target_pairs={{0,4},{4,8},{8,12},{12,0},{16,20},{20,24},{24,28},{28,16},{32,36},... | collective-permute-start | bytes 1769480 | tf_op jit(solution)/shard_map/ppermute | solution.py:53
  4.6 30.1 %collective-permute-start = (bf16[256,1152]{1,0:T(8,128)(2,1)}, bf16[256,1152]{1,0:T(8,128)(2,1)S(1)}, u32[]{:S(2)}, u32[]{:S(2)}) collective-permute-start(bf16[256,1152]{1,0:T(8,128)(2,1)} %bitcast.13), channel_id=1, source_target_pairs={{0,508},{4,0},{8,4},{12,8},{16,12},{20,16},{24,20},{28,24},{32,28}... | collective-permute-start | bytes 1769480 | tf_op jit(solution)/shard_map/ppermute | solution.py:53
  19.5 37.3 %collective-permute-start.4 = (bf16[256,1152]{1,0:T(8,128)(2,1)S(1)}, bf16[256,1152]{1,0:T(8,128)(2,1)S(1)}, u32[]{:S(2)}, u32[]{:S(2)}) collective-permute-start(bf16[256,1152]{1,0:T(8,128)(2,1)S(1)} %collective-permute-done.2.right_ref), channel_id=1, source_target_pairs={{0,16},{4,500},{8,504},{12,508},{16,32},{20,4},{24,8},{28,12},{32,... | collective-permute-start | bytes 1769480 | tf_op jit(solution)/shard_map/ppermute | solution.py:53
  22.5 35.9 %collective-permute-start.3 = (bf16[256,1152]{1,0:T(8,128)(2,1)S(1)}, bf16[256,1152]{1,0:T(8,128)(2,1)S(1)}, u32[]{:S(2)}, u32[]{:S(2)}) collective-permute-start(bf16[256,1152]{1,0:T(8,128)(2,1)S(1)} %collective-permute-done.2.right_ref), channel_id=1, source_target_pairs={{0,4},{4,8},{8,12},{12,16},{16,20},{20,24},{24,28},{28,32},{32,36}... | collective-permute-start | bytes 1769480 | tf_op jit(solution)/shard_map/ppermute | solution.py:53
  34.6 25.4 %collective-permute-start.1 = (bf16[256,1152]{1,0:T(8,128)(2,1)S(1)}, bf16[256,1152]{1,0:T(8,128)(2,1)S(1)}, u32[]{:S(2)}, u32[]{:S(2)}) collective-permute-start(bf16[256,1152]{1,0:T(8,128)(2,1)S(1)} %collective-permute-done.left_ref), channel_id=1, source_target_pairs={{0,508},{4,0},{8,20},{12,8},{16,12},{20,16},{24,36},{28,24},{32,28... | collective-permute-start | bytes 1769480 | tf_op jit(solution)/shard_map/ppermute | solution.py:53
  41.3 1.1 copy-start.2
  42.4 7.3 %copy-start.1 = (bf16[1,256,1152]{2,1,0:T(8,128)(2,1)S(1)}, bf16[1,256,1152]{2,1,0:T(8,128)(2,1)}, u32[]{:S(2)}) copy-start(bf16[1,256,1152]{2,1,0:T(8,128)(2,1)} %param.5) | copy-start | bytes 1769476
  42.4 7.3 %copy-start.3 = (bf16[1,256,1152]{2,1,0:T(8,128)(2,1)S(1)}, bf16[1,256,1152]{2,1,0:T(8,128)(2,1)}, u32[]{:S(2)}) copy-start(bf16[1,256,1152]{2,1,0:T(8,128)(2,1)} %param.6) | copy-start | bytes 1769476
  42.4 7.3 %copy-start.4 = (s32[1,32768]{1,0:T(1,128)S(1)}, s32[1,32768]{1,0:T(1,128)}, u32[]{:S(2)}) copy-start(s32[1,32768]{1,0:T(1,128)} %step_hbm.1) | copy-start | bytes 393220
  42.4 7.3 %copy-start.5 = (s32[1,32768]{1,0:T(1,128)S(1)}, s32[1,32768]{1,0:T(1,128)}, u32[]{:S(2)}) copy-start(s32[1,32768]{1,0:T(1,128)} %col_hbm.1) | copy-start | bytes 393220
  44.8 23.3 %collective-permute-start.6 = (bf16[1152,256]{1,0:T(8,128)(2,1)S(1)}, bf16[1152,256]{1,0:T(8,128)(2,1)S(1)}, u32[]{:S(2)}, u32[]{:S(2)}) collective-permute-start(bf16[1152,256]{1,0:T(8,128)(2,1)S(1)} %get-tuple-element.29.turned_ref), channel_id=1, source_target_pairs={{0,1},{1,0},{2,3},{3,2},{4,5},{5,4},{6,7},{7,6},{8,9},{9,8},{10,11... | collective-permute-start | bytes 1769480 | tf_op jit(solution)/shard_map/ppermute | solution.py:258
  60.1 5.7 %copy-start = (bf16[1152,1152]{1,0:T(8,128)(2,1)S(1)}, bf16[1152,1152]{1,0:T(8,128)(2,1)}, u32[]{:S(2)}) copy-start(bf16[1152,1152]{1,0:T(8,128)(2,1)} %proj_ref.1) | copy-start | bytes 7962628
  62.7 5.4 %collective-permute-start.5 = (bf16[256,768]{1,0:T(8,128)(2,1)S(1)}, bf16[256,768]{1,0:T(8,128)(2,1)S(1)}, u32[]{:S(2)}, u32[]{:S(2)}) collective-permute-start(bf16[256,768]{1,0:T(8,128)(2,1)S(1)} %get-tuple-element.28), channel_id=1, source_target_pairs={{0,1},{1,0},{2,3},{3,2},{4,5},{5,4},{6,7},{7,6},{8,9},{9,8},{10,11... | collective-permute-start | bytes 1179656 | tf_op jit(solution)/shard_map/ppermute | solution.py:270
  93.6 6.1 %collective-permute-start.7 = (bf16[8,2688]{1,0:T(8,128)(2,1)S(1)}, bf16[8,2688]{1,0:T(8,128)(2,1)S(1)}, u32[]{:S(2)}, u32[]{:S(2)}) collective-permute-start(bf16[8,2688]{1,0:T(8,128)(2,1)S(1)} %reduce_sum.12), channel_id=1, source_target_pairs={{0,32},{32,0},{1,33},{33,1},{2,34},{34,2},{3,35},{35,3},{4,36},{36... | collective-permute-start | bytes 129032 | tf_op jit(solution)/shard_map/ppermute | solution.py:278

commit v12 on v11

--- a/solution.py
+++ b/solution.py
@@ -157,9 +157,12 @@
     out_ref[...] = dot(grad, pick_ref[...]).astype(BF16)
 
 
-def own_kernel(grad_ref, pick_ref, proj_ref, out_ref, text_ref):
+def own_kernel(grad_ref, pick_ref, out_ref):
     out_ref[...] = dot(grad_ref[...], pick_ref[...]).astype(BF16)
-    text_ref[...] = dot_t(grad_ref[...], proj_ref[...]).astype(BF16)
+
+
+def text_kernel(grad_ref, proj_ref, out_ref):
+    out_ref[...] = dot_t(grad_ref[...], proj_ref[...]).astype(BF16)
 
 
 def partial_kernel(own_ref, came_ref, turned_ref, opposite_ref, out_ref):
@@ -268,14 +271,14 @@
         1 << 30, 32, "far_left",
     )
     columns = lax.ppermute(columns, "c", swap)
-    own, grad_text = call(
-        own_kernel, (grad, pick_here, projection), (((ROWS, PICK), BF16), (full, BF16)), 1 << 28, 24, "own_columns"
-    )
+    (own,) = call(own_kernel, (grad, pick_here), (((ROWS, PICK), BF16),), 1 << 28, 24, "own_columns")
     (both,) = call(
         partial_kernel, (own, columns, turned, opposite), (((2, 2, SHARDS // 2, WIDTH), BF16),), 1 << 30, 32, "partial"
     )
     rows = total(traded(both.reshape(32, 8, WIDTH), NEAR)).astype(BF16)
     near = lax.ppermute(rows, "z1", swap)
+    (grad_text,) = call(text_kernel, (grad, projection), ((full, BF16),), 1 << 28, 24, "grad_text")
+    near, grad_text = lax.optimization_barrier((near, grad_text))
     rows = (rows.astype(F32) + near.astype(F32)).astype(BF16)
     rows = traded(jnp.broadcast_to(rows[None], (4, 8, WIDTH)), "zh")
     block, square = call(block_kernel, (place, rows), (((RB, CB), F32), ((64, 1, 128), F32)), 1 << 20, 16, "block")

time: 137 us -> 138 us (level)
    ppermute x1, waiting for transfers between devices: 4.2 us -> 2.34 us  [local(): near = lax.ppermute(rows, 'z1', swap)]
    pallas_call x10 -> x11, Pallas kernels: 20.2 us -> 20.4 us  [call(): pl.pallas_call(kernel, out_shape=[jax.ShapeDtypeStruct(shape, dtype) for...]
  transfers between devices with their start and end apart: 8 -> 8, of which waited for: 1 -> 2; matrix products, arithmetic and copies ran while one was open for 0% -> 0% of each run, Pallas kernels for 13% -> 13%
where the time goes in v12:
time: 138 us; the launch traced here: 137 us
  blocking collectives  59.8 us (43%)
  starting transfers between devices  50.4 us (37%)
  Pallas kernels  20.4 us (15%)
  waiting for transfers between devices  2.98 us (2%)
  other arithmetic  1.55 us (1%)
    all_to_all x3, blocking collectives, traded(): return lax.all_to_all(value, axis, split_axis=0, concat_axis=0)  59.8 us
    ppermute x5, starting transfers between devices, shifted(): return lax.ppermute(value, DP, pairs)  40.5 us
    pallas_call x11, Pallas kernels, call(): pl.pallas_call(kernel, out_shape=[jax.ShapeDtypeStruct(shape, dtype) for...  20.4 us
    ppermute x1, starting transfers between devices, local(): opposite = lax.ppermute(turned, 'c', swap)  4.84 us
    ppermute x1, starting transfers between devices, local(): columns = lax.ppermute(columns, 'c', swap)  3.07 us
  transfers between devices with their start and end apart: 8, of which 2 were waited for; matrix products, arithmetic and copies ran while one was open for 0% of the time, Pallas kernels for 13%

profile of v12, /device:TPU:1, one launch (start us, length us, event | category | flops | bytes accessed | tf_op | source)
XLA Modules:
  0.0 137.2 jit_solution(7336464662306470103)
XLA Ops:
  0.6 4.0 %collective-permute-start.2 = (bf16[256,1152]{1,0:T(8,128)(2,1)}, bf16[256,1152]{1,0:T(8,128)(2,1)S(1)}, u32[]{:S(2)}, u32[]{:S(2)}) collective-permute-start(bf16[256,1152]{1,0:T(8,128)(2,1)} %bitcast.12), channel_id=1, source_target_pairs={{0,4},{4,8},{8,12},{12,0},{16,20},{20,24},{24,28},{28,16},{32,36},... | collective-permute-start | bytes 1769480 | tf_op jit(solution)/shard_map/ppermute | solution.py:53
  4.6 14.9 %collective-permute-start = (bf16[256,1152]{1,0:T(8,128)(2,1)}, bf16[256,1152]{1,0:T(8,128)(2,1)S(1)}, u32[]{:S(2)}, u32[]{:S(2)}) collective-permute-start(bf16[256,1152]{1,0:T(8,128)(2,1)} %bitcast.13), channel_id=1, source_target_pairs={{0,508},{4,0},{8,4},{12,8},{16,12},{20,16},{24,20},{28,24},{32,28}... | collective-permute-start | bytes 1769480 | tf_op jit(solution)/shard_map/ppermute | solution.py:53
  19.5 3.0 %collective-permute-start.4 = (bf16[256,1152]{1,0:T(8,128)(2,1)S(1)}, bf16[256,1152]{1,0:T(8,128)(2,1)S(1)}, u32[]{:S(2)}, u32[]{:S(2)}) collective-permute-start(bf16[256,1152]{1,0:T(8,128)(2,1)S(1)} %collective-permute-done.2.right_ref), channel_id=1, source_target_pairs={{0,16},{4,500},{8,504},{12,508},{16,32},{20,4},{24,8},{28,12},{32,... | collective-permute-start | bytes 1769480 | tf_op jit(solution)/shard_map/ppermute | solution.py:53
  22.5 12.1 %collective-permute-start.3 = (bf16[256,1152]{1,0:T(8,128)(2,1)S(1)}, bf16[256,1152]{1,0:T(8,128)(2,1)S(1)}, u32[]{:S(2)}, u32[]{:S(2)}) collective-permute-start(bf16[256,1152]{1,0:T(8,128)(2,1)S(1)} %collective-permute-done.2.right_ref), channel_id=1, source_target_pairs={{0,4},{4,8},{8,12},{12,16},{16,20},{20,24},{24,28},{28,32},{32,36}... | collective-permute-start | bytes 1769480 | tf_op jit(solution)/shard_map/ppermute | solution.py:53
  34.6 6.6 %collective-permute-start.1 = (bf16[256,1152]{1,0:T(8,128)(2,1)S(1)}, bf16[256,1152]{1,0:T(8,128)(2,1)S(1)}, u32[]{:S(2)}, u32[]{:S(2)}) collective-permute-start(bf16[256,1152]{1,0:T(8,128)(2,1)S(1)} %collective-permute-done.left_ref), channel_id=1, source_target_pairs={{0,508},{4,0},{8,20},{12,8},{16,12},{20,16},{24,36},{28,24},{32,28... | collective-permute-start | bytes 1769480 | tf_op jit(solution)/shard_map/ppermute | solution.py:53
  41.3 1.1 copy-done.2
  42.4 2.4 %order.1 = (bf16[1152,256]{1,0:T(8,128)(2,1)S(1)}, bf16[1152,768]{1,0:T(8,128)(2,1)S(1)}, bf16[1152,768]{1,0:T(8,128)(2,1)S(1)}) custom-call(s32[7]{0:T(128)S(1)} %stack.31.place_ref, bf16[256,1152]{1,0:T(8,128)(2,1)S(1)} %bitcast.15), custom_call_target="tpu_custom_call" | custom-call | flops 1073741824 | bytes 4194304 | tf_op jit(solution)/shard_map/order/pallas_call | solution.py:212
  44.8 4.8 %collective-permute-start.6 = (bf16[1152,256]{1,0:T(8,128)(2,1)S(1)}, bf16[1152,256]{1,0:T(8,128)(2,1)S(1)}, u32[]{:S(2)}, u32[]{:S(2)}) collective-permute-start(bf16[1152,256]{1,0:T(8,128)(2,1)S(1)} %get-tuple-element.27.turned_ref), channel_id=1, source_target_pairs={{0,1},{1,0},{2,3},{3,2},{4,5},{5,4},{6,7},{7,6},{8,9},{9,8},{10,11... | collective-permute-start | bytes 1769480 | tf_op jit(solution)/shard_map/ppermute | solution.py:261
  49.7 4.8 %hidden_and_own.1 = (f32[256,1152]{1,0:T(8,128)S(1)}, f32[256,128]{1,0:T(8,128)S(1)}, bf16[256,1152]{1,0:T(8,128)(2,1)S(1)}, f32[256,1152]{1,0:T(8,128)S(1)}, s3...) custom-call(s32[7]{0:T(128)S(1)} %stack.31.place_ref, bf16[256,1152]{1,0:T(8,128)(2,1)S(1)} %bitcast.16, ...), custom_call_target="tpu_custom_call" | custom-call | flops 1073741824 | bytes 4194304 | tf_op jit(solution)/shard_map/hidden_and_own/pallas_call | solution.py:212
  54.5 2.3 %near_pairs.1.acc_ref = f32[256,1152]{1,0:T(8,128)S(1)} custom-call(s32[7]{0:T(128)S(1)} %stack.31.place_ref, bf16[256,1152]{1,0:T(8,128)(2,1)S(1)} %collective-permute-done.2.right_ref, bf16[256,1152]{1,0:T(8,128)(2,1)S(1)} %collective-permute-done.left_ref, s32[8,256]{1,0:T(8,128)S(1)} %get-tuple-element.17.step_ref, ...), custom_call_target="tpu_custom_call" | custom-call | flops 1073741824 | bytes 4194304 | tf_op jit(solution)/shard_map/near_pairs/pallas_call | solution.py:212
  56.8 1.6 %far_across.1.acc_ref = f32[256,1152]{1,0:T(8,128)S(1)} custom-call(s32[7]{0:T(128)S(1)} %stack.31.place_ref, bf16[256,1152]{1,0:T(8,128)(2,1)S(1)} %collective-permute-done.4.image_ref, s32[8,256]{1,0:T(8,128)S(1)} %get-tuple-element.17.step_ref, s32[8,256]{1,0:T(8,128)S(1)} %get-tuple-element.18.col_ref, bf16[256,1152]{1,0:T(8,128)(2,1)S(1)} %get-tuple-element.19.text_ref, ...), custom_call_target="tpu_custom_call" | custom-call | flops 268435456 | bytes 4194304 | tf_op jit(solution)/shard_map/far_across/pallas_call | solution.py:212
  58.5 1.6 %far_right.1.acc_ref = f32[256,1152]{1,0:T(8,128)S(1)} custom-call(s32[7]{0:T(128)S(1)} %stack.31.place_ref, bf16[256,1152]{1,0:T(8,128)(2,1)S(1)} %collective-permute-done.3.image_ref, s32[8,256]{1,0:T(8,128)S(1)} %get-tuple-element.17.step_ref, s32[8,256]{1,0:T(8,128)S(1)} %get-tuple-element.18.col_ref, bf16[256,1152]{1,0:T(8,128)(2,1)S(1)} %get-tuple-element.19.text_ref, ...), custom_call_target="tpu_custom_call" | custom-call | flops 268435456 | bytes 4194304 | tf_op jit(solution)/shard_map/far_right/pallas_call | solution.py:212
  60.1 2.6 %far_left.1 = (bf16[256,1152]{1,0:T(8,128)(2,1)S(1)}, bf16[256,768]{1,0:T(8,128)(2,1)S(1)}) custom-call(s32[7]{0:T(128)S(1)} %stack.31.place_ref, bf16[256,1152]{1,0:T(8,128)(2,1)S(1)} %collective-permute-done.1.left_ref, s32[8,256]{1,0:T(8,128)S(1)} %get-tuple-element.17.step_ref, s32[8,256]{1,0:T(8,128)S(1)} %get-tuple-element.18.col_ref, ...), custom_call_target="tpu_custom_call" | custom-call | flops 1073741824 | bytes 4194304 | tf_op jit(solution)/shard_map/far_left/pallas_call | solution.py:212
  62.7 3.1 %collective-permute-start.5 = (bf16[256,768]{1,0:T(8,128)(2,1)S(1)}, bf16[256,768]{1,0:T(8,128)(2,1)S(1)}, u32[]{:S(2)}, u32[]{:S(2)}) collective-permute-start(bf16[256,768]{1,0:T(8,128)(2,1)S(1)} %get-tuple-element.26), channel_id=1, source_target_pairs={{0,1},{1,0},{2,3},{3,2},{4,5},{5,4},{6,7},{7,6},{8,9},{9,8},{10,11... | collective-permute-start | bytes 1179656 | tf_op jit(solution)/shard_map/ppermute | solution.py:273
  65.8 0.7 own_columns.1.own_ref
  67.1 1.1 partial.1
  68.2 24.8 %all_to_all.15 = bf16[32,8,2688]{2,1,0:T(8,128)(2,1)} all-to-all(bf16[32,8,2688]{2,1,0:T(8,128)(2,1)S(1)} %bitcast.11), channel_id=1, replica_groups=mesh['yh'=2,'zh'=4,'z1'=2,'z0'=2,'x'=4,'yl'=2,'c'=2] {'yh','yl','x','z0'}, dimensions={0} | all-to-all | bytes 2752512 | tf_op jit(solution)/shard_map/all_to_all | solution.py:225
  93.0 1.5 %reduce_sum.12 = bf16[8,2688]{1,0:T(8,128)(2,1)S(1)} reduce(bf16[32,8,2688]{2,1,0:T(8,128)(2,1)} %all_to_all.15, bf16[]{:T(256)} %constant.43.clone.1), dimensions={0}, to_apply=%region_0.1 | reduce | flops 666624 | bytes 1419266 | tf_op jit(solution)/shard_map/reduce_sum | solution.py:229
  94.5 1.9 %collective-permute-start.7 = (bf16[8,2688]{1,0:T(8,128)(2,1)S(1)}, bf16[8,2688]{1,0:T(8,128)(2,1)S(1)}, u32[]{:S(2)}, u32[]{:S(2)}) collective-permute-start(bf16[8,2688]{1,0:T(8,128)(2,1)S(1)} %reduce_sum.12), channel_id=1, source_target_pairs={{0,32},{32,0},{1,33},{33,1},{2,34},{34,2},{3,35},{35,3},{4,36},{36... | collective-permute-start | bytes 129032 | tf_op jit(solution)/shard_map/ppermute | solution.py:279
  96.4 1.8 %grad_text.1 = bf16[256,1152]{1,0:T(8,128)(2,1)} custom-call(bf16[256,1152]{1,0:T(8,128)(2,1)S(1)} %get-tuple-element.24.grad_ref, bf16[1152,1152]{1,0:T(8,128)(2,1)S(1)} %copy-done), custom_call_target="tpu_custom_call" | custom-call | flops 268435456 | bytes 4194304 | tf_op jit(solution)/shard_map/grad_text/pallas_call | solution.py:212
  98.3 2.3 %collective-permute-done.7 = bf16[8,2688]{1,0:T(8,128)(2,1)S(1)} collective-permute-done((bf16[8,2688]{1,0:T(8,128)(2,1)S(1)}, bf16[8,2688]{1,0:T(8,128)(2,1)S(1)}, u32[]{:S(2)}, u32[]{:S(2)}) %collective-permute-start.7) | collective-permute-done | bytes 43040 | tf_op jit(solution)/shard_map/ppermute | solution.py:279
  100.7 18.5 %all_to_all.16.came_ref = bf16[4,8,2688]{2,1,0:T(8,128)(2,1)S(1)} all-to-all(bf16[4,8,2688]{2,1,0:T(8,128)(2,1)S(1)} %broadcast_in_dim.10), channel_id=1, replica_groups=mesh['yh'=2,'zh'=4,'z1'=2,'z0'=2,'x'=4,'yl'=2,'c'=2] {'zh'}, dimensions={0} | all-to-all | bytes 344064 | tf_op jit(solution)/shard_map/all_to_all | solution.py:225
  119.8 16.6 %all_to_all.17.square_ref = f32[64,1,128]{2,1,0:T(1,128)S(1)} all-to-all(f32[64,1,128]{2,1,0:T(1,128)S(1)} %get-tuple-element.30), channel_id=1, replica_groups=mesh['yh'=2,'zh'=4,'z1'=2,'z0'=2,'x'=4,'yl'=2,'c'=2] {'yh','yl','x','z0'..., dimensions={0} | all-to-all | bytes 65536 | tf_op jit(solution)/shard_map/all_to_all | solution.py:225
  136.4 0.8 clip.1
  (22 shorter events, 1.5 us)
Async XLA Ops:
  0.6 18.9 %collective-permute-start.2 = (bf16[256,1152]{1,0:T(8,128)(2,1)}, bf16[256,1152]{1,0:T(8,128)(2,1)S(1)}, u32[]{:S(2)}, u32[]{:S(2)}) collective-permute-start(bf16[256,1152]{1,0:T(8,128)(2,1)} %bitcast.12), channel_id=1, source_target_pairs={{0,4},{4,8},{8,12},{12,0},{16,20},{20,24},{24,28},{28,16},{32,36},... | collective-permute-start | bytes 1769480 | tf_op jit(solution)/shard_map/ppermute | solution.py:53
  4.6 30.1 %collective-permute-start = (bf16[256,1152]{1,0:T(8,128)(2,1)}, bf16[256,1152]{1,0:T(8,128)(2,1)S(1)}, u32[]{:S(2)}, u32[]{:S(2)}) collective-permute-start(bf16[256,1152]{1,0:T(8,128)(2,1)} %bitcast.13), channel_id=1, source_target_pairs={{0,508},{4,0},{8,4},{12,8},{16,12},{20,16},{24,20},{28,24},{32,28}... | collective-permute-start | bytes 1769480 | tf_op jit(solution)/shard_map/ppermute | solution.py:53
  19.5 37.3 %collective-permute-start.4 = (bf16[256,1152]{1,0:T(8,128)(2,1)S(1)}, bf16[256,1152]{1,0:T(8,128)(2,1)S(1)}, u32[]{:S(2)}, u32[]{:S(2)}) collective-permute-start(bf16[256,1152]{1,0:T(8,128)(2,1)S(1)} %collective-permute-done.2.right_ref), channel_id=1, source_target_pairs={{0,16},{4,500},{8,504},{12,508},{16,32},{20,4},{24,8},{28,12},{32,... | collective-permute-start | bytes 1769480 | tf_op jit(solution)/shard_map/ppermute | solution.py:53
  22.5 35.9 %collective-permute-start.3 = (bf16[256,1152]{1,0:T(8,128)(2,1)S(1)}, bf16[256,1152]{1,0:T(8,128)(2,1)S(1)}, u32[]{:S(2)}, u32[]{:S(2)}) collective-permute-start(bf16[256,1152]{1,0:T(8,128)(2,1)S(1)} %collective-permute-done.2.right_ref), channel_id=1, source_target_pairs={{0,4},{4,8},{8,12},{12,16},{16,20},{20,24},{24,28},{28,32},{32,36}... | collective-permute-start | bytes 1769480 | tf_op jit(solution)/shard_map/ppermute | solution.py:53
  34.6 25.4 %collective-permute-start.1 = (bf16[256,1152]{1,0:T(8,128)(2,1)S(1)}, bf16[256,1152]{1,0:T(8,128)(2,1)S(1)}, u32[]{:S(2)}, u32[]{:S(2)}) collective-permute-start(bf16[256,1152]{1,0:T(8,128)(2,1)S(1)} %collective-permute-done.left_ref), channel_id=1, source_target_pairs={{0,508},{4,0},{8,20},{12,8},{16,12},{20,16},{24,36},{28,24},{32,28... | collective-permute-start | bytes 1769480 | tf_op jit(solution)/shard_map/ppermute | solution.py:53
  41.3 1.1 copy-start.2
  42.4 7.3 %copy-start.1 = (bf16[1,256,1152]{2,1,0:T(8,128)(2,1)S(1)}, bf16[1,256,1152]{2,1,0:T(8,128)(2,1)}, u32[]{:S(2)}) copy-start(bf16[1,256,1152]{2,1,0:T(8,128)(2,1)} %param.5) | copy-start | bytes 1769476
  42.4 7.3 %copy-start.3 = (bf16[1,256,1152]{2,1,0:T(8,128)(2,1)S(1)}, bf16[1,256,1152]{2,1,0:T(8,128)(2,1)}, u32[]{:S(2)}) copy-start(bf16[1,256,1152]{2,1,0:T(8,128)(2,1)} %param.6) | copy-start | bytes 1769476
  42.4 7.3 %copy-start.4 = (s32[1,32768]{1,0:T(1,128)S(1)}, s32[1,32768]{1,0:T(1,128)}, u32[]{:S(2)}) copy-start(s32[1,32768]{1,0:T(1,128)} %step_hbm.1) | copy-start | bytes 393220
  42.4 7.3 %copy-start.5 = (s32[1,32768]{1,0:T(1,128)S(1)}, s32[1,32768]{1,0:T(1,128)}, u32[]{:S(2)}) copy-start(s32[1,32768]{1,0:T(1,128)} %col_hbm.1) | copy-start | bytes 393220
  44.8 21.6 %collective-permute-start.6 = (bf16[1152,256]{1,0:T(8,128)(2,1)S(1)}, bf16[1152,256]{1,0:T(8,128)(2,1)S(1)}, u32[]{:S(2)}, u32[]{:S(2)}) collective-permute-start(bf16[1152,256]{1,0:T(8,128)(2,1)S(1)} %get-tuple-element.27.turned_ref), channel_id=1, source_target_pairs={{0,1},{1,0},{2,3},{3,2},{4,5},{5,4},{6,7},{7,6},{8,9},{9,8},{10,11... | collective-permute-start | bytes 1769480 | tf_op jit(solution)/shard_map/ppermute | solution.py:261
  62.7 4.4 %collective-permute-start.5 = (bf16[256,768]{1,0:T(8,128)(2,1)S(1)}, bf16[256,768]{1,0:T(8,128)(2,1)S(1)}, u32[]{:S(2)}, u32[]{:S(2)}) collective-permute-start(bf16[256,768]{1,0:T(8,128)(2,1)S(1)} %get-tuple-element.26), channel_id=1, source_target_pairs={{0,1},{1,0},{2,3},{3,2},{4,5},{5,4},{6,7},{7,6},{8,9},{9,8},{10,11... | collective-permute-start | bytes 1179656 | tf_op jit(solution)/shard_map/ppermute | solution.py:273
  68.2 28.2 %copy-start = (bf16[1152,1152]{1,0:T(8,128)(2,1)S(1)}, bf16[1152,1152]{1,0:T(8,128)(2,1)}, u32[]{:S(2)}) copy-start(bf16[1152,1152]{1,0:T(8,128)(2,1)} %proj_ref.1) | copy-start | bytes 7962628
  94.5 6.1 %collective-permute-start.7 = (bf16[8,2688]{1,0:T(8,128)(2,1)S(1)}, bf16[8,2688]{1,0:T(8,128)(2,1)S(1)}, u32[]{:S(2)}, u32[]{:S(2)}) collective-permute-start(bf16[8,2688]{1,0:T(8,128)(2,1)S(1)} %reduce_sum.12), channel_id=1, source_target_pairs={{0,32},{32,0},{1,33},{33,1},{2,34},{34,2},{3,35},{35,3},{4,36},{36... | collective-permute-start | bytes 129032 | tf_op jit(solution)/shard_map/ppermute | solution.py:279

commit v13 on v12

--- a/solution.py
+++ b/solution.py
@@ -161,7 +161,10 @@
     out_ref[...] = dot(grad_ref[...], pick_ref[...]).astype(BF16)
 
 
-def text_kernel(grad_ref, proj_ref, out_ref):
+def text_kernel(grad_ref, proj_hbm, out_ref, proj_ref, sem):
+    copy = pltpu.make_async_copy(proj_hbm, proj_ref, sem)
+    copy.start()
+    copy.wait()
     out_ref[...] = dot_t(grad_ref[...], proj_ref[...]).astype(BF16)
 
 
@@ -277,7 +280,10 @@
     )
     rows = total(traded(both.reshape(32, 8, WIDTH), NEAR)).astype(BF16)
     near = lax.ppermute(rows, "z1", swap)
-    (grad_text,) = call(text_kernel, (grad, projection), ((full, BF16),), 1 << 28, 24, "grad_text")
+    (grad_text,) = call(
+        text_kernel, (grad, projection), ((full, BF16),), 1 << 28, 52, "grad_text", (1,),
+        (pltpu.VMEM((D, E), BF16), pltpu.SemaphoreType.DMA),
+    )
     near, grad_text = lax.optimization_barrier((near, grad_text))
     rows = (rows.astype(F32) + near.astype(F32)).astype(BF16)
     rows = traded(jnp.broadcast_to(rows[None], (4, 8, WIDTH)), "zh")

time: 138 us -> 138 us (level)
  blocking collectives: 59.8 us -> 61.6 us
  Pallas kernels: 20.4 us -> 22.2 us
  waiting for transfers between devices: 2.98 us -> 1.22 us
    all_to_all x3, blocking collectives: 59.8 us -> 61.6 us  [traded(): return lax.all_to_all(value, axis, split_axis=0, concat_axis=0)]
    pallas_call x11, Pallas kernels: 20.4 us -> 22.2 us  [call(): pl.pallas_call(kernel, out_shape=[jax.ShapeDtypeStruct(shape, dtype) for...]
    ppermute x1, waiting for transfers between devices: 2.34 us -> 0.58 us  [local(): near = lax.ppermute(rows, 'z1', swap)]
  transfers between devices with their start and end apart: 8 -> 8, of which waited for: 2 -> 2; matrix products, arithmetic and copies ran while one was open for 0% -> 0% of each run, Pallas kernels for 13% -> 14%
where the time goes in v13:
time: 138 us
  blocking collectives  61.6 us (45%)
  starting transfers between devices  50.4 us (37%)
  Pallas kernels  22.2 us (16%)
    all_to_all x3, blocking collectives, traded(): return lax.all_to_all(value, axis, split_axis=0, concat_axis=0)  61.6 us
    ppermute x5, starting transfers between devices, shifted(): return lax.ppermute(value, DP, pairs)  40.5 us
    pallas_call x11, Pallas kernels, call(): pl.pallas_call(kernel, out_shape=[jax.ShapeDtypeStruct(shape, dtype) for...  22.2 us
    ppermute x1, starting transfers between devices, local(): opposite = lax.ppermute(turned, 'c', swap)  4.84 us
    ppermute x1, starting transfers between devices, local(): columns = lax.ppermute(columns, 'c', swap)  3.07 us
  transfers between devices with their start and end apart: 8, of which 2 were waited for; matrix products, arithmetic and copies ran while one was open for 0% of the time, Pallas kernels for 14%

profile of v13, /device:TPU:1, one launch (start us, length us, event | category | flops | bytes accessed | tf_op | source)
XLA Modules:
  0.0 137.7 jit_solution(16770424535538847357)
XLA Ops:
  0.6 4.0 %collective-permute-start.2 = (bf16[256,1152]{1,0:T(8,128)(2,1)}, bf16[256,1152]{1,0:T(8,128)(2,1)S(1)}, u32[]{:S(2)}, u32[]{:S(2)}) collective-permute-start(bf16[256,1152]{1,0:T(8,128)(2,1)} %bitcast.12), channel_id=1, source_target_pairs={{0,4},{4,8},{8,12},{12,0},{16,20},{20,24},{24,28},{28,16},{32,36},... | collective-permute-start | bytes 1769480 | tf_op jit(solution)/shard_map/ppermute | solution.py:53
  4.6 14.9 %collective-permute-start = (bf16[256,1152]{1,0:T(8,128)(2,1)}, bf16[256,1152]{1,0:T(8,128)(2,1)S(1)}, u32[]{:S(2)}, u32[]{:S(2)}) collective-permute-start(bf16[256,1152]{1,0:T(8,128)(2,1)} %bitcast.13), channel_id=1, source_target_pairs={{0,508},{4,0},{8,4},{12,8},{16,12},{20,16},{24,20},{28,24},{32,28}... | collective-permute-start | bytes 1769480 | tf_op jit(solution)/shard_map/ppermute | solution.py:53
  19.5 3.0 %collective-permute-start.4 = (bf16[256,1152]{1,0:T(8,128)(2,1)S(1)}, bf16[256,1152]{1,0:T(8,128)(2,1)S(1)}, u32[]{:S(2)}, u32[]{:S(2)}) collective-permute-start(bf16[256,1152]{1,0:T(8,128)(2,1)S(1)} %collective-permute-done.2.right_ref), channel_id=1, source_target_pairs={{0,16},{4,500},{8,504},{12,508},{16,32},{20,4},{24,8},{28,12},{32,... | collective-permute-start | bytes 1769480 | tf_op jit(solution)/shard_map/ppermute | solution.py:53
  22.5 12.1 %collective-permute-start.3 = (bf16[256,1152]{1,0:T(8,128)(2,1)S(1)}, bf16[256,1152]{1,0:T(8,128)(2,1)S(1)}, u32[]{:S(2)}, u32[]{:S(2)}) collective-permute-start(bf16[256,1152]{1,0:T(8,128)(2,1)S(1)} %collective-permute-done.2.right_ref), channel_id=1, source_target_pairs={{0,4},{4,8},{8,12},{12,16},{16,20},{20,24},{24,28},{28,32},{32,36}... | collective-permute-start | bytes 1769480 | tf_op jit(solution)/shard_map/ppermute | solution.py:53
  34.6 6.6 %collective-permute-start.1 = (bf16[256,1152]{1,0:T(8,128)(2,1)S(1)}, bf16[256,1152]{1,0:T(8,128)(2,1)S(1)}, u32[]{:S(2)}, u32[]{:S(2)}) collective-permute-start(bf16[256,1152]{1,0:T(8,128)(2,1)S(1)} %collective-permute-done.left_ref), channel_id=1, source_target_pairs={{0,508},{4,0},{8,20},{12,8},{16,12},{20,16},{24,36},{28,24},{32,28... | collective-permute-start | bytes 1769480 | tf_op jit(solution)/shard_map/ppermute | solution.py:53
  41.3 1.1 copy-done.1
  42.4 2.4 %order.1 = (bf16[1152,256]{1,0:T(8,128)(2,1)S(1)}, bf16[1152,768]{1,0:T(8,128)(2,1)S(1)}, bf16[1152,768]{1,0:T(8,128)(2,1)S(1)}) custom-call(s32[7]{0:T(128)S(1)} %stack.31.place_ref, bf16[256,1152]{1,0:T(8,128)(2,1)S(1)} %bitcast.15), custom_call_target="tpu_custom_call" | custom-call | flops 1073741824 | bytes 4194304 | tf_op jit(solution)/shard_map/order/pallas_call | solution.py:215
  44.8 4.8 %collective-permute-start.6 = (bf16[1152,256]{1,0:T(8,128)(2,1)S(1)}, bf16[1152,256]{1,0:T(8,128)(2,1)S(1)}, u32[]{:S(2)}, u32[]{:S(2)}) collective-permute-start(bf16[1152,256]{1,0:T(8,128)(2,1)S(1)} %get-tuple-element.27.turned_ref), channel_id=1, source_target_pairs={{0,1},{1,0},{2,3},{3,2},{4,5},{5,4},{6,7},{7,6},{8,9},{9,8},{10,11... | collective-permute-start | bytes 1769480 | tf_op jit(solution)/shard_map/ppermute | solution.py:264
  49.7 4.8 %hidden_and_own.1 = (f32[256,1152]{1,0:T(8,128)S(1)}, f32[256,128]{1,0:T(8,128)S(1)}, bf16[256,1152]{1,0:T(8,128)(2,1)S(1)}, f32[256,1152]{1,0:T(8,128)S(1)}, s3...) custom-call(s32[7]{0:T(128)S(1)} %stack.31.place_ref, bf16[256,1152]{1,0:T(8,128)(2,1)S(1)} %bitcast.16, ...), custom_call_target="tpu_custom_call" | custom-call | flops 1073741824 | bytes 4194304 | tf_op jit(solution)/shard_map/hidden_and_own/pallas_call | solution.py:215
  54.5 2.3 %near_pairs.1.acc_ref = f32[256,1152]{1,0:T(8,128)S(1)} custom-call(s32[7]{0:T(128)S(1)} %stack.31.place_ref, bf16[256,1152]{1,0:T(8,128)(2,1)S(1)} %collective-permute-done.2.right_ref, bf16[256,1152]{1,0:T(8,128)(2,1)S(1)} %collective-permute-done.left_ref, s32[8,256]{1,0:T(8,128)S(1)} %get-tuple-element.17.step_ref, ...), custom_call_target="tpu_custom_call" | custom-call | flops 1073741824 | bytes 4194304 | tf_op jit(solution)/shard_map/near_pairs/pallas_call | solution.py:215
  56.8 1.6 %far_across.1.acc_ref = f32[256,1152]{1,0:T(8,128)S(1)} custom-call(s32[7]{0:T(128)S(1)} %stack.31.place_ref, bf16[256,1152]{1,0:T(8,128)(2,1)S(1)} %collective-permute-done.4.image_ref, s32[8,256]{1,0:T(8,128)S(1)} %get-tuple-element.17.step_ref, s32[8,256]{1,0:T(8,128)S(1)} %get-tuple-element.18.col_ref, bf16[256,1152]{1,0:T(8,128)(2,1)S(1)} %get-tuple-element.19.text_ref, ...), custom_call_target="tpu_custom_call" | custom-call | flops 268435456 | bytes 4194304 | tf_op jit(solution)/shard_map/far_across/pallas_call | solution.py:215
  58.5 1.6 %far_right.1.acc_ref = f32[256,1152]{1,0:T(8,128)S(1)} custom-call(s32[7]{0:T(128)S(1)} %stack.31.place_ref, bf16[256,1152]{1,0:T(8,128)(2,1)S(1)} %collective-permute-done.3.image_ref, s32[8,256]{1,0:T(8,128)S(1)} %get-tuple-element.17.step_ref, s32[8,256]{1,0:T(8,128)S(1)} %get-tuple-element.18.col_ref, bf16[256,1152]{1,0:T(8,128)(2,1)S(1)} %get-tuple-element.19.text_ref, ...), custom_call_target="tpu_custom_call" | custom-call | flops 268435456 | bytes 4194304 | tf_op jit(solution)/shard_map/far_right/pallas_call | solution.py:215
  60.1 2.6 %far_left.1 = (bf16[256,1152]{1,0:T(8,128)(2,1)S(1)}, bf16[256,768]{1,0:T(8,128)(2,1)S(1)}) custom-call(s32[7]{0:T(128)S(1)} %stack.31.place_ref, bf16[256,1152]{1,0:T(8,128)(2,1)S(1)} %collective-permute-done.1.left_ref, s32[8,256]{1,0:T(8,128)S(1)} %get-tuple-element.17.step_ref, s32[8,256]{1,0:T(8,128)S(1)} %get-tuple-element.18.col_ref, ...), custom_call_target="tpu_custom_call" | custom-call | flops 1073741824 | bytes 4194304 | tf_op jit(solution)/shard_map/far_left/pallas_call | solution.py:215
  62.7 3.1 %collective-permute-start.5 = (bf16[256,768]{1,0:T(8,128)(2,1)S(1)}, bf16[256,768]{1,0:T(8,128)(2,1)S(1)}, u32[]{:S(2)}, u32[]{:S(2)}) collective-permute-start(bf16[256,768]{1,0:T(8,128)(2,1)S(1)} %get-tuple-element.26), channel_id=1, source_target_pairs={{0,1},{1,0},{2,3},{3,2},{4,5},{5,4},{6,7},{7,6},{8,9},{9,8},{10,11... | collective-permute-start | bytes 1179656 | tf_op jit(solution)/shard_map/ppermute | solution.py:276
  65.8 0.7 own_columns.1.own_ref
  66.5 0.6 collective-permute-done.5.came_ref
  67.1 1.1 partial.1
  68.2 23.8 %all_to_all.15 = bf16[32,8,2688]{2,1,0:T(8,128)(2,1)S(1)} all-to-all(bf16[32,8,2688]{2,1,0:T(8,128)(2,1)S(1)} %bitcast.11), channel_id=1, replica_groups=mesh['yh'=2,'zh'=4,'z1'=2,'z0'=2,'x'=4,'yl'=2,'c'=2] {'yh','yl','x','z0'}, dimensions={0} | all-to-all | bytes 2752512 | tf_op jit(solution)/shard_map/all_to_all | solution.py:228
  92.2 1.9 %collective-permute-start.7 = (bf16[8,2688]{1,0:T(8,128)(2,1)S(1)}, bf16[8,2688]{1,0:T(8,128)(2,1)S(1)}, u32[]{:S(2)}, u32[]{:S(2)}) collective-permute-start(bf16[8,2688]{1,0:T(8,128)(2,1)S(1)} %reduce_sum.12), channel_id=1, source_target_pairs={{0,32},{32,0},{1,33},{33,1},{2,34},{34,2},{3,35},{35,3},{4,36},{36... | collective-permute-start | bytes 129032 | tf_op jit(solution)/shard_map/ppermute | solution.py:282
  94.1 3.6 %grad_text.1 = bf16[256,1152]{1,0:T(8,128)(2,1)} custom-call(bf16[256,1152]{1,0:T(8,128)(2,1)S(1)} %get-tuple-element.24.grad_ref, bf16[1152,1152]{1,0:T(8,128)(2,1)} %proj_hbm.3), custom_call_target="tpu_custom_call" | custom-call | flops 268435456 | bytes 4194304 | tf_op jit(solution)/shard_map/grad_text/pallas_call | solution.py:215
  98.4 20.2 %all_to_all.16.came_ref = bf16[4,8,2688]{2,1,0:T(8,128)(2,1)S(1)} all-to-all(bf16[4,8,2688]{2,1,0:T(8,128)(2,1)S(1)} %broadcast_in_dim.10), channel_id=1, replica_groups=mesh['yh'=2,'zh'=4,'z1'=2,'z0'=2,'x'=4,'yl'=2,'c'=2] {'zh'}, dimensions={0} | all-to-all | bytes 344064 | tf_op jit(solution)/shard_map/all_to_all | solution.py:228
  118.5 0.7 block.1
  119.2 17.7 %all_to_all.17.square_ref = f32[64,1,128]{2,1,0:T(1,128)S(1)} all-to-all(f32[64,1,128]{2,1,0:T(1,128)S(1)} %get-tuple-element.30), channel_id=1, replica_groups=mesh['yh'=2,'zh'=4,'z1'=2,'z0'=2,'x'=4,'yl'=2,'c'=2] {'yh','yl','x','z0'..., dimensions={0} | all-to-all | bytes 65536 | tf_op jit(solution)/shard_map/all_to_all | solution.py:228
  136.9 0.8 clip.1
  (20 shorter events, 0.9 us)
Async XLA Ops:
  0.6 18.9 %collective-permute-start.2 = (bf16[256,1152]{1,0:T(8,128)(2,1)}, bf16[256,1152]{1,0:T(8,128)(2,1)S(1)}, u32[]{:S(2)}, u32[]{:S(2)}) collective-permute-start(bf16[256,1152]{1,0:T(8,128)(2,1)} %bitcast.12), channel_id=1, source_target_pairs={{0,4},{4,8},{8,12},{12,0},{16,20},{20,24},{24,28},{28,16},{32,36},... | collective-permute-start | bytes 1769480 | tf_op jit(solution)/shard_map/ppermute | solution.py:53
  4.6 30.1 %collective-permute-start = (bf16[256,1152]{1,0:T(8,128)(2,1)}, bf16[256,1152]{1,0:T(8,128)(2,1)S(1)}, u32[]{:S(2)}, u32[]{:S(2)}) collective-permute-start(bf16[256,1152]{1,0:T(8,128)(2,1)} %bitcast.13), channel_id=1, source_target_pairs={{0,508},{4,0},{8,4},{12,8},{16,12},{20,16},{24,20},{28,24},{32,28}... | collective-permute-start | bytes 1769480 | tf_op jit(solution)/shard_map/ppermute | solution.py:53
  19.5 37.3 %collective-permute-start.4 = (bf16[256,1152]{1,0:T(8,128)(2,1)S(1)}, bf16[256,1152]{1,0:T(8,128)(2,1)S(1)}, u32[]{:S(2)}, u32[]{:S(2)}) collective-permute-start(bf16[256,1152]{1,0:T(8,128)(2,1)S(1)} %collective-permute-done.2.right_ref), channel_id=1, source_target_pairs={{0,16},{4,500},{8,504},{12,508},{16,32},{20,4},{24,8},{28,12},{32,... | collective-permute-start | bytes 1769480 | tf_op jit(solution)/shard_map/ppermute | solution.py:53
  22.5 35.9 %collective-permute-start.3 = (bf16[256,1152]{1,0:T(8,128)(2,1)S(1)}, bf16[256,1152]{1,0:T(8,128)(2,1)S(1)}, u32[]{:S(2)}, u32[]{:S(2)}) collective-permute-start(bf16[256,1152]{1,0:T(8,128)(2,1)S(1)} %collective-permute-done.2.right_ref), channel_id=1, source_target_pairs={{0,4},{4,8},{8,12},{12,16},{16,20},{20,24},{24,28},{28,32},{32,36}... | collective-permute-start | bytes 1769480 | tf_op jit(solution)/shard_map/ppermute | solution.py:53
  34.6 25.4 %collective-permute-start.1 = (bf16[256,1152]{1,0:T(8,128)(2,1)S(1)}, bf16[256,1152]{1,0:T(8,128)(2,1)S(1)}, u32[]{:S(2)}, u32[]{:S(2)}) collective-permute-start(bf16[256,1152]{1,0:T(8,128)(2,1)S(1)} %collective-permute-done.left_ref), channel_id=1, source_target_pairs={{0,508},{4,0},{8,20},{12,8},{16,12},{20,16},{24,36},{28,24},{32,28... | collective-permute-start | bytes 1769480 | tf_op jit(solution)/shard_map/ppermute | solution.py:53
  41.3 1.1 copy-start.1
  42.4 7.3 %copy-start = (bf16[1,256,1152]{2,1,0:T(8,128)(2,1)S(1)}, bf16[1,256,1152]{2,1,0:T(8,128)(2,1)}, u32[]{:S(2)}) copy-start(bf16[1,256,1152]{2,1,0:T(8,128)(2,1)} %param.5) | copy-start | bytes 1769476
  42.4 7.3 %copy-start.2 = (bf16[1,256,1152]{2,1,0:T(8,128)(2,1)S(1)}, bf16[1,256,1152]{2,1,0:T(8,128)(2,1)}, u32[]{:S(2)}) copy-start(bf16[1,256,1152]{2,1,0:T(8,128)(2,1)} %param.6) | copy-start | bytes 1769476
  42.4 7.3 %copy-start.3 = (s32[1,32768]{1,0:T(1,128)S(1)}, s32[1,32768]{1,0:T(1,128)}, u32[]{:S(2)}) copy-start(s32[1,32768]{1,0:T(1,128)} %step_hbm.1) | copy-start | bytes 393220
  42.4 7.3 %copy-start.4 = (s32[1,32768]{1,0:T(1,128)S(1)}, s32[1,32768]{1,0:T(1,128)}, u32[]{:S(2)}) copy-start(s32[1,32768]{1,0:T(1,128)} %col_hbm.1) | copy-start | bytes 393220
  44.8 21.6 %collective-permute-start.6 = (bf16[1152,256]{1,0:T(8,128)(2,1)S(1)}, bf16[1152,256]{1,0:T(8,128)(2,1)S(1)}, u32[]{:S(2)}, u32[]{:S(2)}) collective-permute-start(bf16[1152,256]{1,0:T(8,128)(2,1)S(1)} %get-tuple-element.27.turned_ref), channel_id=1, source_target_pairs={{0,1},{1,0},{2,3},{3,2},{4,5},{5,4},{6,7},{7,6},{8,9},{9,8},{10,11... | collective-permute-start | bytes 1769480 | tf_op jit(solution)/shard_map/ppermute | solution.py:264
  62.7 4.4 %collective-permute-start.5 = (bf16[256,768]{1,0:T(8,128)(2,1)S(1)}, bf16[256,768]{1,0:T(8,128)(2,1)S(1)}, u32[]{:S(2)}, u32[]{:S(2)}) collective-permute-start(bf16[256,768]{1,0:T(8,128)(2,1)S(1)} %get-tuple-element.26), channel_id=1, source_target_pairs={{0,1},{1,0},{2,3},{3,2},{4,5},{5,4},{6,7},{7,6},{8,9},{9,8},{10,11... | collective-permute-start | bytes 1179656 | tf_op jit(solution)/shard_map/ppermute | solution.py:276
  92.2 6.1 %collective-permute-start.7 = (bf16[8,2688]{1,0:T(8,128)(2,1)S(1)}, bf16[8,2688]{1,0:T(8,128)(2,1)S(1)}, u32[]{:S(2)}, u32[]{:S(2)}) collective-permute-start(bf16[8,2688]{1,0:T(8,128)(2,1)S(1)} %reduce_sum.12), channel_id=1, source_target_pairs={{0,32},{32,0},{1,33},{33,1},{2,34},{34,2},{3,35},{35,3},{4,36},{36... | collective-permute-start | bytes 129032 | tf_op jit(solution)/shard_map/ppermute | solution.py:282

commit v14 on v11

--- a/solution.py
+++ b/solution.py
@@ -28,6 +28,7 @@
 REST = 32
 SPLIT = RB * MAIN
 WIDTH = 2688
+STRIP = 16
 PICK = 2 * MAIN + 2 * 128
 
 F32 = jnp.float32
@@ -71,8 +72,10 @@
     return values * inverse, inverse
 
 
-def pair_grad(step_ref, col_ref, texts, block, position):
-    images = unit_rows(block)[0].astype(BF16)
+def pair_grad(step_ref, col_ref, texts, block_ref, image_ref, position):
+    for row in range(0, ROWS, STRIP):
+        image_ref[row : row + STRIP, :] = unit_rows(block_ref[row : row + STRIP, :])[0].astype(BF16)
+    images = image_ref[...]
     steps = step_ref[pl.ds(position, 1), :]
     cols = col_ref[pl.ds(position, 1), :]
     logits = LOGIT_SCALE * dot_t(texts, images) + LOGIT_BIAS
@@ -109,13 +112,13 @@
         spot = pl.ds(pl.multiple_of(shard * ROWS, ROWS), ROWS)
         steps_ref[position : position + 1, :] = step_ref[:, spot]
         cols_ref[position : position + 1, :] = col_ref[:, spot]
-    acc_ref[...] = pair_grad(steps_ref, cols_ref, texts, image_ref[...], 2)
-
-
-def near_kernel(place_ref, right_ref, left_ref, step_ref, col_ref, text_ref, acc_ref, out_ref):
+    acc_ref[...] = pair_grad(steps_ref, cols_ref, texts, image_ref, image_ref, 2)
+
+
+def near_kernel(place_ref, right_ref, left_ref, step_ref, col_ref, text_ref, acc_ref, out_ref, *scratch):
     texts = text_ref[...]
-    total = acc_ref[...] + pair_grad(step_ref, col_ref, texts, right_ref[...], place_ref[1])
-    out_ref[...] = total + pair_grad(step_ref, col_ref, texts, left_ref[...], 3)
+    total = acc_ref[...] + pair_grad(step_ref, col_ref, texts, right_ref, scratch[0], place_ref[1])
+    out_ref[...] = total + pair_grad(step_ref, col_ref, texts, left_ref, scratch[1], 3)
 
 
 def column_of(lane, core):
@@ -140,21 +143,22 @@
     here_ref[...] = jnp.where(rows == column_of(lane, core), 1.0, 0.0).astype(BF16)
 
 
-def far_kernel(at, place_ref, image_ref, step_ref, col_ref, text_ref, acc_ref, out_ref):
-    part = pair_grad(step_ref, col_ref, text_ref[...], image_ref[...], place_ref[at])
+def far_kernel(at, place_ref, image_ref, step_ref, col_ref, text_ref, acc_ref, out_ref, scratch):
+    part = pair_grad(step_ref, col_ref, text_ref[...], image_ref, scratch, place_ref[at])
     out_ref[...] = acc_ref[...] + part
 
 
 def last_kernel(
-    place_ref, left_ref, step_ref, col_ref, text_ref, acc_ref, unit_ref, inv_ref, pick_ref, grad_ref, out_ref
+    place_ref, left_ref, step_ref, col_ref, text_ref, acc_ref, unit_ref, inv_ref, pick_ref, grad_ref, out_ref, scratch
 ):
-    part = pair_grad(step_ref, col_ref, text_ref[...], left_ref[...], place_ref[3])
-    total = acc_ref[...] + part
-    unit = unit_ref[...]
-    radial = jnp.sum(unit * total, axis=-1, keepdims=True)
-    grad = (inv_ref[:, :1] * (total - unit * radial)).astype(BF16)
-    grad_ref[...] = grad
-    out_ref[...] = dot(grad, pick_ref[...]).astype(BF16)
+    part = pair_grad(step_ref, col_ref, text_ref[...], left_ref, scratch, place_ref[3])
+    for row in range(0, ROWS, STRIP):
+        strip = slice(row, row + STRIP)
+        total = acc_ref[strip, :] + part[strip]
+        unit = unit_ref[strip, :]
+        radial = jnp.sum(unit * total, axis=-1, keepdims=True)
+        grad_ref[strip, :] = (inv_ref[strip, :1] * (total - unit * radial)).astype(BF16)
+    out_ref[...] = dot(grad_ref[...], pick_ref[...]).astype(BF16)
 
 
 def own_kernel(grad_ref, pick_ref, proj_ref, out_ref, text_ref):
@@ -241,6 +245,7 @@
 
     full = (ROWS, E)
     table = (8, ROWS)
+    strips = (pltpu.VMEM(full, BF16),)
     unit, inverse, texts, acc, steps, cols = call(
         first_kernel,
         (place, features, projection, image, pair_step, pair_col),
@@ -256,16 +261,16 @@
     )
     swap = [(0, 1), (1, 0)]
     opposite = lax.ppermute(turned, "c", swap)
-    (acc,) = call(near_kernel, (place, right, left, steps, cols, texts, acc), ((full, F32),), 1 << 30, 24, "near_pairs")
+    (acc,) = call(near_kernel, (place, right, left, steps, cols, texts, acc), ((full, F32),), 1 << 30, 24, "near_pairs", (), strips * 2)
     for at, block, name in ((4, across, "far_across"), (2, right2, "far_right")):
         (acc,) = call(
-            functools.partial(far_kernel, at), (place, block, steps, cols, texts, acc), ((full, F32),), 1 << 28, 24, name
+            functools.partial(far_kernel, at), (place, block, steps, cols, texts, acc), ((full, F32),), 1 << 28, 24, name, (), strips
         )
     grad, columns = call(
         last_kernel,
         (place, left2, steps, cols, texts, acc, unit, inverse, pick_there),
         ((full, BF16), ((ROWS, PICK), BF16)),
-        1 << 30, 32, "far_left",
+        1 << 30, 32, "far_left", (), strips,
     )
     columns = lax.ppermute(columns, "c", swap)
     own, grad_text = call(

time: 137 us -> 137 us (level)
  no operation moved by 1% of the time
where the time goes in v14:
time: 137 us
  blocking collectives  60 us (44%)
  starting transfers between devices  50.4 us (37%)
  Pallas kernels  20.2 us (15%)
  waiting for transfers between devices  3.77 us (3%)
    all_to_all x3, blocking collectives, traded(): return lax.all_to_all(value, axis, split_axis=0, concat_axis=0)  60 us
    ppermute x5, starting transfers between devices, shifted(): return lax.ppermute(value, DP, pairs)  40.5 us
    pallas_call x10, Pallas kernels, call(): pl.pallas_call(kernel, out_shape=[jax.ShapeDtypeStruct(shape, dtype) for...  20.2 us
    ppermute x1, starting transfers between devices, local(): opposite = lax.ppermute(turned, 'c', swap)  4.84 us
    ppermute x1, waiting for transfers between devices, local(): near = lax.ppermute(rows, 'z1', swap)  3.75 us
    ppermute x1, starting transfers between devices, local(): columns = lax.ppermute(columns, 'c', swap)  3.08 us
  transfers between devices with their start and end apart: 8, of which 1 were waited for; matrix products, arithmetic and copies ran while one was open for 0% of the time, Pallas kernels for 13%

profile of v14, /device:TPU:1, one launch (start us, length us, event | category | flops | bytes accessed | tf_op | source)
XLA Modules:
  0.0 136.7 jit_solution(6563866679356800738)
XLA Ops:
  0.6 4.0 %collective-permute-start.2 = (bf16[256,1152]{1,0:T(8,128)(2,1)}, bf16[256,1152]{1,0:T(8,128)(2,1)S(1)}, u32[]{:S(2)}, u32[]{:S(2)}) collective-permute-start(bf16[256,1152]{1,0:T(8,128)(2,1)} %bitcast.12), channel_id=1, source_target_pairs={{0,4},{4,8},{8,12},{12,0},{16,20},{20,24},{24,28},{28,16},{32,36},... | collective-permute-start | bytes 1769480 | tf_op jit(solution)/shard_map/ppermute | solution.py:54
  4.6 14.9 %collective-permute-start = (bf16[256,1152]{1,0:T(8,128)(2,1)}, bf16[256,1152]{1,0:T(8,128)(2,1)S(1)}, u32[]{:S(2)}, u32[]{:S(2)}) collective-permute-start(bf16[256,1152]{1,0:T(8,128)(2,1)} %bitcast.13), channel_id=1, source_target_pairs={{0,508},{4,0},{8,4},{12,8},{16,12},{20,16},{24,20},{28,24},{32,28}... | collective-permute-start | bytes 1769480 | tf_op jit(solution)/shard_map/ppermute | solution.py:54
  19.5 3.0 %collective-permute-start.4 = (bf16[256,1152]{1,0:T(8,128)(2,1)S(1)}, bf16[256,1152]{1,0:T(8,128)(2,1)S(1)}, u32[]{:S(2)}, u32[]{:S(2)}) collective-permute-start(bf16[256,1152]{1,0:T(8,128)(2,1)S(1)} %collective-permute-done.2.right_ref), channel_id=1, source_target_pairs={{0,16},{4,500},{8,504},{12,508},{16,32},{20,4},{24,8},{28,12},{32,... | collective-permute-start | bytes 1769480 | tf_op jit(solution)/shard_map/ppermute | solution.py:54
  22.5 12.1 %collective-permute-start.3 = (bf16[256,1152]{1,0:T(8,128)(2,1)S(1)}, bf16[256,1152]{1,0:T(8,128)(2,1)S(1)}, u32[]{:S(2)}, u32[]{:S(2)}) collective-permute-start(bf16[256,1152]{1,0:T(8,128)(2,1)S(1)} %collective-permute-done.2.right_ref), channel_id=1, source_target_pairs={{0,4},{4,8},{8,12},{12,16},{16,20},{20,24},{24,28},{28,32},{32,36}... | collective-permute-start | bytes 1769480 | tf_op jit(solution)/shard_map/ppermute | solution.py:54
  34.6 6.6 %collective-permute-start.1 = (bf16[256,1152]{1,0:T(8,128)(2,1)S(1)}, bf16[256,1152]{1,0:T(8,128)(2,1)S(1)}, u32[]{:S(2)}, u32[]{:S(2)}) collective-permute-start(bf16[256,1152]{1,0:T(8,128)(2,1)S(1)} %collective-permute-done.left_ref), channel_id=1, source_target_pairs={{0,508},{4,0},{8,20},{12,8},{16,12},{20,16},{24,36},{28,24},{32,28... | collective-permute-start | bytes 1769480 | tf_op jit(solution)/shard_map/ppermute | solution.py:54
  41.3 1.1 copy-done.2
  42.4 2.4 %order.1 = (bf16[1152,256]{1,0:T(8,128)(2,1)S(1)}, bf16[1152,768]{1,0:T(8,128)(2,1)S(1)}, bf16[1152,768]{1,0:T(8,128)(2,1)S(1)}) custom-call(s32[7]{0:T(128)S(1)} %stack.31.place_ref, bf16[256,1152]{1,0:T(8,128)(2,1)S(1)} %bitcast.15), custom_call_target="tpu_custom_call" | custom-call | flops 1073741824 | bytes 4194304 | tf_op jit(solution)/shard_map/order/pallas_call | solution.py:213
  44.8 4.8 %collective-permute-start.6 = (bf16[1152,256]{1,0:T(8,128)(2,1)S(1)}, bf16[1152,256]{1,0:T(8,128)(2,1)S(1)}, u32[]{:S(2)}, u32[]{:S(2)}) collective-permute-start(bf16[1152,256]{1,0:T(8,128)(2,1)S(1)} %get-tuple-element.29.turned_ref), channel_id=1, source_target_pairs={{0,1},{1,0},{2,3},{3,2},{4,5},{5,4},{6,7},{7,6},{8,9},{9,8},{10,11... | collective-permute-start | bytes 1769480 | tf_op jit(solution)/shard_map/ppermute | solution.py:263
  49.7 4.8 %hidden_and_own.1 = (f32[256,1152]{1,0:T(8,128)S(1)}, f32[256,128]{1,0:T(8,128)S(1)}, bf16[256,1152]{1,0:T(8,128)(2,1)S(1)}, f32[256,1152]{1,0:T(8,128)S(1)}, s3...) custom-call(s32[7]{0:T(128)S(1)} %stack.31.place_ref, bf16[256,1152]{1,0:T(8,128)(2,1)S(1)} %bitcast.16, ...), custom_call_target="tpu_custom_call" | custom-call | flops 1073741824 | bytes 4194304 | tf_op jit(solution)/shard_map/hidden_and_own/pallas_call | solution.py:213
  54.5 2.3 %near_pairs.1.acc_ref = f32[256,1152]{1,0:T(8,128)S(1)} custom-call(s32[7]{0:T(128)S(1)} %stack.31.place_ref, bf16[256,1152]{1,0:T(8,128)(2,1)S(1)} %collective-permute-done.2.right_ref, bf16[256,1152]{1,0:T(8,128)(2,1)S(1)} %collective-permute-done.left_ref, s32[8,256]{1,0:T(8,128)S(1)} %get-tuple-element.17.step_ref, ...), custom_call_target="tpu_custom_call" | custom-call | flops 1073741824 | bytes 4194304 | tf_op jit(solution)/shard_map/near_pairs/pallas_call | solution.py:213
  56.8 1.6 %far_across.1.acc_ref = f32[256,1152]{1,0:T(8,128)S(1)} custom-call(s32[7]{0:T(128)S(1)} %stack.31.place_ref, bf16[256,1152]{1,0:T(8,128)(2,1)S(1)} %collective-permute-done.4.image_ref, s32[8,256]{1,0:T(8,128)S(1)} %get-tuple-element.17.step_ref, s32[8,256]{1,0:T(8,128)S(1)} %get-tuple-element.18.col_ref, bf16[256,1152]{1,0:T(8,128)(2,1)S(1)} %get-tuple-element.19.text_ref, ...), custom_call_target="tpu_custom_call" | custom-call | flops 268435456 | bytes 4194304 | tf_op jit(solution)/shard_map/far_across/pallas_call | solution.py:213
  58.4 1.6 %far_right.1.acc_ref = f32[256,1152]{1,0:T(8,128)S(1)} custom-call(s32[7]{0:T(128)S(1)} %stack.31.place_ref, bf16[256,1152]{1,0:T(8,128)(2,1)S(1)} %collective-permute-done.3.image_ref, s32[8,256]{1,0:T(8,128)S(1)} %get-tuple-element.17.step_ref, s32[8,256]{1,0:T(8,128)S(1)} %get-tuple-element.18.col_ref, bf16[256,1152]{1,0:T(8,128)(2,1)S(1)} %get-tuple-element.19.text_ref, ...), custom_call_target="tpu_custom_call" | custom-call | flops 268435456 | bytes 4194304 | tf_op jit(solution)/shard_map/far_right/pallas_call | solution.py:213
  60.1 2.6 %far_left.1 = (bf16[256,1152]{1,0:T(8,128)(2,1)S(1)}, bf16[256,768]{1,0:T(8,128)(2,1)S(1)}) custom-call(s32[7]{0:T(128)S(1)} %stack.31.place_ref, bf16[256,1152]{1,0:T(8,128)(2,1)S(1)} %collective-permute-done.1.left_ref, s32[8,256]{1,0:T(8,128)S(1)} %get-tuple-element.17.step_ref, s32[8,256]{1,0:T(8,128)S(1)} %get-tuple-element.18.col_ref, ...), custom_call_target="tpu_custom_call" | custom-call | flops 1073741824 | bytes 4194304 | tf_op jit(solution)/shard_map/far_left/pallas_call | solution.py:213
  62.7 3.1 %collective-permute-start.5 = (bf16[256,768]{1,0:T(8,128)(2,1)S(1)}, bf16[256,768]{1,0:T(8,128)(2,1)S(1)}, u32[]{:S(2)}, u32[]{:S(2)}) collective-permute-start(bf16[256,768]{1,0:T(8,128)(2,1)S(1)} %get-tuple-element.28), channel_id=1, source_target_pairs={{0,1},{1,0},{2,3},{3,2},{4,5},{5,4},{6,7},{7,6},{8,9},{9,8},{10,11... | collective-permute-start | bytes 1179656 | tf_op jit(solution)/shard_map/ppermute | solution.py:275
  65.8 2.3 %own_columns.1 = (bf16[256,768]{1,0:T(8,128)(2,1)S(1)}, bf16[256,1152]{1,0:T(8,128)(2,1)}) custom-call(bf16[256,1152]{1,0:T(8,128)(2,1)S(1)} %get-tuple-element.24.grad_ref, bf16[1152,768]{1,0:T(8,128)(2,1)S(1)} %get-tuple-element.25.pick_ref, bf16[1152,1152]{1,0:T(8,128)(2,1)S(1)} %copy-done), custom_call_target="tpu_custom_call" | custom-call | flops 268435456 | bytes 4194304 | tf_op jit(solution)/shard_map/own_columns/pallas_call | solution.py:213
  68.1 1.1 partial.1
  69.2 24.2 %all_to_all.15 = bf16[32,8,2688]{2,1,0:T(8,128)(2,1)S(1)} all-to-all(bf16[32,8,2688]{2,1,0:T(8,128)(2,1)S(1)} %bitcast.11), channel_id=1, replica_groups=mesh['yh'=2,'zh'=4,'z1'=2,'z0'=2,'x'=4,'yl'=2,'c'=2] {'yh','yl','x','z0'}, dimensions={0} | all-to-all | bytes 2752512 | tf_op jit(solution)/shard_map/all_to_all | solution.py:226
  93.4 0.2 reduce_sum.12
  93.6 1.9 %collective-permute-start.7 = (bf16[8,2688]{1,0:T(8,128)(2,1)S(1)}, bf16[8,2688]{1,0:T(8,128)(2,1)S(1)}, u32[]{:S(2)}, u32[]{:S(2)}) collective-permute-start(bf16[8,2688]{1,0:T(8,128)(2,1)S(1)} %reduce_sum.12), channel_id=1, source_target_pairs={{0,32},{32,0},{1,33},{33,1},{2,34},{34,2},{3,35},{35,3},{4,36},{36... | collective-permute-start | bytes 129032 | tf_op jit(solution)/shard_map/ppermute | solution.py:283
  95.6 3.8 %collective-permute-done.7 = bf16[8,2688]{1,0:T(8,128)(2,1)S(1)} collective-permute-done((bf16[8,2688]{1,0:T(8,128)(2,1)S(1)}, bf16[8,2688]{1,0:T(8,128)(2,1)S(1)}, u32[]{:S(2)}, u32[]{:S(2)}) %collective-permute-start.7) | collective-permute-done | bytes 43040 | tf_op jit(solution)/shard_map/ppermute | solution.py:283
  99.4 19.2 %all_to_all.16.came_ref = bf16[4,8,2688]{2,1,0:T(8,128)(2,1)S(1)} all-to-all(bf16[4,8,2688]{2,1,0:T(8,128)(2,1)S(1)} %broadcast_in_dim.10), channel_id=1, replica_groups=mesh['yh'=2,'zh'=4,'z1'=2,'z0'=2,'x'=4,'yl'=2,'c'=2] {'zh'}, dimensions={0} | all-to-all | bytes 344064 | tf_op jit(solution)/shard_map/all_to_all | solution.py:226
  118.6 0.7 block.1
  119.3 16.6 %all_to_all.17.square_ref = f32[64,1,128]{2,1,0:T(1,128)S(1)} all-to-all(f32[64,1,128]{2,1,0:T(1,128)S(1)} %get-tuple-element.30), channel_id=1, replica_groups=mesh['yh'=2,'zh'=4,'z1'=2,'z0'=2,'x'=4,'yl'=2,'c'=2] {'yh','yl','x','z0'..., dimensions={0} | all-to-all | bytes 65536 | tf_op jit(solution)/shard_map/all_to_all | solution.py:226
  135.9 0.8 clip.1
  (21 shorter events, 0.2 us)
Async XLA Ops:
  0.6 18.9 %collective-permute-start.2 = (bf16[256,1152]{1,0:T(8,128)(2,1)}, bf16[256,1152]{1,0:T(8,128)(2,1)S(1)}, u32[]{:S(2)}, u32[]{:S(2)}) collective-permute-start(bf16[256,1152]{1,0:T(8,128)(2,1)} %bitcast.12), channel_id=1, source_target_pairs={{0,4},{4,8},{8,12},{12,0},{16,20},{20,24},{24,28},{28,16},{32,36},... | collective-permute-start | bytes 1769480 | tf_op jit(solution)/shard_map/ppermute | solution.py:54
  4.6 30.1 %collective-permute-start = (bf16[256,1152]{1,0:T(8,128)(2,1)}, bf16[256,1152]{1,0:T(8,128)(2,1)S(1)}, u32[]{:S(2)}, u32[]{:S(2)}) collective-permute-start(bf16[256,1152]{1,0:T(8,128)(2,1)} %bitcast.13), channel_id=1, source_target_pairs={{0,508},{4,0},{8,4},{12,8},{16,12},{20,16},{24,20},{28,24},{32,28}... | collective-permute-start | bytes 1769480 | tf_op jit(solution)/shard_map/ppermute | solution.py:54
  19.5 37.2 %collective-permute-start.4 = (bf16[256,1152]{1,0:T(8,128)(2,1)S(1)}, bf16[256,1152]{1,0:T(8,128)(2,1)S(1)}, u32[]{:S(2)}, u32[]{:S(2)}) collective-permute-start(bf16[256,1152]{1,0:T(8,128)(2,1)S(1)} %collective-permute-done.2.right_ref), channel_id=1, source_target_pairs={{0,16},{4,500},{8,504},{12,508},{16,32},{20,4},{24,8},{28,12},{32,... | collective-permute-start | bytes 1769480 | tf_op jit(solution)/shard_map/ppermute | solution.py:54
  22.5 35.9 %collective-permute-start.3 = (bf16[256,1152]{1,0:T(8,128)(2,1)S(1)}, bf16[256,1152]{1,0:T(8,128)(2,1)S(1)}, u32[]{:S(2)}, u32[]{:S(2)}) collective-permute-start(bf16[256,1152]{1,0:T(8,128)(2,1)S(1)} %collective-permute-done.2.right_ref), channel_id=1, source_target_pairs={{0,4},{4,8},{8,12},{12,16},{16,20},{20,24},{24,28},{28,32},{32,36}... | collective-permute-start | bytes 1769480 | tf_op jit(solution)/shard_map/ppermute | solution.py:54
  34.6 25.4 %collective-permute-start.1 = (bf16[256,1152]{1,0:T(8,128)(2,1)S(1)}, bf16[256,1152]{1,0:T(8,128)(2,1)S(1)}, u32[]{:S(2)}, u32[]{:S(2)}) collective-permute-start(bf16[256,1152]{1,0:T(8,128)(2,1)S(1)} %collective-permute-done.left_ref), channel_id=1, source_target_pairs={{0,508},{4,0},{8,20},{12,8},{16,12},{20,16},{24,36},{28,24},{32,28... | collective-permute-start | bytes 1769480 | tf_op jit(solution)/shard_map/ppermute | solution.py:54
  41.3 1.1 copy-start.2
  42.4 7.3 %copy-start.1 = (bf16[1,256,1152]{2,1,0:T(8,128)(2,1)S(1)}, bf16[1,256,1152]{2,1,0:T(8,128)(2,1)}, u32[]{:S(2)}) copy-start(bf16[1,256,1152]{2,1,0:T(8,128)(2,1)} %param.5) | copy-start | bytes 1769476
  42.4 7.3 %copy-start.3 = (bf16[1,256,1152]{2,1,0:T(8,128)(2,1)S(1)}, bf16[1,256,1152]{2,1,0:T(8,128)(2,1)}, u32[]{:S(2)}) copy-start(bf16[1,256,1152]{2,1,0:T(8,128)(2,1)} %param.6) | copy-start | bytes 1769476
  42.4 7.3 %copy-start.4 = (s32[1,32768]{1,0:T(1,128)S(1)}, s32[1,32768]{1,0:T(1,128)}, u32[]{:S(2)}) copy-start(s32[1,32768]{1,0:T(1,128)} %step_hbm.1) | copy-start | bytes 393220
  42.4 7.3 %copy-start.5 = (s32[1,32768]{1,0:T(1,128)S(1)}, s32[1,32768]{1,0:T(1,128)}, u32[]{:S(2)}) copy-start(s32[1,32768]{1,0:T(1,128)} %col_hbm.1) | copy-start | bytes 393220
  44.8 23.3 %collective-permute-start.6 = (bf16[1152,256]{1,0:T(8,128)(2,1)S(1)}, bf16[1152,256]{1,0:T(8,128)(2,1)S(1)}, u32[]{:S(2)}, u32[]{:S(2)}) collective-permute-start(bf16[1152,256]{1,0:T(8,128)(2,1)S(1)} %get-tuple-element.29.turned_ref), channel_id=1, source_target_pairs={{0,1},{1,0},{2,3},{3,2},{4,5},{5,4},{6,7},{7,6},{8,9},{9,8},{10,11... | collective-permute-start | bytes 1769480 | tf_op jit(solution)/shard_map/ppermute | solution.py:263
  60.1 5.7 %copy-start = (bf16[1152,1152]{1,0:T(8,128)(2,1)S(1)}, bf16[1152,1152]{1,0:T(8,128)(2,1)}, u32[]{:S(2)}) copy-start(bf16[1152,1152]{1,0:T(8,128)(2,1)} %proj_ref.1) | copy-start | bytes 7962628
  62.7 5.4 %collective-permute-start.5 = (bf16[256,768]{1,0:T(8,128)(2,1)S(1)}, bf16[256,768]{1,0:T(8,128)(2,1)S(1)}, u32[]{:S(2)}, u32[]{:S(2)}) collective-permute-start(bf16[256,768]{1,0:T(8,128)(2,1)S(1)} %get-tuple-element.28), channel_id=1, source_target_pairs={{0,1},{1,0},{2,3},{3,2},{4,5},{5,4},{6,7},{7,6},{8,9},{9,8},{10,11... | collective-permute-start | bytes 1179656 | tf_op jit(solution)/shard_map/ppermute | solution.py:275
  93.6 5.7 %collective-permute-start.7 = (bf16[8,2688]{1,0:T(8,128)(2,1)S(1)}, bf16[8,2688]{1,0:T(8,128)(2,1)S(1)}, u32[]{:S(2)}, u32[]{:S(2)}) collective-permute-start(bf16[8,2688]{1,0:T(8,128)(2,1)S(1)} %reduce_sum.12), channel_id=1, source_target_pairs={{0,32},{32,0},{1,33},{33,1},{2,34},{34,2},{3,35},{35,3},{4,36},{36... | collective-permute-start | bytes 129032 | tf_op jit(solution)/shard_map/ppermute | solution.py:283
